TPU v7x, 256 devices: a whole 4x4x8 slice. The times are simulated.
256 devices in a mesh: grp: 8 (over x, core), tp: 32 (over y, z).
Axes of the slice: x: 4, y: 4, z: 8, core: 2. Of those that a mesh axis runs over, the one named last changes fastest.
Arguments:
- attention_output: bfloat16 [4096, 8192], P('grp', 'tp'), may hold values from -6 to 6
- quantized_weight_codes: bfloat16 [8192, 8192], P('tp'), may hold values from -127 to 127, as said below
- column_scale: float32 [8192], P('tp'), may hold values from 0 to 1
- adapter_down_maps: bfloat16 [512, 64, 8192], P('grp', None, 'tp'), may hold values from -0.0625 to 0.0625
- adapter_up_maps: bfloat16 [512, 64, 8192], P('grp', None, 'tp'), may hold values from -0.75 to 0.75
- owning_group_index: int32 [4096, 1], P('grp'), may hold values from 0 to 7; in each aligned block of 512 rows (0 to 511, 512 to 1023, ...) at most 128 rows name the same one
- token_adapter_slot: int32 [4096], P('grp'), may hold values from 0 to 63
Outputs:
- projected: bfloat16 [4096, 8192], P('grp', 'tp')
Inputs may be any that keep to these rules, and one draw needn't show every extreme that they name: `owning_group_index`: among the tokens of one index of grp (aligned blocks of 512 tokens) at most 128 name the same owner, and in some blocks some owner is named by exactly 128 of them. `quantized_weight_codes`: every entry is a whole number.
All inputs are finite; a program needn't handle non-finite values.
Results may differ from a plain program's by a relative error of at most 0.0046.
Values may be sent and summed in bfloat16 or wider, within the bound.
No kernel may reach another device: no remote copies, remote signals or barrier semaphores. Data moves between devices by JAX's collectives and lax.ppermute only.
A program may use at most 128 MiB of HBM per device.

v0:
```python
import math

import jax
import jax.numpy as jnp
from jax import lax
from jax.sharding import PartitionSpec as P


def dense_down(token_row_block, slot_indices, adapter_down_maps):
    adapters, rank_width, feat_width = adapter_down_maps.shape
    stacked = adapter_down_maps.reshape(adapters * rank_width, feat_width)
    all_products = lax.dot_general(
        token_row_block, stacked, (((1,), (1,)), ((), ())), preferred_element_type=jnp.float32
    )
    all_products = all_products.reshape(token_row_block.shape[0], adapters, rank_width)
    select = (slot_indices[:, None] == jnp.arange(adapters, dtype=jnp.int32)[None, :]).astype(
        jnp.float32
    )
    return jnp.sum(select[:, :, None] * all_products, axis=1)


def dense_up(rank_product, slot_indices, adapter_up_maps):
    adapters, rank_width, feat_width = adapter_up_maps.shape
    select = (slot_indices[:, None] == jnp.arange(adapters, dtype=jnp.int32)[None, :]).astype(
        rank_product.dtype
    )
    spread = (select[:, :, None] * rank_product[:, None, :]).reshape(
        rank_product.shape[0], adapters * rank_width
    )
    return jnp.dot(
        spread,
        adapter_up_maps.reshape(adapters * rank_width, feat_width),
        preferred_element_type=jnp.float32,
    )


def grouped_blocks(kernel, inputs, slot_indices, weights, rows_per_block):
    total_rows = inputs.shape[0]

    def apply_block(block_pair):
        return kernel(block_pair[0], block_pair[1], weights)

    shaped = (
        inputs.reshape(total_rows // rows_per_block, rows_per_block, inputs.shape[1]),
        slot_indices.reshape(total_rows // rows_per_block, rows_per_block),
    )
    result = lax.map(apply_block, shaped)
    return result.reshape(total_rows, result.shape[2])


def on_device(
    attention_output,
    quantized_weight_codes,
    column_scale,
    adapter_down_maps,
    adapter_up_maps,
    owning_group_index,
    token_adapter_slot,
):
    tok_rows, feat_width = attention_output.shape
    groups = lax.axis_size("grp")
    capacity = 2 * tok_rows // groups
    summed = lax.psum_scatter(
        lax.dot_general(
            quantized_weight_codes,
            attention_output,
            (((0,), (1,)), ((), ())),
            preferred_element_type=jnp.float32,
        ),
        "tp",
        scatter_dimension=0,
        tiled=True,
    ).T
    base = summed * column_scale[None, :]
    owners = owning_group_index[:, 0]
    member = (owners[:, None] == jnp.arange(groups, dtype=jnp.int32)[None, :]).astype(jnp.int32)
    earlier = jnp.cumsum(member, axis=0) - member
    position = jnp.sum(earlier * member, axis=1)
    target = owners * capacity + position
    send_rows = (
        jnp.zeros((groups * capacity, feat_width), attention_output.dtype)
        .at[target]
        .set(attention_output)
    )
    send_slots = jnp.zeros((groups * capacity,), jnp.int32).at[target].set(token_adapter_slot)
    arrived_rows, arrived_slots = (
        lax.all_to_all(
            send_rows.reshape(groups, capacity, feat_width),
            "grp",
            split_axis=0,
            concat_axis=0,
            tiled=True,
        ),
        lax.all_to_all(
            send_slots.reshape(groups, capacity), "grp", split_axis=0, concat_axis=0, tiled=True
        ),
    )
    flattened_rows = arrived_rows.reshape(groups * capacity, feat_width)
    flattened_slots = arrived_slots.reshape(groups * capacity)
    received = groups * capacity
    rows_per_block = math.gcd(received, 512)
    down_product = grouped_blocks(
        dense_down, flattened_rows, flattened_slots, adapter_down_maps, rows_per_block
    )
    rank_product = lax.psum(down_product, "tp").astype(jnp.bfloat16)
    adapter_update = grouped_blocks(
        dense_up, rank_product, flattened_slots, adapter_up_maps, rows_per_block
    ).astype(jnp.bfloat16)
    returned = lax.all_to_all(
        adapter_update.reshape(groups, capacity, feat_width),
        "grp",
        split_axis=0,
        concat_axis=0,
        tiled=True,
    )
    back_rows = returned.reshape(groups * capacity, feat_width)[target]
    return (base + back_rows.astype(jnp.float32)).astype(jnp.bfloat16)


def solution(mesh):
    in_specs = (
        P("grp", "tp"),
        P("tp", None),
        P("tp"),
        P("grp", None, "tp"),
        P("grp", None, "tp"),
        P("grp", None),
        P("grp"),
    )
    out_specs = P("grp", "tp")
    return jax.shard_map(
        on_device, mesh=mesh, in_specs=in_specs, out_specs=out_specs, check_vma=False
    )
```

profile of v0, /device:TPU:1, one launch (start us, length us, event | category | flops | bytes accessed | tf_op | source)
XLA Modules:
  0.0 271.8 jit_solution(17877626195868347438)
XLA Ops:
  6.5 10.3 %fusion.23 = f32[8192,512]{1,0:T(8,128)} fusion(bf16[256,8192]{1,0:T(8,128)(2,1)} %param.12, bf16[512,256]{1,0:T(8,128)(2,1)} %param.11), kind=kOutput, calls=%fused_computation.36 | convolution fusion | flops 2147483648 | bytes 21233664 | tf_op jit(solution)/shard_map/dot_general | solution.py:64
  16.9 0.7 copy-done
  17.6 1.1 reduce-window.6
  19.0 3.2 %scatter_custom_fusion = s32[1024]{0:T(1024)} fusion(s32[512]{0:T(512)S(1)} %bitcast.76, s32[512]{0:T(512)} %param.17, s32[]{:T(128)} %copy.46), kind=kCustom, calls=%fused_computation.34 | custom fusion | bytes 4608 | tf_op jit(solution)/shard_map/scatter | solution.py:85
  22.2 6.5 %all-to-all-start = ((s32[8,1,128]{2,1,0:T(1,128)}), s32[8,1,128]{2,1,0:T(1,128)S(1)}, u32[]{:S(2)}, u32[]{:S(2)}) async-start(s32[8,1,128]{2,1,0:T(1,128)} %bitcast.15), calls=%async_computation.1 | async-start | bytes 8192 | tf_op jit(solution)/shard_map/all_to_all | solution.py:94
  28.7 3.6 %scatter_custom_fusion.1 = bf16[1024,256]{1,0:T(8,128)(2,1)} fusion(s32[512]{0:T(512)S(1)} %bitcast.77, bf16[512,256]{1,0:T(8,128)(2,1)} %param.11, bf16[]{:T(256)} %constant.28.clone.1), kind=kCustom, calls=%fused_computation.22 | custom fusion | bytes 524800 | tf_op jit(solution)/shard_map/scatter | solution.py:83
  32.2 1.0 all-to-all-done
  33.2 4.1 %all-to-all-start.1 = ((bf16[8,128,256]{2,1,0:T(8,128)(2,1)}), bf16[8,128,256]{2,1,0:T(8,128)(2,1)S(1)}, u32[]{:S(2)}, u32[]{:S(2)}) async-start(bf16[8,128,256]{2,1,0:T(8,128)(2,1)} %bitcast.16), calls=%async_computation.2 | async-start | bytes 1048576 | tf_op jit(solution)/shard_map/all_to_all | solution.py:87
  38.5 8.3 %all-to-all-done.1 = bf16[8,128,256]{2,1,0:T(8,128)(2,1)S(1)} async-done(((bf16[8,128,256]{2,1,0:T(8,128)(2,1)}), bf16[8,128,256]{2,1,0:T(8,128)(2,1)S(1)}, u32[]{:S(2)}, u32[]{:S(2)}) %all-to-all-start.1) | async-done | bytes 524320 | tf_op jit(solution)/shard_map/all_to_all | solution.py:87
  46.8 5.4 %while.20 = (s32[]{:T(128)}, f32[2,512,64]{1,0,2:T(2,128)S(1)}, s32[2,512]{1,0:T(2,128)S(1)}, bf16[2,512,256]{2,1,0:T(8,128)(2,1)S(1)}, bf16[64,64,256]{2,1,0:T(8,128)(2,1)S(1)}, /*index=5*/s32[]{:T(128)}, s32[]{:T(128)}) while((s32[]{:T(128)}, f32[2,512,64]{1,0,2:T(2,128)S(1)}, s32[2,512]{1,0:T(2,128)S(1)}, ...), condition=%wide.region_8.9_spmd, body=%wide.region_6.8_spmd.sunk | while | flops 1077968896 | bytes 3283041 | solution.py:47
  46.8 1.3 multiply_reduce_fusion.2
  48.3 1.2 dynamic_update_slice.11
  49.5 1.3 multiply_reduce_fusion.2
  51.0 1.2 dynamic_update_slice.11
  52.3 120.6 %all-reduce.1 = bf16[1024,64]{0,1:T(8,128)(2,1)S(1)} all-reduce(f32[1024,64]{0,1:T(8,128)S(1)} %bitcast.68), channel_id=1, replica_groups=mesh['grp'=8,'tp'=32] {'tp'}, use_global_device_ids=true, to_apply=%region_9.10 | all-reduce | flops 65536 | bytes 393216 | tf_op jit(solution)/shard_map/psum | solution.py:105
  172.9 7.5 %while.21 = (s32[]{:T(128)}, bf16[2,512,256]{2,1,0:T(8,128)(2,1)}, s32[2,512]{1,0:T(2,128)S(1)}, bf16[2,512,64]{1,2,0:T(8,128)(2,1)S(1)}, bf16[64,64,256]{2,1,0:T(8,128)(2,1)}, /*index=5*/s32[]{:T(128)}) while((s32[]{:T(128)}, bf16[2,512,256]{2,1,0:T(8,128)(2,1)}, s32[2,512]{1,0:T(2,128)S(1)}, bf16[2,512,64]{1,2,0:T(8,128)(2,1)S(1)}, ...), condition=%wide.region_11.12_spmd, body=%wide.region_10.11_spmd.sunk | while | flops 1075904512 | bytes 2955353 | solution.py:47
  173.0 3.7 %fusion.41 = bf16[2,512,256]{2,1,0:T(8,128)(2,1)} fusion(bf16[2,512,256]{2,1,0:T(8,128)(2,1)} %get-tuple-element.186, s32[]{:T(128)S(6)} %copy.40, bf16[64,64,256]{2,1,0:T(8,128)(2,1)} %get-tuple-element.195, bf16[512,64]{0,1:T(8,128)(2,1)S(1)} %dynamic-slice_bitcast_fusion.2, bf16[512,64]{0,1:T(8,128)(2,1)S(1)} %fusion.40), kind=kOutput, calls=%fused_computation.15.clone.1 | convolution fusion | flops 1075838976 | bytes 2752516 | tf_op jit(solution)/shard_map/while/body/eval_jaxpr/dot_general | solution.py:30
  176.7 3.7 %fusion.41 = bf16[2,512,256]{2,1,0:T(8,128)(2,1)} fusion(bf16[2,512,256]{2,1,0:T(8,128)(2,1)} %get-tuple-element.186, s32[]{:T(128)S(6)} %copy.40, bf16[64,64,256]{2,1,0:T(8,128)(2,1)} %get-tuple-element.195, bf16[512,64]{0,1:T(8,128)(2,1)S(1)} %dynamic-slice_bitcast_fusion.2, bf16[512,64]{0,1:T(8,128)(2,1)S(1)} %fusion.40), kind=kOutput, calls=%fused_computation.15.clone.1 | convolution fusion | flops 1075838976 | bytes 2752516 | tf_op jit(solution)/shard_map/while/body/eval_jaxpr/dot_general | solution.py:30
  180.4 31.4 %all-to-all-start.2 = ((bf16[8,128,256]{2,1,0:T(8,128)(2,1)}), bf16[8,128,256]{2,1,0:T(8,128)(2,1)S(1)}, u32[]{:S(2)}, u32[]{:S(2)}) async-start(bf16[8,128,256]{2,1,0:T(8,128)(2,1)} %bitcast.18), calls=%async_computation.3 | async-start | bytes 1048576 | tf_op jit(solution)/shard_map/all_to_all | solution.py:109
  211.8 9.5 %all-to-all-done.2 = bf16[8,128,256]{2,1,0:T(8,128)(2,1)S(1)} async-done(((bf16[8,128,256]{2,1,0:T(8,128)(2,1)}), bf16[8,128,256]{2,1,0:T(8,128)(2,1)S(1)}, u32[]{:S(2)}, u32[]{:S(2)}) %all-to-all-start.2) | async-done | bytes 524320 | tf_op jit(solution)/shard_map/all_to_all | solution.py:109
  221.3 1.9 gather_fusion
  223.4 39.6 %reduce-scatter.2.cloned.1.call-done = f32[256,512]{1,0:T(8,128)} async-done(((f32[8192,512]{1,0:T(8,128)}), f32[256,512]{1,0:T(8,128)}) %reduce-scatter.2.cloned.1.call-update) | async-done | bytes 524304 | tf_op jit(solution)/shard_map/reduce_scatter | solution.py:63
  262.9 1.2 fusion.15
  264.1 0.8 copy.20
  (34 shorter events, 2.2 us)
Async XLA Ops:
  6.5 256.4 %reduce-scatter.2.cloned.1.call-start = ((), (), s32[]{:S(2)}) async-start(), calls=%async_computation.4 | async-start | bytes 17301504 | tf_op jit(solution)/shard_map/reduce_scatter | solution.py:63
  16.9 0.7 copy-start
  16.9 29.9 %copy-start.2 = (bf16[64,64,256]{2,1,0:T(8,128)(2,1)S(1)}, bf16[64,64,256]{2,1,0:T(8,128)(2,1)}, u32[]{:S(2)}) copy-start(bf16[64,64,256]{2,1,0:T(8,128)(2,1)} %param.14) | copy-start | bytes 6291460
  22.2 11.0 %all-to-all-start = ((s32[8,1,128]{2,1,0:T(1,128)}), s32[8,1,128]{2,1,0:T(1,128)S(1)}, u32[]{:S(2)}, u32[]{:S(2)}) async-start(s32[8,1,128]{2,1,0:T(1,128)} %bitcast.15), calls=%async_computation.1 | async-start | bytes 8192 | tf_op jit(solution)/shard_map/all_to_all | solution.py:94
  33.2 13.6 %all-to-all-start.1 = ((bf16[8,128,256]{2,1,0:T(8,128)(2,1)}), bf16[8,128,256]{2,1,0:T(8,128)(2,1)S(1)}, u32[]{:S(2)}, u32[]{:S(2)}) async-start(bf16[8,128,256]{2,1,0:T(8,128)(2,1)} %bitcast.16), calls=%async_computation.2 | async-start | bytes 1048576 | tf_op jit(solution)/shard_map/all_to_all | solution.py:87
  172.9 90.1 %copy-start.1 = (f32[256]{0:T(256)S(1)}, f32[256]{0:T(256)}, u32[]{:S(2)}) copy-start(f32[256]{0:T(256)} %param.13) | copy-start | bytes 3076
  180.4 40.9 %all-to-all-start.2 = ((bf16[8,128,256]{2,1,0:T(8,128)(2,1)}), bf16[8,128,256]{2,1,0:T(8,128)(2,1)S(1)}, u32[]{:S(2)}, u32[]{:S(2)}) async-start(bf16[8,128,256]{2,1,0:T(8,128)(2,1)} %bitcast.18), calls=%async_computation.3 | async-start | bytes 1048576 | tf_op jit(solution)/shard_map/all_to_all | solution.py:109
Sparse Core Ops, SparseCore 0:
  17.0 245.8 reduce-scatter.1
where the time goes:
time: 276 us; the launch traced here: 272 us
  blocking collectives  121 us (44%)
  waiting for transfers between devices  58.4 us (21%)
  starting transfers between devices  42 us (15%)
  matrix products  20.3 us (7%)
  local copies, waits for them, and re-layouts  13.9 us (5%)
  between operations  13.5 us (5%)
  other arithmetic  3.12 us (1%)
    psum x1, blocking collectives, on_device(): rank_product = lax.psum(down_product, 'tp').astype(jnp.bfloat16)  121 us
    reduce_scatter x1, waiting for transfers between devices, on_device(): lax.psum_scatter(lax.dot_general(quantized_weight_codes, attention_output...  39.6 us
    all_to_all x1, starting transfers between devices, on_device(): lax.all_to_all(adapter_update.reshape(groups, capacity, feat_width), 'grp...  31.4 us
    dot_general x1, matrix products, on_device(): lax.dot_general(quantized_weight_codes, attention_output, (((0,), (1,)),...  10.3 us
    all_to_all x1, waiting for transfers between devices, on_device(): lax.all_to_all(adapter_update.reshape(groups, capacity, feat_width), 'grp...  9.47 us
    all_to_all x1, waiting for transfers between devices, on_device(): lax.all_to_all(send_rows.reshape(groups, capacity, feat_width), 'grp', sp...  8.32 us
    dot_general x2, matrix products, dense_up(): jnp.dot(spread, adapter_up_maps.reshape(adapters * rank_width, feat_width...  7.33 us
    all_to_all x1, starting transfers between devices, on_device(): lax.all_to_all(send_slots.reshape(groups, capacity), 'grp', split_axis=0,...  6.45 us
  transfers between devices with their start and end apart: 4, of which 4 were waited for; matrix products, arithmetic and copies ran while one was open for 9% of the time, Pallas kernels for 0%

commit v1 on v0

v1 whole, which is shorter than its diff:
```python
import jax
import jax.numpy as jnp
from jax import lax
from jax.experimental import pallas as pl
from jax.experimental.pallas import tpu as pltpu
from jax.sharding import Mesh, PartitionSpec as P

NX, NC, NY, NZ = 4, 2, 4, 8
GROUPS = NX * NC
CAP = 128
EXTRA = 16
ROWS = CAP + EXTRA
RANK = 64
F32, BF16 = jnp.float32, jnp.bfloat16
NT = (((1,), (1,)), ((), ()))


def params(mib=40):
    return pltpu.CompilerParams(vmem_limit_bytes=mib * 1024 * 1024)


def cost(flops, nbytes):
    return pl.CostEstimate(flops=flops, bytes_accessed=nbytes, transcendentals=0)


def pick_body(index_ref, w_ref, o_ref):
    o_ref[...] = w_ref[...]


def pick_block(weights, column, width):
    depth = weights.shape[0]
    return pl.pallas_call(
        pick_body,
        out_shape=jax.ShapeDtypeStruct((depth, NY * width), weights.dtype),
        grid_spec=pltpu.PrefetchScalarGridSpec(
            num_scalar_prefetch=1,
            grid=(NY,),
            in_specs=[pl.BlockSpec((depth, width), lambda i, at: (0, i * NZ + at[0]))],
            out_specs=pl.BlockSpec((depth, width), lambda i, at: (0, i)),
        ),
        compiler_params=params(),
        cost_estimate=cost(0, 4 * depth * NY * width),
    )(column, weights)


def route_body(owner_ref, slot_ref, rows_ref, send_ref, place_ref):
    tokens = rows_ref.shape[0]
    owner = owner_ref[...]
    member = lax.broadcasted_iota(jnp.int32, (GROUPS, tokens), 0) == owner
    before = lax.broadcasted_iota(jnp.int32, (tokens, tokens), 0) < lax.broadcasted_iota(
        jnp.int32, (tokens, tokens), 1
    )
    earlier = jnp.dot(
        member.astype(F32).astype(BF16), before.astype(F32).astype(BF16), preferred_element_type=F32
    )
    position = jnp.sum(jnp.where(member, earlier, 0.0), axis=0, keepdims=True)
    target = owner.astype(F32) * CAP + position
    rows = rows_ref[...]
    slots = jnp.broadcast_to(slot_ref[...].astype(F32), (EXTRA, tokens)).astype(BF16)
    for g in range(GROUPS):
        spot = lax.broadcasted_iota(jnp.int32, (CAP, tokens), 0).astype(F32) + float(g * CAP)
        select = jnp.where(spot == target, 1.0, 0.0).astype(BF16)
        send_ref[g, :CAP, :] = jnp.dot(select, rows, preferred_element_type=F32).astype(BF16)
        sent = lax.dot_general(slots, select, NT, preferred_element_type=F32).astype(BF16)
        send_ref[g, CAP:, :CAP] = sent
        send_ref[g, CAP:, CAP:] = sent
    same = lax.broadcasted_iota(jnp.int32, (tokens, tokens), 0) == lax.broadcasted_iota(
        jnp.int32, (tokens, tokens), 1
    )
    column = jnp.sum(jnp.where(same, target, 0.0), axis=1, keepdims=True)
    place_ref[...] = jnp.broadcast_to(column, place_ref.shape)


def route(owner, slot, rows):
    tokens, width = rows.shape
    return pl.pallas_call(
        route_body,
        out_shape=(
            jax.ShapeDtypeStruct((GROUPS, ROWS, width), BF16),
            jax.ShapeDtypeStruct((tokens, 128), F32),
        ),
        compiler_params=params(),
        cost_estimate=cost(2 * GROUPS * CAP * tokens * width, 4 * GROUPS * ROWS * width),
    )(owner, slot, rows)


def down_body(got_ref, map_ref, low_ref, diff_ref, rows_ref, total_ref):
    step = pl.program_id(0)
    half = lax.broadcasted_iota(jnp.int32, (CAP, 128), 1) >= RANK

    @pl.when(step == 0)
    def _():
        same = lax.broadcasted_iota(jnp.int32, (CAP, CAP), 0) == lax.broadcasted_iota(
            jnp.int32, (CAP, CAP), 1
        )
        ones = jnp.ones((CAP, 128), BF16)
        for g in range(GROUPS):
            rows_ref[g * CAP : (g + 1) * CAP, :] = got_ref[g, :CAP, :]
            slot = got_ref[g, CAP:, :CAP].astype(F32)[:1, :]
            spread = jnp.where(same, slot, 0.0).astype(BF16)
            slots = jnp.dot(spread, ones, preferred_element_type=F32)
            diff_ref[g * CAP : (g + 1) * CAP, :] = slots - jnp.where(half, 1.0, 0.0)
        total_ref[...] = jnp.zeros_like(total_ref)

    wide = map_ref.shape[0]
    for n in range(wide // 256):
        product = lax.dot_general(
            rows_ref[...], map_ref[n * 256 : (n + 1) * 256, :], NT, preferred_element_type=F32
        )
        base = (step * (wide // RANK) + n * 4).astype(F32)
        total_ref[...] += jnp.where(diff_ref[...] == base, product[:, :128], 0.0) + jnp.where(
            diff_ref[...] == base + 2.0, product[:, 128:], 0.0
        )

    @pl.when(step == pl.num_programs(0) - 1)
    def _():
        whole = total_ref[...]
        whole = whole + pltpu.roll(whole, RANK, 1)
        packed = whole.shape[0] // 2
        left = lax.broadcasted_iota(jnp.int32, (packed, 128), 1) < RANK
        low_ref[...] = jnp.where(left, whole[:packed], whole[packed:])


def down(got, maps, steps=8):
    wide, width = maps.shape
    rows = GROUPS * CAP
    return pl.pallas_call(
        down_body,
        out_shape=(
            jax.ShapeDtypeStruct((rows // 2, 128), F32),
            jax.ShapeDtypeStruct((rows, 128), F32),
        ),
        grid=(steps,),
        in_specs=[
            pl.BlockSpec(got.shape, lambda i: (0, 0, 0)),
            pl.BlockSpec((wide // steps, width), lambda i: (i, 0)),
        ],
        out_specs=(
            pl.BlockSpec((rows // 2, 128), lambda i: (0, 0)),
            pl.BlockSpec((rows, 128), lambda i: (0, 0)),
        ),
        scratch_shapes=[pltpu.VMEM((rows, width), BF16), pltpu.VMEM((rows, 128), F32)],
        compiler_params=params(),
        cost_estimate=cost(2 * rows * wide * width, 2 * wide * width),
    )(got, maps)


def total_body(parts_ref, o_ref):
    whole = jnp.sum(parts_ref[...], axis=0).astype(BF16)
    o_ref[...] = jnp.broadcast_to(whole[None], o_ref.shape)


def total(parts):
    return pl.pallas_call(
        total_body,
        out_shape=jax.ShapeDtypeStruct(parts.shape, BF16),
        compiler_params=params(),
        cost_estimate=cost(parts.size, 6 * parts.size),
    )(parts)


def up_body(low_ref, diff_ref, map_ref, o_ref, twice_ref, total_ref):
    step = pl.program_id(0)

    @pl.when(step == 0)
    def _():
        packed = low_ref[...].astype(F32)
        swapped = pltpu.roll(packed, RANK, 1)
        left = lax.broadcasted_iota(jnp.int32, packed.shape, 1) < RANK
        twice_ref[: packed.shape[0], :] = jnp.where(left, packed, swapped)
        twice_ref[packed.shape[0] :, :] = jnp.where(left, swapped, packed)
        total_ref[...] = jnp.zeros_like(total_ref)

    wide = map_ref.shape[0]
    diff, twice = diff_ref[...], twice_ref[...]
    pieces = []
    for n in range(wide // 128):
        base = (step * (wide // RANK) + n * 2).astype(F32)
        pieces.append(jnp.where(diff == base, twice, 0.0).astype(BF16))
    total_ref[...] += jnp.dot(
        jnp.concatenate(pieces, axis=1), map_ref[...], preferred_element_type=F32
    )

    @pl.when(step == pl.num_programs(0) - 1)
    def _():
        o_ref[...] = total_ref[...].astype(BF16).reshape(o_ref.shape)


def up(low, diff, maps, steps=8):
    wide, width = maps.shape
    rows = GROUPS * CAP
    return pl.pallas_call(
        up_body,
        out_shape=jax.ShapeDtypeStruct((GROUPS, CAP, width), BF16),
        grid=(steps,),
        in_specs=[
            pl.BlockSpec(low.shape, lambda i: (0, 0)),
            pl.BlockSpec(diff.shape, lambda i: (0, 0)),
            pl.BlockSpec((wide // steps, width), lambda i: (i, 0)),
        ],
        out_specs=pl.BlockSpec((GROUPS, CAP, width), lambda i: (0, 0, 0)),
        scratch_shapes=[pltpu.VMEM((rows, 128), F32), pltpu.VMEM((rows, width), F32)],
        compiler_params=params(),
        cost_estimate=cost(2 * rows * wide * width, 2 * wide * width),
    )(low, diff, maps)


def base_body(index_ref, a_ref, *refs):
    o_ref = refs[-1]
    whole = jnp.zeros(o_ref.shape[1:], F32)
    for core in range(NC):
        own, left, right, top, bottom = refs[5 * core : 5 * core + 5]
        far = jnp.concatenate([top[...], bottom[...]], axis=0)
        for at, block in enumerate((own[...], left[...], right[...], far)):
            whole += jnp.dot(
                a_ref[index_ref[4 * core + at]], block, preferred_element_type=F32
            )
    o_ref[0] = whole.astype(BF16)


def base_product(index, gathered, pieces, width):
    depth = gathered.shape[2]
    tokens = gathered.shape[1]
    specs = [
        pl.BlockSpec((piece.shape[0], width), lambda i, at: (0, i)) for piece in pieces
    ]
    return pl.pallas_call(
        base_body,
        out_shape=jax.ShapeDtypeStruct((NY, tokens, width), BF16),
        grid_spec=pltpu.PrefetchScalarGridSpec(
            num_scalar_prefetch=1,
            grid=(NY,),
            in_specs=[pl.BlockSpec(gathered.shape, lambda i, at: (0, 0, 0))] + specs,
            out_specs=pl.BlockSpec((1, tokens, width), lambda i, at: (i, 0, 0)),
        ),
        compiler_params=params(),
        cost_estimate=cost(2 * tokens * NZ * depth * NY * width, 8 * 1024 * 1024),
    )(index, gathered, *pieces)


def final_body(parts_ref, scale_ref, place_ref, back_ref, o_ref):
    summed = jnp.sum(parts_ref[...].astype(F32), axis=0)
    place = place_ref[...]
    lane = lax.broadcasted_iota(jnp.int32, place.shape, 1).astype(F32)
    pieces = [
        jnp.where(place == lane + float(g * CAP), 1.0, 0.0).astype(BF16) for g in range(GROUPS)
    ]
    delta = jnp.dot(
        jnp.concatenate(pieces, axis=1),
        back_ref[...].reshape(GROUPS * CAP, back_ref.shape[2]),
        preferred_element_type=F32,
    )
    o_ref[...] = (summed * scale_ref[...] + delta).astype(BF16)


def final(parts, scale, place, back):
    return pl.pallas_call(
        final_body,
        out_shape=jax.ShapeDtypeStruct(parts.shape[1:], BF16),
        compiler_params=params(),
        cost_estimate=cost(2 * GROUPS * CAP * parts.shape[1] * parts.shape[2], 4 * 1024 * 1024),
    )(parts, scale, place, back)


def shift(a, axis, by, size):
    return lax.ppermute(a, axis, [(i, (i + by) % size) for i in range(size)])


def on_device(rows, weights, scale, down_maps, up_maps, owner, slot):
    tokens, width = rows.shape
    x, c, z = lax.axis_index("x"), lax.axis_index("c"), lax.axis_index("z")

    turn = x + NX * c
    picked = pick_block(weights, ((z + turn) % NZ).reshape(1), width)
    pairs = []
    for at in range(NX * NC * NZ):
        i, j, k = at // (NC * NZ), at // NZ % NC, at % NZ
        pairs.append((at, (i * NC + j) * NZ + (k + i + NX * j) % NZ))
    own = lax.ppermute(picked, ("x", "c", "z"), pairs)
    gathered = lax.all_gather(rows, "z")

    send, place = route(owner.reshape(1, tokens), slot.reshape(1, tokens), rows)
    got = lax.all_to_all(send, ("x", "c"), 0, 0, tiled=True)

    left = shift(own, "x", 1, NX)
    right = shift(own, "x", -1, NX)
    depth = own.shape[0] // 2
    top = shift(left[:depth], "x", 1, NX)
    bottom = shift(right[depth:], "x", -1, NX)
    mine = [own, left, right, top, bottom]
    other = [shift(piece, "c", 1, NC) for piece in mine]

    low_part, diff = down(got, down_maps.reshape(-1, width))
    low_part = low_part.reshape(NY * NZ, -1, 128)
    low_all = total(lax.all_to_all(low_part, ("y", "z"), 0, 0, tiled=True))
    low = lax.all_to_all(low_all, ("y", "z"), 0, 0, tiled=True).reshape(-1, 128)
    delta = up(low, diff, up_maps.reshape(-1, width))
    back = lax.all_to_all(delta, ("x", "c"), 0, 0, tiled=True)

    turns = [x, x - 1, x + 1, x + 2]
    index = jnp.stack(
        [(z - (t % NX) - NX * k) % NZ for k in (c, 1 - c) for t in turns]
    ).astype(jnp.int32)
    parts = base_product(index, gathered, mine + other, width)
    parts = lax.all_to_all(parts, "y", 0, 0, tiled=True)
    return final(parts, scale.reshape(1, width), place, back)


def solution(mesh):
    fine = Mesh(mesh.devices.reshape(NX, NC, NY, NZ), ("x", "c", "y", "z"))
    grp, tp = ("x", "c"), ("y", "z")
    in_specs = (
        P(grp, tp),
        P(tp, None),
        P(tp),
        P(grp, None, tp),
        P(grp, None, tp),
        P(grp, None),
        P(grp),
    )
    return jax.shard_map(
        on_device, mesh=fine, in_specs=in_specs, out_specs=P(grp, tp), check_vma=False
    )
```

time: 276 us -> 141 us (0.51); the launches traced: 272 us -> 140 us
  blocking collectives: 121 us -> 17.3 us
  waiting for transfers between devices: 58.4 us -> 16.9 us
  matrix products: 20.3 us -> 0 us
  starting transfers between devices: 42 us -> 60.9 us
  Pallas kernels: 0 us -> 18.3 us
  other arithmetic: 3.12 us -> 0 us
    psum x1 -> x0, blocking collectives: 121 us -> none  [on_device(): rank_product = lax.psum(down_product, 'tp').astype(jnp.bfloat16)]
    reduce_scatter x1 -> x0, waiting for transfers between devices: 39.6 us -> none  [on_device(): lax.psum_scatter(lax.dot_general(quantized_weight_codes, attention_output...]
    ppermute x0 -> x10, starting transfers between devices: none -> 31.8 us  [the longest x9 22.1 us: shift(): return lax.ppermute(a, axis, [(i, (i + by) % size) for i in range(size)])]
    dot_general x5 -> x0, matrix products: 20.3 us -> none  [the longest x1 10.3 us: on_device(): lax.dot_general(quantized_weight_codes, attention_output, (((0,), (1,)),...]
    pallas_call x0 -> x7, Pallas kernels: none -> 18.3 us  [the longest x1 5 us: base_product(): pl.pallas_call(base_body, out_shape=jax.ShapeDtypeStruct((NY, tokens, wid...]
    all_to_all x0 -> x1, blocking collectives: none -> 17.3 us  [on_device(): parts = lax.all_to_all(parts, 'y', 0, 0, tiled=True)]
    all_to_all x3 -> x4, starting transfers between devices: 42 us -> 29.1 us  [the longest x1 11.9 us: on_device(): back = lax.all_to_all(delta, ('x', 'c'), 0, 0, tiled=True)]
    unnamed x7 -> x28, local copies, waits for them, and re-layouts: 0.71 us -> 12.5 us
  transfers between devices with their start and end apart: 4 -> 15, of which waited for: 4 -> 3; matrix products, arithmetic and copies ran while one was open for 9% -> 1% of each run, Pallas kernels for 0% -> 12%
where the time goes in v1:
time: 141 us; the launch traced here: 140 us
  starting transfers between devices  60.9 us (43%)
  Pallas kernels  18.3 us (13%)
  blocking collectives  17.3 us (12%)
  waiting for transfers between devices  16.9 us (12%)
  between operations  13.6 us (10%)
  local copies, waits for them, and re-layouts  13.3 us (9%)
    ppermute x9, starting transfers between devices, shift(): return lax.ppermute(a, axis, [(i, (i + by) % size) for i in range(size)])  22.1 us
    all_to_all x1, blocking collectives, on_device(): parts = lax.all_to_all(parts, 'y', 0, 0, tiled=True)  17.3 us
    unnamed x28, local copies, waits for them, and re-layouts  12.5 us
    all_to_all x1, starting transfers between devices, on_device(): back = lax.all_to_all(delta, ('x', 'c'), 0, 0, tiled=True)  11.9 us
    ppermute x1, starting transfers between devices, on_device(): own = lax.ppermute(picked, ('x', 'c', 'z'), pairs)  9.65 us
    all_to_all x1, starting transfers between devices, on_device(): low_all = total(lax.all_to_all(low_part, ('y', 'z'), 0, 0, tiled=True))  9.21 us
    all_to_all x1, waiting for transfers between devices, on_device(): low_all = total(lax.all_to_all(low_part, ('y', 'z'), 0, 0, tiled=True))  7.34 us
    ppermute x1, waiting for transfers between devices, on_device(): own = lax.ppermute(picked, ('x', 'c', 'z'), pairs)  6.98 us
  transfers between devices with their start and end apart: 15, of which 3 were waited for; matrix products, arithmetic and copies ran while one was open for 1% of the time, Pallas kernels for 12%

profile of v1, /device:TPU:1, one launch (start us, length us, event | category | flops | bytes accessed | tf_op | source)
XLA Modules:
  0.0 140.3 jit_solution(17581052190637432438)
XLA Ops:
  7.3 2.2 %copy-done = bf16[256,8192]{1,0:T(8,128)(2,1)S(1)} copy-done((bf16[256,8192]{1,0:T(8,128)(2,1)S(1)}, bf16[256,8192]{1,0:T(8,128)(2,1)}, u32[]{:S(2)}) %copy-start) | copy-done | bytes 4194328
  9.7 9.6 %collective-permute-start = (bf16[256,1024]{1,0:T(8,128)(2,1)S(1)}, bf16[256,1024]{1,0:T(8,128)(2,1)S(1)}, u32[]{:S(2)}, u32[]{:S(2)}) collective-permute-start(bf16[256,1024]{1,0:T(8,128)(2,1)S(1)} %shard_map.73), channel_id=1, source_target_pairs={{0,0},{1,1},{2,2},{3,3},{4,4},{5,5},{6,6},{7,7},{32,36},{33,37},{3... | collective-permute-start | bytes 1572872 | tf_op jit(solution)/shard_map/ppermute | solution.py:279
  19.4 1.7 %shard_map.75 = (bf16[8,144,256]{2,1,0:T(8,128)(2,1)}, f32[512,128]{1,0:T(8,128)S(1)}) custom-call(s32[1,512]{1,0:T(1,128)S(1)} %bitcast.22, s32[1,512]{1,0:T(1,128)S(1)} %bitcast.23, bf16[512,256]{1,0:T(8,128)(2,1)S(1)} %copy-done.1), custom_call_target="tpu_custom_call" | custom-call | flops 268435456 | bytes 1179648 | tf_op jit(solution)/shard_map/pallas_call | solution.py:76
  21.1 3.5 %all-to-all-start.1 = ((bf16[8,144,256]{2,1,0:T(8,128)(2,1)}), bf16[8,144,256]{2,1,0:T(8,128)(2,1)S(1)}, u32[]{:S(2)}, u32[]{:S(2)}) async-start(bf16[8,144,256]{2,1,0:T(8,128)(2,1)} %get-tuple-element.10), calls=%async_computation.1 | async-start | bytes 1179648 | tf_op jit(solution)/shard_map/all_to_all | solution.py:283
  24.7 7.0 %collective-permute-done.refs_0_ = bf16[256,1024]{1,0:T(8,128)(2,1)S(1)} collective-permute-done((bf16[256,1024]{1,0:T(8,128)(2,1)S(1)}, bf16[256,1024]{1,0:T(8,128)(2,1)S(1)}, u32[]{:S(2)}, u32[]{:S(2)}) %collective-permute-start) | collective-permute-done | bytes 524320 | tf_op jit(solution)/shard_map/ppermute | solution.py:279
  31.6 13.2 %collective-permute-start.1 = (bf16[256,1024]{1,0:T(8,128)(2,1)S(1)}, bf16[256,1024]{1,0:T(8,128)(2,1)S(1)}, u32[]{:S(2)}, u32[]{:S(2)}) collective-permute-start(bf16[256,1024]{1,0:T(8,128)(2,1)S(1)} %collective-permute-done.refs_0_), channel_id=1, source_target_pairs={{0,64},{64,128},{128,192},{192,0},{1,65},{65,129},{129,193},{193,1... | collective-permute-start | bytes 1572872 | tf_op jit(solution)/shard_map/ppermute | solution.py:266
  44.9 1.6 %copy-done.3 = bf16[64,64,256]{2,1,0:T(8,128)(2,1)S(1)} copy-done((bf16[64,64,256]{2,1,0:T(8,128)(2,1)S(1)}, bf16[64,64,256]{2,1,0:T(8,128)(2,1)}, u32[]{:S(2)}) %copy-start.3) | copy-done | bytes 2097176
  46.5 5.0 %shard_map.76 = (f32[512,128]{1,0:T(8,128)}, f32[1024,128]{1,0:T(8,128)S(1)}) custom-call(bf16[8,144,256]{2,1,0:T(8,128)(2,1)S(1)} %all-to-all-done.1.got_ref, bf16[4096,256]{1,0:T(8,128)(2,1)S(1)} %bitcast.19), custom_call_target="tpu_custom_call" | custom-call | flops 2147483648 | bytes 2097152 | tf_op jit(solution)/shard_map/pallas_call | solution.py:127
  52.2 9.2 %all-to-all-start.2 = ((f32[32,16,128]{2,1,0:T(8,128)}), f32[32,16,128]{2,1,0:T(8,128)S(1)}, u32[]{:S(2)}, u32[]{:S(2)}) async-start(f32[32,16,128]{2,1,0:T(8,128)} %bitcast.14), calls=%async_computation.2 | async-start | bytes 524288 | tf_op jit(solution)/shard_map/all_to_all | solution.py:295
  62.3 1.5 %collective-permute-start.3 = (bf16[128,1024]{1,0:T(8,128)(2,1)}, bf16[128,1024]{1,0:T(8,128)(2,1)}, u32[]{:S(2)}, u32[]{:S(2)}) collective-permute-start(bf16[128,1024]{1,0:T(8,128)(2,1)} %slice.8), channel_id=1, source_target_pairs={{0,64},{64,128},{128,192},{192,0},{1,65},{65,129},{129,193},{193,1... | collective-permute-start | bytes 786440 | tf_op jit(solution)/shard_map/ppermute | solution.py:266
  63.8 7.3 %all-to-all-done.2.parts_ref = f32[32,16,128]{2,1,0:T(8,128)S(1)} async-done(((f32[32,16,128]{2,1,0:T(8,128)}), f32[32,16,128]{2,1,0:T(8,128)S(1)}, u32[]{:S(2)}, u32[]{:S(2)}) %all-to-all-start.2) | async-done | bytes 262176 | tf_op jit(solution)/shard_map/all_to_all | solution.py:295
  71.8 4.5 %all-to-all-start.3 = ((bf16[32,16,128]{2,1,0:T(8,128)(2,1)}), bf16[32,16,128]{2,1,0:T(8,128)(2,1)S(1)}, u32[]{:S(2)}, u32[]{:S(2)}) async-start(bf16[32,16,128]{2,1,0:T(8,128)(2,1)} %shard_map.77), calls=%async_computation.3 | async-start | bytes 262144 | tf_op jit(solution)/shard_map/all_to_all | solution.py:296
  76.3 6.3 %collective-permute-start.5 = (bf16[256,1024]{1,0:T(8,128)(2,1)S(1)}, bf16[256,1024]{1,0:T(8,128)(2,1)S(1)}, u32[]{:S(2)}, u32[]{:S(2)}) collective-permute-start(bf16[256,1024]{1,0:T(8,128)(2,1)S(1)} %collective-permute-done.refs_0_), channel_id=1, source_target_pairs={{0,32},{32,0},{1,33},{33,1},{2,34},{34,2},{3,35},{35,3},{4,36},{36... | collective-permute-start | bytes 1572872 | tf_op jit(solution)/shard_map/ppermute | solution.py:266
  83.6 1.8 %all-to-all-done.3 = bf16[32,16,128]{2,1,0:T(8,128)(2,1)S(1)} async-done(((bf16[32,16,128]{2,1,0:T(8,128)(2,1)}), bf16[32,16,128]{2,1,0:T(8,128)(2,1)S(1)}, u32[]{:S(2)}, u32[]{:S(2)}) %all-to-all-start.3) | async-done | bytes 131104 | tf_op jit(solution)/shard_map/all_to_all | solution.py:296
  85.4 1.6 %copy-done.4 = bf16[64,64,256]{2,1,0:T(8,128)(2,1)S(1)} copy-done((bf16[64,64,256]{2,1,0:T(8,128)(2,1)S(1)}, bf16[64,64,256]{2,1,0:T(8,128)(2,1)}, u32[]{:S(2)}) %copy-start.4) | copy-done | bytes 2097176
  87.0 1.0 copy-done.13
  88.0 4.5 %shard_map.78 = bf16[8,128,256]{2,1,0:T(8,128)(2,1)} custom-call(bf16[512,128]{1,0:T(8,128)(2,1)S(1)} %bitcast.17, f32[1024,128]{1,0:T(8,128)S(1)} %copy-done.13, bf16[4096,256]{1,0:T(8,128)(2,1)S(1)} %bitcast.20), custom_call_target="tpu_custom_call" | custom-call | flops 2147483648 | bytes 2097152 | tf_op jit(solution)/shard_map/pallas_call | solution.py:192
  92.6 11.9 %all-to-all-start.4 = ((bf16[8,128,256]{2,1,0:T(8,128)(2,1)}), bf16[8,128,256]{2,1,0:T(8,128)(2,1)S(1)}, u32[]{:S(2)}, u32[]{:S(2)}) async-start(bf16[8,128,256]{2,1,0:T(8,128)(2,1)} %shard_map.78), calls=%async_computation.4 | async-start | bytes 1048576 | tf_op jit(solution)/shard_map/all_to_all | solution.py:298
  106.2 1.6 %copy-done.5 = bf16[4096,256]{1,0:T(8,128)(2,1)S(1)} copy-done((bf16[4096,256]{1,0:T(8,128)(2,1)S(1)}, bf16[4096,256]{1,0:T(8,128)(2,1)}, u32[]{:S(2)}) %copy-start.5) | copy-done | bytes 2097176
  107.8 1.0 copy-done.7
  108.9 1.0 copy-done.9
  109.9 5.0 %shard_map.74 = bf16[4,512,256]{2,1,0:T(8,128)(2,1)S(1)} custom-call(s32[8]{0:T(128)S(1)} %stack.35.index_ref, bf16[8,512,256]{2,1,0:T(8,128)(2,1)S(1)} %bitcast.21, bf16[256,1024]{1,0:T(8,128)(2,1)S(1)} %collective-permute-done.refs_0_, bf16[256,1024]{1,0:T(8,128)(2,1)S(1)} %collective-permute-done.1.refs_1_, ...), custom_call_target="tpu_custom_call" | custom-call | flops 2147483648 | bytes 8388608 | tf_op jit(solution)/shard_map/pallas_call | solution.py:227
  114.9 17.3 %all_to_all.25.parts_ref = bf16[4,512,256]{2,1,0:T(8,128)(2,1)S(1)} all-to-all(bf16[4,512,256]{2,1,0:T(8,128)(2,1)S(1)} %shard_map.74), channel_id=1, replica_groups=mesh['x'=4,'c'=2,'y'=4,'z'=8] {'y'}, dimensions={0} | all-to-all | bytes 2097152 | tf_op jit(solution)/shard_map/all_to_all | solution.py:305
  132.3 1.2 shard_map.79
  (46 shorter events, 6.1 us)
Async XLA Ops:
  6.5 99.7 %all-gather.3.cloned.1.call-start = ((), (), s32[]{:S(2)}) async-start(), calls=%async_computation.5 | async-start | bytes 2359296 | tf_op jit(solution)/shard_map/all_gather | solution.py:280
  7.3 2.2 %copy-start = (bf16[256,8192]{1,0:T(8,128)(2,1)S(1)}, bf16[256,8192]{1,0:T(8,128)(2,1)}, u32[]{:S(2)}) copy-start(bf16[256,8192]{1,0:T(8,128)(2,1)} %w_ref.1) | copy-start | bytes 12582916
  9.5 9.9 %copy-start.1 = (bf16[512,256]{1,0:T(8,128)(2,1)S(1)}, bf16[512,256]{1,0:T(8,128)(2,1)}, u32[]{:S(2)}) copy-start(bf16[512,256]{1,0:T(8,128)(2,1)} %rows_ref.1) | copy-start | bytes 786436
  9.5 9.9 %copy-start.10 = (s32[512,1]{0,1:T(1,128)S(1)}, s32[512,1]{0,1:T(1,128)}, u32[]{:S(2)}) copy-start(s32[512,1]{0,1:T(1,128)} %param.12) | copy-start | bytes 6148
  9.5 9.9 %copy-start.11 = (s32[512]{0:T(512)S(1)}, s32[512]{0:T(512)}, u32[]{:S(2)}) copy-start(s32[512]{0:T(512)} %param.13) | copy-start | bytes 6148
  9.7 21.9 %collective-permute-start = (bf16[256,1024]{1,0:T(8,128)(2,1)S(1)}, bf16[256,1024]{1,0:T(8,128)(2,1)S(1)}, u32[]{:S(2)}, u32[]{:S(2)}) collective-permute-start(bf16[256,1024]{1,0:T(8,128)(2,1)S(1)} %shard_map.73), channel_id=1, source_target_pairs={{0,0},{1,1},{2,2},{3,3},{4,4},{5,5},{6,6},{7,7},{32,36},{33,37},{3... | collective-permute-start | bytes 1572872 | tf_op jit(solution)/shard_map/ppermute | solution.py:279
  21.1 23.7 %all-to-all-start.1 = ((bf16[8,144,256]{2,1,0:T(8,128)(2,1)}), bf16[8,144,256]{2,1,0:T(8,128)(2,1)S(1)}, u32[]{:S(2)}, u32[]{:S(2)}) async-start(bf16[8,144,256]{2,1,0:T(8,128)(2,1)} %get-tuple-element.10), calls=%async_computation.1 | async-start | bytes 1179648 | tf_op jit(solution)/shard_map/all_to_all | solution.py:283
  31.6 29.8 %collective-permute-start.2 = (bf16[256,1024]{1,0:T(8,128)(2,1)S(1)}, bf16[256,1024]{1,0:T(8,128)(2,1)S(1)}, u32[]{:S(2)}, u32[]{:S(2)}) collective-permute-start(bf16[256,1024]{1,0:T(8,128)(2,1)S(1)} %collective-permute-done.refs_0_), channel_id=1, source_target_pairs={{0,192},{64,0},{128,64},{192,128},{1,193},{65,1},{129,65},{193,129... | collective-permute-start | bytes 1572872 | tf_op jit(solution)/shard_map/ppermute | solution.py:266
  31.6 29.9 %collective-permute-start.1 = (bf16[256,1024]{1,0:T(8,128)(2,1)S(1)}, bf16[256,1024]{1,0:T(8,128)(2,1)S(1)}, u32[]{:S(2)}, u32[]{:S(2)}) collective-permute-start(bf16[256,1024]{1,0:T(8,128)(2,1)S(1)} %collective-permute-done.refs_0_), channel_id=1, source_target_pairs={{0,64},{64,128},{128,192},{192,0},{1,65},{65,129},{129,193},{193,1... | collective-permute-start | bytes 1572872 | tf_op jit(solution)/shard_map/ppermute | solution.py:266
  44.9 1.6 %copy-start.3 = (bf16[64,64,256]{2,1,0:T(8,128)(2,1)S(1)}, bf16[64,64,256]{2,1,0:T(8,128)(2,1)}, u32[]{:S(2)}) copy-start(bf16[64,64,256]{2,1,0:T(8,128)(2,1)} %param.10) | copy-start | bytes 6291460
  52.2 18.9 %all-to-all-start.2 = ((f32[32,16,128]{2,1,0:T(8,128)}), f32[32,16,128]{2,1,0:T(8,128)S(1)}, u32[]{:S(2)}, u32[]{:S(2)}) async-start(f32[32,16,128]{2,1,0:T(8,128)} %bitcast.14), calls=%async_computation.2 | async-start | bytes 524288 | tf_op jit(solution)/shard_map/all_to_all | solution.py:295
  61.5 21.6 %collective-permute-start.4 = (bf16[128,1024]{1,0:T(8,128)(2,1)S(1)}, bf16[128,1024]{1,0:T(8,128)(2,1)}, u32[]{:S(2)}, u32[]{:S(2)}) collective-permute-start(bf16[128,1024]{1,0:T(8,128)(2,1)S(1)} %slice.9), channel_id=1, source_target_pairs={{0,192},{64,0},{128,64},{192,128},{1,193},{65,1},{129,65},{193,129... | collective-permute-start | bytes 786440 | tf_op jit(solution)/shard_map/ppermute | solution.py:266
  62.3 20.9 %collective-permute-start.3 = (bf16[128,1024]{1,0:T(8,128)(2,1)}, bf16[128,1024]{1,0:T(8,128)(2,1)}, u32[]{:S(2)}, u32[]{:S(2)}) collective-permute-start(bf16[128,1024]{1,0:T(8,128)(2,1)} %slice.8), channel_id=1, source_target_pairs={{0,64},{64,128},{128,192},{192,0},{1,65},{65,129},{129,193},{193,1... | collective-permute-start | bytes 786440 | tf_op jit(solution)/shard_map/ppermute | solution.py:266
  71.8 13.6 %all-to-all-start.3 = ((bf16[32,16,128]{2,1,0:T(8,128)(2,1)}), bf16[32,16,128]{2,1,0:T(8,128)(2,1)S(1)}, u32[]{:S(2)}, u32[]{:S(2)}) async-start(bf16[32,16,128]{2,1,0:T(8,128)(2,1)} %shard_map.77), calls=%async_computation.3 | async-start | bytes 262144 | tf_op jit(solution)/shard_map/all_to_all | solution.py:296
  76.3 28.3 %collective-permute-start.5 = (bf16[256,1024]{1,0:T(8,128)(2,1)S(1)}, bf16[256,1024]{1,0:T(8,128)(2,1)S(1)}, u32[]{:S(2)}, u32[]{:S(2)}) collective-permute-start(bf16[256,1024]{1,0:T(8,128)(2,1)S(1)} %collective-permute-done.refs_0_), channel_id=1, source_target_pairs={{0,32},{32,0},{1,33},{33,1},{2,34},{34,2},{3,35},{35,3},{4,36},{36... | collective-permute-start | bytes 1572872 | tf_op jit(solution)/shard_map/ppermute | solution.py:266
  82.6 22.8 %collective-permute-start.7 = (bf16[256,1024]{1,0:T(8,128)(2,1)S(1)}, bf16[256,1024]{1,0:T(8,128)(2,1)S(1)}, u32[]{:S(2)}, u32[]{:S(2)}) collective-permute-start(bf16[256,1024]{1,0:T(8,128)(2,1)S(1)} %collective-permute-done.2.refs_2_), channel_id=1, source_target_pairs={{0,32},{32,0},{1,33},{33,1},{2,34},{34,2},{3,35},{35,3},{4,36},{36... | collective-permute-start | bytes 1572872 | tf_op jit(solution)/shard_map/ppermute | solution.py:266
  82.7 23.5 %collective-permute-start.6 = (bf16[256,1024]{1,0:T(8,128)(2,1)S(1)}, bf16[256,1024]{1,0:T(8,128)(2,1)}, u32[]{:S(2)}, u32[]{:S(2)}) collective-permute-start(bf16[256,1024]{1,0:T(8,128)(2,1)S(1)} %collective-permute-done.1.refs_1_), channel_id=1, source_target_pairs={{0,32},{32,0},{1,33},{33,1},{2,34},{34,2},{3,35},{35,3},{4,36},{36... | collective-permute-start | bytes 1572872 | tf_op jit(solution)/shard_map/ppermute | solution.py:266
  83.1 23.1 %collective-permute-start.9 = (bf16[128,1024]{1,0:T(8,128)(2,1)}, bf16[128,1024]{1,0:T(8,128)(2,1)}, u32[]{:S(2)}, u32[]{:S(2)}) collective-permute-start(bf16[128,1024]{1,0:T(8,128)(2,1)} %collective-permute-done.4.refs_4_), channel_id=1, source_target_pairs={{0,32},{32,0},{1,33},{33,1},{2,34},{34,2},{3,35},{35,3},{4,36},{36... | collective-permute-start | bytes 786440 | tf_op jit(solution)/shard_map/ppermute | solution.py:266
  83.2 23.0 %collective-permute-start.8 = (bf16[128,1024]{1,0:T(8,128)(2,1)}, bf16[128,1024]{1,0:T(8,128)(2,1)}, u32[]{:S(2)}, u32[]{:S(2)}) collective-permute-start(bf16[128,1024]{1,0:T(8,128)(2,1)} %collective-permute-done.3.refs_3_), channel_id=1, source_target_pairs={{0,32},{32,0},{1,33},{33,1},{2,34},{34,2},{3,35},{35,3},{4,36},{36... | collective-permute-start | bytes 786440 | tf_op jit(solution)/shard_map/ppermute | solution.py:266
  85.4 1.6 %copy-start.4 = (bf16[64,64,256]{2,1,0:T(8,128)(2,1)S(1)}, bf16[64,64,256]{2,1,0:T(8,128)(2,1)}, u32[]{:S(2)}) copy-start(bf16[64,64,256]{2,1,0:T(8,128)(2,1)} %param.11) | copy-start | bytes 6291460
  87.0 1.0 copy-start.13
  92.6 22.4 %all-to-all-start.4 = ((bf16[8,128,256]{2,1,0:T(8,128)(2,1)}), bf16[8,128,256]{2,1,0:T(8,128)(2,1)S(1)}, u32[]{:S(2)}, u32[]{:S(2)}) async-start(bf16[8,128,256]{2,1,0:T(8,128)(2,1)} %shard_map.78), calls=%async_computation.4 | async-start | bytes 1048576 | tf_op jit(solution)/shard_map/all_to_all | solution.py:298
  106.2 1.6 %copy-start.5 = (bf16[4096,256]{1,0:T(8,128)(2,1)S(1)}, bf16[4096,256]{1,0:T(8,128)(2,1)}, u32[]{:S(2)}) copy-start(bf16[4096,256]{1,0:T(8,128)(2,1)} %all-gather.3.cloned.1.call-done) | copy-start | bytes 6291460
  114.9 17.4 %copy-start.2 = (f32[256]{0:T(256)S(1)}, f32[256]{0:T(256)}, u32[]{:S(2)}) copy-start(f32[256]{0:T(256)} %param.9) | copy-start | bytes 3076
  (5 other events, 4.5 us)
Sparse Core Ops, SparseCore 0:
  9.1 45.5 all-gather.2

commit v2 on v0

v2 whole, which is shorter than its diff:
```python
import jax
import jax.numpy as jnp
from jax import lax
from jax.experimental import pallas as pl
from jax.experimental.pallas import tpu as pltpu
from jax.sharding import Mesh, PartitionSpec as P

NX, NC, NY, NZ = 4, 2, 4, 8
GROUPS = NX * NC
CAP = 128
EXTRA = 16
ROWS = CAP + EXTRA
RANK = 64
PARTS = 2
F32, BF16 = jnp.float32, jnp.bfloat16
NT = (((1,), (1,)), ((), ()))
TN = (((0,), (0,)), ((), ()))
LOCAL = pl.BlockSpec(memory_space=pltpu.VMEM)
REMOTE = pl.BlockSpec(memory_space=pltpu.HBM)
ANY = pl.BlockSpec(memory_space=pl.ANY)


def in_hbm(a):
    return pltpu.with_memory_space_constraint(a, pltpu.HBM)


def params(mib=12):
    return pltpu.CompilerParams(vmem_limit_bytes=mib * 1024 * 1024)


def cost(flops, nbytes):
    return pl.CostEstimate(flops=8 * flops, bytes_accessed=8 * nbytes, transcendentals=0)


def turn_of(chunk, x, c):
    return (x if chunk == 0 else x + 1 - 2 * (x % 2)) + NX * c


CHUNKS = ((2, 1), (3, 0))


def start_body(
    owner_ref, slot_ref, rows_ref, w_ref, first_ref, second_ref, send_ref, target_ref, sem
):
    x, c, y, z = (lax.axis_index(name) for name in ("x", "c", "y", "z"))
    width = rows_ref.shape[1]
    copies = []
    for chunk, out in enumerate((first_ref, second_ref)):
        column = (z + turn_of(chunk, x, c)) % NZ
        for at, by in enumerate(CHUNKS[chunk]):
            offset = pl.multiple_of(((y + by) % NY * NZ + column) * width, 256)
            copies.append(
                pltpu.make_async_copy(
                    w_ref.at[:, pl.ds(offset, width)],
                    out.at[:, pl.ds(at * width, width)],
                    sem.at[2 * chunk + at],
                )
            )
    for copy in copies:
        copy.start()

    tokens = rows_ref.shape[0]
    owner = owner_ref[...]
    member = lax.broadcasted_iota(jnp.int32, (GROUPS, tokens), 0) == owner
    before = lax.broadcasted_iota(jnp.int32, (tokens, tokens), 0) < lax.broadcasted_iota(
        jnp.int32, (tokens, tokens), 1
    )
    earlier = jnp.dot(
        member.astype(F32).astype(BF16), before.astype(F32).astype(BF16), preferred_element_type=F32
    )
    position = jnp.sum(jnp.where(member, earlier, 0.0), axis=0, keepdims=True)
    target = owner.astype(F32) * CAP + position
    target_ref[...] = jnp.broadcast_to(target, target_ref.shape)
    rows = rows_ref[...]
    slots = jnp.broadcast_to(slot_ref[...].astype(F32), (EXTRA, tokens)).astype(BF16)
    for g in range(GROUPS):
        spot = lax.broadcasted_iota(jnp.int32, (CAP, tokens), 0).astype(F32) + float(g * CAP)
        select = jnp.where(spot == target, 1.0, 0.0).astype(BF16)
        send_ref[g, :CAP, :] = jnp.dot(select, rows, preferred_element_type=F32).astype(BF16)
        sent = lax.dot_general(slots, select, NT, preferred_element_type=F32).astype(BF16)
        send_ref[g, CAP:, :CAP] = sent
        send_ref[g, CAP:, CAP:] = sent
    for copy in copies:
        copy.wait()


def start(owner, slot, rows, weights):
    tokens, width = rows.shape
    depth = weights.shape[0]
    return pl.pallas_call(
        start_body,
        out_shape=(
            pltpu.VMEM((depth, 2 * width), BF16),
            pltpu.VMEM((depth, 2 * width), BF16),
            pltpu.HBM((GROUPS, ROWS, width), BF16),
            jax.ShapeDtypeStruct((8, tokens), F32),
        ),
        in_specs=[LOCAL, LOCAL, LOCAL, REMOTE],
        out_specs=(LOCAL, LOCAL, LOCAL, LOCAL),
        scratch_shapes=[pltpu.SemaphoreType.DMA((4,))],
        compiler_params=params(),
        cost_estimate=cost(2 * GROUPS * CAP * tokens * width, 4 * GROUPS * ROWS * width),
    )(in_hbm(owner), in_hbm(slot), in_hbm(rows), in_hbm(weights))


def fetch(source, target, sem, parts):
    size = source.shape[0] // parts
    copies = []
    for i in range(parts):
        here = pl.ds(i * size, size)
        copies.append(pltpu.make_async_copy(source.at[here], target.at[here], sem.at[i]))
    for copy in copies:
        copy.start()
    return copies


def down_body(got_ref, source_ref, *refs):
    low_ref, slot_ref, map_ref, total_ref, sem = refs[-5:]
    copies = fetch(source_ref, map_ref, sem, PARTS)
    slot = jnp.concatenate(
        [got_ref[g, CAP:, :CAP].astype(F32)[:1, :] for g in range(GROUPS)], axis=1
    )
    slot_ref[...] = jnp.broadcast_to(slot, slot_ref.shape)
    per = map_ref.shape[0] // PARTS // 256
    for p in range(PARTS):
        copies[p].wait()
        for b in range(GROUPS // 2):
            rows = jnp.concatenate([got_ref[2 * b, :CAP, :], got_ref[2 * b + 1, :CAP, :]], axis=0)
            columns = slice(2 * b * CAP, 2 * (b + 1) * CAP)
            here = slot[:, columns]
            total = total_ref[:, columns] if p else jnp.zeros((RANK, 2 * CAP), F32)
            for n in range(p * per, (p + 1) * per):
                product = lax.dot_general(
                    map_ref[n * 256 : (n + 1) * 256, :], rows, NT, preferred_element_type=F32
                )
                for j in range(256 // RANK):
                    part = product[RANK * j : RANK * (j + 1), :]
                    total = jnp.where(here == float(n * 256 // RANK + j), part, total)
            if p < PARTS - 1:
                total_ref[:, columns] = total
                continue
            for g in range(2):
                for i in range(RANK // 16):
                    low_ref[(2 * b + g) * (RANK // 16) + i] = total[
                        16 * i : 16 * (i + 1), g * CAP : (g + 1) * CAP
                    ]


def down(got, maps, *deps):
    rows, width = GROUPS * CAP, maps.shape[1]
    return pl.pallas_call(
        down_body,
        out_shape=(
            pltpu.HBM((NY * NZ, 16, CAP), F32),
            jax.ShapeDtypeStruct((8, rows), F32),
        ),
        in_specs=[LOCAL, REMOTE] + [ANY] * len(deps),
        out_specs=(LOCAL, LOCAL),
        scratch_shapes=[
            pltpu.VMEM(maps.shape, BF16),
            pltpu.VMEM((RANK, rows), F32),
            pltpu.SemaphoreType.DMA((PARTS,)),
        ],
        compiler_params=params(),
        cost_estimate=cost(2 * rows * maps.shape[0] * width, 2 * maps.shape[0] * width),
    )(got, in_hbm(maps), *deps)


def total_body(parts_ref, *refs):
    o_ref = refs[-1]
    whole = jnp.sum(parts_ref[...], axis=0).astype(BF16)
    o_ref[...] = jnp.broadcast_to(whole[None], o_ref.shape)


def total(parts, *deps):
    return pl.pallas_call(
        total_body,
        out_shape=pltpu.HBM(parts.shape, BF16),
        in_specs=[LOCAL] + [ANY] * len(deps),
        out_specs=LOCAL,
        compiler_params=params(4),
        cost_estimate=cost(parts.size, 6 * parts.size),
    )(parts, *deps)


def up_body(low_ref, slot_ref, source_ref, *refs):
    o_ref, token_ref, map_ref, sem = refs[-4:]
    token_ref[...] = slot_ref[:, :128]
    copies = fetch(source_ref, map_ref, sem, PARTS)
    per = RANK // 16
    for b in range(GROUPS // 2):
        halves = [
            jnp.concatenate([low_ref[g * per + i].astype(F32) for i in range(per)], axis=0)
            for g in (2 * b, 2 * b + 1)
        ]
        low = jnp.concatenate(halves, axis=1)
        here = slot_ref[:1, 2 * b * CAP : 2 * (b + 1) * CAP]
        spread = jnp.concatenate(
            [
                jnp.where(here == float(a), low, 0.0).astype(BF16)
                for a in range(map_ref.shape[0] // RANK)
            ],
            axis=0,
        )
        if b == 0:
            for copy in copies:
                copy.wait()
        out = lax.dot_general(spread, map_ref[...], TN, preferred_element_type=F32).astype(BF16)
        o_ref[2 * b] = out[:CAP]
        o_ref[2 * b + 1] = out[CAP:]


def up(low, slots, maps, *deps):
    rows, width = GROUPS * CAP, maps.shape[1]
    return pl.pallas_call(
        up_body,
        out_shape=(
            pltpu.HBM((GROUPS, CAP, width), BF16),
            jax.ShapeDtypeStruct((8, 128), F32),
        ),
        in_specs=[LOCAL, LOCAL, REMOTE] + [ANY] * len(deps),
        out_specs=(LOCAL, LOCAL),
        scratch_shapes=[pltpu.VMEM(maps.shape, BF16), pltpu.SemaphoreType.DMA((PARTS,))],
        compiler_params=params(20),
        cost_estimate=cost(2 * rows * maps.shape[0] * width, 2 * maps.shape[0] * width),
    )(low, slots, in_hbm(maps), *deps)


def base_body(chunk, *refs):
    ring, pieces = refs[:NZ], refs[NZ : 2 * NZ]
    o_ref, p_ref, token_ref, a_ref, w_ref, sem = refs[-6:]
    token_ref[...] = jnp.zeros_like(token_ref)
    x, c = lax.axis_index("x"), lax.axis_index("c")
    depth, width = w_ref.shape[1], o_ref.shape[1]
    copies = []
    for at, slot in enumerate((0, 1, 7, 2, 6, 3, 5, 4)):
        copies.append(pltpu.make_async_copy(ring[at], a_ref.at[slot], sem.at[at]))
    turns = [x, x + NX - 1, x + 1, x + 2]
    for at in range(NZ):
        slot = turn_of(chunk, turns[at % NX] % NX, c if at < NX else 1 - c)
        copies.append(pltpu.make_async_copy(pieces[at], w_ref.at[slot], sem.at[NZ + at]))
    for copy in copies:
        copy.start()
    for copy in copies:
        copy.wait()
    whole = jnp.dot(
        jnp.concatenate([a_ref[k] for k in range(NZ)], axis=1),
        w_ref[...].reshape(NZ * depth, w_ref.shape[2]),
        preferred_element_type=F32,
    )
    o_ref[...] = whole[:, :width].astype(BF16)
    p_ref[...] = whole[:, width:].astype(BF16)


def base_product(chunk, ring, pieces, space, *deps):
    tokens, width = ring[0].shape
    depth, wide = pieces[0].shape

    def body(*refs):
        base_body(chunk, *refs)

    return pl.pallas_call(
        body,
        out_shape=[space((tokens, width), BF16)] * 2 + [jax.ShapeDtypeStruct((8, 128), F32)],
        in_specs=[ANY] * (2 * NZ + len(deps)),
        out_specs=[LOCAL] * 3,
        scratch_shapes=[
            pltpu.VMEM((NZ, tokens, width), BF16),
            pltpu.VMEM((NZ, depth, wide), BF16),
            pltpu.SemaphoreType.DMA((2 * NZ,)),
        ],
        compiler_params=params(),
        cost_estimate=cost(2 * tokens * NZ * depth * wide, 4 * 1024 * 1024),
    )(*ring, *pieces, *deps)


def final_body(*refs):
    parts, (scale_ref, target_ref, back_ref, o_ref) = refs[:NY], refs[NY:]
    tokens = o_ref.shape[0]
    back = back_ref[...].reshape(GROUPS * CAP, back_ref.shape[2])
    step = 256
    for b in range(tokens // step):
        here = slice(b * step, (b + 1) * step)
        spot = lax.broadcasted_iota(jnp.int32, (GROUPS * CAP, step), 0).astype(F32)
        select = jnp.where(spot == target_ref[:1, here], 1.0, 0.0).astype(BF16)
        delta = lax.dot_general(select, back, TN, preferred_element_type=F32)
        summed = parts[0][here, :].astype(F32)
        for part in parts[1:]:
            summed += part[here, :].astype(F32)
        o_ref[here, :] = (summed * scale_ref[...] + delta).astype(BF16)


def final(parts, scale, target, back):
    tokens, width = parts[0].shape
    return pl.pallas_call(
        final_body,
        out_shape=jax.ShapeDtypeStruct((tokens, width), BF16),
        in_specs=[LOCAL] * (NY + 3),
        out_specs=LOCAL,
        compiler_params=params(),
        cost_estimate=cost(2 * GROUPS * CAP * tokens * width, 4 * 1024 * 1024),
    )(*parts, scale, target, back)


def shift(a, axis, by, size):
    return lax.ppermute(a, axis, [(i, (i + by) % size) for i in range(size)])


def pass_on(chunk, a):
    pairs = []
    for at in range(NX * NC * NZ):
        i, j, k = at // (NC * NZ), at // NZ % NC, at % NZ
        pairs.append((at, (i * NC + j) * NZ + (k + turn_of(chunk, i, j)) % NZ))
    return lax.ppermute(a, ("x", "c", "z"), pairs)


def on_device(rows, weights, scale, down_maps, up_maps, owner, slot):
    tokens, width = rows.shape
    first, second, send, target = start(
        owner.reshape(1, tokens), slot.reshape(1, tokens), rows, weights
    )
    owns = [pass_on(0, first), pass_on(1, second)]
    got = lax.all_to_all(send, ("x", "c"), 0, 0, tiled=True)
    ring = [rows, shift(rows, "z", 1, NZ), shift(rows, "z", -1, NZ)]

    low_part, slots = down(got, down_maps.reshape(-1, width), *owns, *ring[1:])
    lefts = [shift(own, "x", 1, NX) for own in owns]
    rights = [shift(own, "x", -1, NX) for own in owns]
    ring += [shift(ring[1], "z", 1, NZ), shift(ring[2], "z", -1, NZ)]
    ring += [shift(ring[3], "z", 1, NZ), shift(ring[4], "z", -1, NZ)]

    low_part = lax.all_to_all(low_part, ("y", "z"), 0, 0, tiled=True)
    low_all = total(low_part, *lefts, *rights, *ring[3:])
    low = lax.all_to_all(low_all, ("y", "z"), 0, 0, tiled=True)

    ring.append(shift(ring[5], "z", 1, NZ))
    fars = [shift(lefts[0], "x", 1, NX), shift(rights[1], "x", -1, NX)]
    chunks = []
    for mine in zip(owns, lefts, rights, fars):
        chunks.append([*mine, *(shift(piece, "c", 1, NC) for piece in mine)])

    two, one, token = base_product(0, ring, chunks[0], pltpu.HBM)
    delta, token = up(low, slots, up_maps.reshape(-1, width), token)
    back = lax.all_to_all(delta, ("x", "c"), 0, 0, tiled=True)

    three, zero, _ = base_product(1, ring, chunks[1], pltpu.VMEM, token)
    parts = [zero, shift(one, "y", 1, NY), shift(two, "y", 2, NY), shift(three, "y", 3, NY)]
    return final(parts, scale.reshape(1, width), target, back)


def solution(mesh):
    fine = Mesh(mesh.devices.reshape(NX, NC, NY, NZ), ("x", "c", "y", "z"))
    grp, tp = ("x", "c"), ("y", "z")
    in_specs = (
        P(grp, tp),
        P(tp, None),
        P(tp),
        P(grp, None, tp),
        P(grp, None, tp),
        P(grp, None),
        P(grp),
    )
    return jax.shard_map(
        on_device, mesh=fine, in_specs=in_specs, out_specs=P(grp, tp), check_vma=False
    )
```

time: 276 us -> 112 us (0.41); the launches traced: 272 us -> 111 us
  blocking collectives: 121 us -> 0 us
  waiting for transfers between devices: 58.4 us -> 16.4 us
  starting transfers between devices: 42 us -> 67.7 us
  Pallas kernels: 0 us -> 21.5 us
  matrix products: 20.3 us -> 0 us
  between operations: 13.5 us -> 0.16 us
  local copies, waits for them, and re-layouts: 13.9 us -> 4.98 us
  other arithmetic: 3.12 us -> 0 us
    psum x1 -> x0, blocking collectives: 121 us -> none  [on_device(): rank_product = lax.psum(down_product, 'tp').astype(jnp.bfloat16)]
    ppermute x0 -> x26, starting transfers between devices: none -> 43.8 us  [the longest x24 32.3 us: shift(): return lax.ppermute(a, axis, [(i, (i + by) % size) for i in range(size)])]
    reduce_scatter x1 -> x0, waiting for transfers between devices: 39.6 us -> none  [on_device(): lax.psum_scatter(lax.dot_general(quantized_weight_codes, attention_output...]
    pallas_call x0 -> x7, Pallas kernels: none -> 21.5 us  [the longest x2 6.59 us: base_product(): pl.pallas_call(body, out_shape=[space((tokens, width), BF16)] * 2 + [jax....]
    dot_general x5 -> x0, matrix products: 20.3 us -> none  [the longest x1 10.3 us: on_device(): lax.dot_general(quantized_weight_codes, attention_output, (((0,), (1,)),...]
    all_to_all x3 -> x4, starting transfers between devices: 42 us -> 23.9 us  [the longest x1 6.71 us: on_device(): back = lax.all_to_all(delta, ('x', 'c'), 0, 0, tiled=True)]
    all_to_all x3 -> x4, waiting for transfers between devices: 18.8 us -> 2.64 us  [the longest x1 2.63 us: on_device(): low_part = lax.all_to_all(low_part, ('y', 'z'), 0, 0, tiled=True)]
    ppermute x0 -> x26, waiting for transfers between devices: none -> 13.8 us  [the longest x24 12.8 us: shift(): return lax.ppermute(a, axis, [(i, (i + by) % size) for i in range(size)])]
  transfers between devices with their start and end apart: 4 -> 30, of which waited for: 4 -> 7; matrix products, arithmetic and copies ran while one was open for 9% -> 0% of each run, Pallas kernels for 0% -> 15%
where the time goes in v2:
time: 112 us; the launch traced here: 111 us
  starting transfers between devices  67.7 us (60%)
  Pallas kernels  21.5 us (19%)
  waiting for transfers between devices  16.4 us (15%)
  local copies, waits for them, and re-layouts  4.98 us (4%)
    ppermute x24, starting transfers between devices, shift(): return lax.ppermute(a, axis, [(i, (i + by) % size) for i in range(size)])  32.3 us
    ppermute x24, waiting for transfers between devices, shift(): return lax.ppermute(a, axis, [(i, (i + by) % size) for i in range(size)])  12.8 us
    ppermute x2, starting transfers between devices, pass_on(): return lax.ppermute(a, ('x', 'c', 'z'), pairs)  11.6 us
    all_to_all x1, starting transfers between devices, on_device(): back = lax.all_to_all(delta, ('x', 'c'), 0, 0, tiled=True)  6.71 us
    pallas_call x2, Pallas kernels, base_product(): pl.pallas_call(body, out_shape=[space((tokens, width), BF16)] * 2 + [jax....  6.59 us
    all_to_all x1, starting transfers between devices, on_device(): low_part = lax.all_to_all(low_part, ('y', 'z'), 0, 0, tiled=True)  5.89 us
    all_to_all x1, starting transfers between devices, on_device(): low = lax.all_to_all(low_all, ('y', 'z'), 0, 0, tiled=True)  5.66 us
    all_to_all x1, starting transfers between devices, on_device(): got = lax.all_to_all(send, ('x', 'c'), 0, 0, tiled=True)  5.62 us
  transfers between devices with their start and end apart: 30, of which 7 were waited for; matrix products, arithmetic and copies ran while one was open for 0% of the time, Pallas kernels for 15%

profile of v2, /device:TPU:1, one launch (start us, length us, event | category | flops | bytes accessed | tf_op | source)
XLA Modules:
  0.0 110.8 jit_solution(5183609434432404017)
XLA Ops:
  0.0 3.7 %shard_map.73 = (bf16[256,512]{1,0:T(8,128)(2,1)S(1)}, bf16[256,512]{1,0:T(8,128)(2,1)S(1)}, bf16[8,144,256]{2,1,0:T(8,128)(2,1)}, f32[8,512]{1,0:T(8,128)S(1)}) custom-call(s32[1,512]{1,0:T(1,128)} %bitcast.8, s32[1,512]{1,0:T(1,128)} %bitcast.9, bf16[512,256]{1,0:T(8,128)(2,1)} %refs_0_.3, bf16[256,8192]{1,0:T(8,128)(2,1)} %w_ref.1), custom_call_target="tpu_custom_call" | custom-call | flops 2147483648 | bytes 9437184 | tf_op jit(solution)/shard_map/pallas_call | solution.py:90
  3.7 9.6 %collective-permute-start.15 = (bf16[256,512]{1,0:T(8,128)(2,1)S(1)}, bf16[256,512]{1,0:T(8,128)(2,1)S(1)}, u32[]{:S(2)}, u32[]{:S(2)}) collective-permute-start(bf16[256,512]{1,0:T(8,128)(2,1)S(1)} %get-tuple-element.20), channel_id=1, source_target_pairs={{0,0},{1,1},{2,2},{3,3},{4,4},{5,5},{6,6},{7,7},{32,36},{33,37},{3... | collective-permute-start | bytes 786440 | tf_op jit(solution)/shard_map/ppermute | solution.py:314
  14.2 1.9 %collective-permute-start.1 = (bf16[512,256]{1,0:T(8,128)(2,1)S(1)}, bf16[512,256]{1,0:T(8,128)(2,1)S(1)}, u32[]{:S(2)}, u32[]{:S(2)}) collective-permute-start(bf16[512,256]{1,0:T(8,128)(2,1)S(1)} %copy-done), channel_id=1, source_target_pairs={{0,7},{1,0},{2,1},{3,2},{4,3},{5,4},{6,5},{7,6},{8,15},{9,8},{10,9... | collective-permute-start | bytes 786440 | tf_op jit(solution)/shard_map/ppermute | solution.py:306
  16.1 1.9 %collective-permute-start.7 = (bf16[256,512]{1,0:T(8,128)(2,1)S(1)}, bf16[256,512]{1,0:T(8,128)(2,1)}, u32[]{:S(2)}, u32[]{:S(2)}) collective-permute-start(bf16[256,512]{1,0:T(8,128)(2,1)S(1)} %get-tuple-element.18), channel_id=1, source_target_pairs={{0,1},{1,2},{2,3},{3,4},{4,5},{5,6},{6,7},{7,0},{32,37},{33,38},{3... | collective-permute-start | bytes 786440 | tf_op jit(solution)/shard_map/ppermute | solution.py:314
  18.0 5.6 %all-to-all-start = ((bf16[8,144,256]{2,1,0:T(8,128)(2,1)}), bf16[8,144,256]{2,1,0:T(8,128)(2,1)S(1)}, u32[]{:S(2)}, u32[]{:S(2)}) async-start(bf16[8,144,256]{2,1,0:T(8,128)(2,1)} %get-tuple-element.19), calls=%async_computation | async-start | bytes 1179648 | tf_op jit(solution)/shard_map/all_to_all | solution.py:323
  23.7 1.7 %collective-permute-start.16 = (bf16[256,512]{1,0:T(8,128)(2,1)S(1)}, bf16[256,512]{1,0:T(8,128)(2,1)S(1)}, u32[]{:S(2)}, u32[]{:S(2)}) collective-permute-start(bf16[256,512]{1,0:T(8,128)(2,1)S(1)} %collective-permute-done.15.refs_0_.refs_8_), channel_id=1, source_target_pairs={{0,64},{64,128},{128,192},{192,0},{1,65},{65,129},{129,193},{193,1... | collective-permute-start | bytes 786440 | tf_op jit(solution)/shard_map/ppermute | solution.py:306
  29.5 3.4 %collective-permute-start.3 = (bf16[512,256]{1,0:T(8,128)(2,1)S(1)}, bf16[512,256]{1,0:T(8,128)(2,1)S(1)}, u32[]{:S(2)}, u32[]{:S(2)}) collective-permute-start(bf16[512,256]{1,0:T(8,128)(2,1)S(1)} %collective-permute-done.1.refs_3_.refs_2_), channel_id=1, source_target_pairs={{0,7},{1,0},{2,1},{3,2},{4,3},{5,4},{6,5},{7,6},{8,15},{9,8},{10,9... | collective-permute-start | bytes 786440 | tf_op jit(solution)/shard_map/ppermute | solution.py:306
  35.3 4.0 %collective-permute-done.16.refs_0_.refs_9_ = bf16[256,512]{1,0:T(8,128)(2,1)S(1)} collective-permute-done((bf16[256,512]{1,0:T(8,128)(2,1)S(1)}, bf16[256,512]{1,0:T(8,128)(2,1)S(1)}, u32[]{:S(2)}, u32[]{:S(2)}) %collective-permute-start.16) | collective-permute-done | bytes 262176 | tf_op jit(solution)/shard_map/ppermute | solution.py:306
  43.5 1.9 %collective-permute-start.5 = (bf16[512,256]{1,0:T(8,128)(2,1)S(1)}, bf16[512,256]{1,0:T(8,128)(2,1)S(1)}, u32[]{:S(2)}, u32[]{:S(2)}) collective-permute-start(bf16[512,256]{1,0:T(8,128)(2,1)S(1)} %collective-permute-done.3.refs_5_.refs_4_), channel_id=1, source_target_pairs={{0,7},{1,0},{2,1},{3,2},{4,3},{5,4},{6,5},{7,6},{8,15},{9,8},{10,9... | collective-permute-start | bytes 786440 | tf_op jit(solution)/shard_map/ppermute | solution.py:306
  46.4 4.6 %shard_map.74 = (f32[32,16,128]{2,1,0:T(8,128)}, f32[8,1024]{1,0:T(8,128)S(1)}) custom-call(bf16[8,144,256]{2,1,0:T(8,128)(2,1)S(1)} %all-to-all-done.got_ref, bf16[4096,256]{1,0:T(8,128)(2,1)} %bitcast.6, bf16[256,512]{1,0:T(8,128)(2,1)S(1)} %copy-done.2, bf16[256,512]{1,0:T(8,128)(2,1)} %collective-permute-done.7.refs_1_.refs_8_, ...), custom_call_target="tpu_custom_call" | custom-call | flops 17179869184 | bytes 16777216 | tf_op jit(solution)/shard_map/pallas_call | solution.py:151
  51.0 5.9 %all-to-all-start.1 = ((f32[32,16,128]{2,1,0:T(8,128)}), f32[32,16,128]{2,1,0:T(8,128)S(1)}, u32[]{:S(2)}, u32[]{:S(2)}) async-start(f32[32,16,128]{2,1,0:T(8,128)} %get-tuple-element.21), calls=%async_computation.1 | async-start | bytes 524288 | tf_op jit(solution)/shard_map/all_to_all | solution.py:332
  56.9 3.5 %collective-permute-start.20 = (bf16[256,512]{1,0:T(8,128)(2,1)S(1)}, bf16[256,512]{1,0:T(8,128)(2,1)}, u32[]{:S(2)}, u32[]{:S(2)}) collective-permute-start(bf16[256,512]{1,0:T(8,128)(2,1)S(1)} %collective-permute-done.16.refs_0_.refs_9_), channel_id=1, source_target_pairs={{0,32},{32,0},{1,33},{33,1},{2,34},{34,2},{3,35},{35,3},{4,36},{36... | collective-permute-start | bytes 786440 | tf_op jit(solution)/shard_map/ppermute | solution.py:306
  62.4 1.5 %collective-permute-start.6 = (bf16[512,256]{1,0:T(8,128)(2,1)S(1)}, bf16[512,256]{1,0:T(8,128)(2,1)}, u32[]{:S(2)}, u32[]{:S(2)}) collective-permute-start(bf16[512,256]{1,0:T(8,128)(2,1)S(1)} %collective-permute-done.4.refs_6_.refs_5_), channel_id=1, source_target_pairs={{0,1},{1,2},{2,3},{3,4},{4,5},{5,6},{6,7},{7,0},{8,9},{9,10},{10,1... | collective-permute-start | bytes 786440 | tf_op jit(solution)/shard_map/ppermute | solution.py:306
  63.9 2.6 %all-to-all-done.1.parts_ref = f32[32,16,128]{2,1,0:T(8,128)S(1)} async-done(((f32[32,16,128]{2,1,0:T(8,128)}), f32[32,16,128]{2,1,0:T(8,128)S(1)}, u32[]{:S(2)}, u32[]{:S(2)}) %all-to-all-start.1) | async-done | bytes 262176 | tf_op jit(solution)/shard_map/all_to_all | solution.py:332
  67.2 5.7 %all-to-all-start.2 = ((bf16[32,16,128]{2,1,0:T(8,128)(2,1)}), bf16[32,16,128]{2,1,0:T(8,128)(2,1)S(1)}, u32[]{:S(2)}, u32[]{:S(2)}) async-start(bf16[32,16,128]{2,1,0:T(8,128)(2,1)} %shard_map.75), calls=%async_computation.2 | async-start | bytes 262144 | tf_op jit(solution)/shard_map/all_to_all | solution.py:334
  72.9 3.8 %collective-permute-start.11 = (bf16[256,512]{1,0:T(8,128)(2,1)}, bf16[256,512]{1,0:T(8,128)(2,1)}, u32[]{:S(2)}, u32[]{:S(2)}) collective-permute-start(bf16[256,512]{1,0:T(8,128)(2,1)} %collective-permute-done.7.refs_1_.refs_8_), channel_id=1, source_target_pairs={{0,32},{32,0},{1,33},{33,1},{2,34},{34,2},{3,35},{35,3},{4,36},{36... | collective-permute-start | bytes 786440 | tf_op jit(solution)/shard_map/ppermute | solution.py:306
  78.3 3.6 %shard_map.76 = (bf16[512,256]{1,0:T(8,128)(2,1)}, bf16[512,256]{1,0:T(8,128)(2,1)}, f32[8,128]{1,0:T(8,128)S(1)}) custom-call(bf16[512,256]{1,0:T(8,128)(2,1)S(1)} %copy-done, bf16[512,256]{1,0:T(8,128)(2,1)S(1)} %collective-permute-done.refs_2_.refs_1_, bf16[512,256]{1,0:T(8,128)(2,1)S(1)} %collective-permute-done.1.refs_3_.refs_2_, ...), custom_call_target="tpu_custom_call" | custom-call | flops 8589934592 | bytes 33554432 | tf_op jit(solution)/shard_map/pallas_call | solution.py:262
  81.9 1.8 %collective-permute-start.23 = (bf16[512,256]{1,0:T(8,128)(2,1)}, bf16[512,256]{1,0:T(8,128)(2,1)S(1)}, u32[]{:S(2)}, u32[]{:S(2)}) collective-permute-start(bf16[512,256]{1,0:T(8,128)(2,1)} %get-tuple-element.26), channel_id=1, source_target_pairs={{0,8},{8,16},{16,24},{24,0},{1,9},{9,17},{17,25},{25,1},{2,10},{10... | collective-permute-start | bytes 786440 | tf_op jit(solution)/shard_map/ppermute | solution.py:306
  83.7 4.7 %shard_map.77 = (bf16[8,128,256]{2,1,0:T(8,128)(2,1)}, f32[8,128]{1,0:T(8,128)S(1)}) custom-call(bf16[32,16,128]{2,1,0:T(8,128)(2,1)S(1)} %all-to-all-done.2.low_ref, f32[8,1024]{1,0:T(8,128)S(1)} %get-tuple-element.22.slot_ref, bf16[4096,256]{1,0:T(8,128)(2,1)} %bitcast.7, f32[8,128]{1,0:T(8,128)S(1)} %get-tuple-element.23.refs_0_), custom_call_target="tpu_custom_call" | custom-call | flops 17179869184 | bytes 16777216 | tf_op jit(solution)/shard_map/pallas_call | solution.py:215
  88.5 6.7 %all-to-all-start.3 = ((bf16[8,128,256]{2,1,0:T(8,128)(2,1)}), bf16[8,128,256]{2,1,0:T(8,128)(2,1)S(1)}, u32[]{:S(2)}, u32[]{:S(2)}) async-start(bf16[8,128,256]{2,1,0:T(8,128)(2,1)} %get-tuple-element.30), calls=%async_computation.3 | async-start | bytes 1048576 | tf_op jit(solution)/shard_map/all_to_all | solution.py:344
  96.2 3.0 %shard_map.78 = (bf16[512,256]{1,0:T(8,128)(2,1)S(1)}, bf16[512,256]{1,0:T(8,128)(2,1)S(1)}, f32[8,128]{1,0:T(8,128)}) custom-call(bf16[512,256]{1,0:T(8,128)(2,1)S(1)} %copy-done, bf16[512,256]{1,0:T(8,128)(2,1)S(1)} %collective-permute-done.refs_2_.refs_1_, bf16[512,256]{1,0:T(8,128)(2,1)S(1)} %collective-permute-done.1.refs_3_.refs_2_, ...), custom_call_target="tpu_custom_call" | custom-call | flops 8589934592 | bytes 33554432 | tf_op jit(solution)/shard_map/pallas_call | solution.py:262
  99.9 1.6 %collective-permute-start.25 = (bf16[512,256]{1,0:T(8,128)(2,1)S(1)}, bf16[512,256]{1,0:T(8,128)(2,1)S(1)}, u32[]{:S(2)}, u32[]{:S(2)}) collective-permute-start(bf16[512,256]{1,0:T(8,128)(2,1)S(1)} %get-tuple-element.28), channel_id=1, source_target_pairs={{0,24},{8,0},{16,8},{24,16},{1,25},{9,1},{17,9},{25,17},{2,26},{10... | collective-permute-start | bytes 786440 | tf_op jit(solution)/shard_map/ppermute | solution.py:306
  101.5 3.1 %collective-permute-done.24.refs_2_ = bf16[512,256]{1,0:T(8,128)(2,1)S(1)} collective-permute-done((bf16[512,256]{1,0:T(8,128)(2,1)}, bf16[512,256]{1,0:T(8,128)(2,1)S(1)}, u32[]{:S(2)}, u32[]{:S(2)}) %collective-permute-start.24) | collective-permute-done | bytes 262176 | tf_op jit(solution)/shard_map/ppermute | solution.py:306
  104.6 4.0 %collective-permute-done.25.refs_3_ = bf16[512,256]{1,0:T(8,128)(2,1)S(1)} collective-permute-done((bf16[512,256]{1,0:T(8,128)(2,1)S(1)}, bf16[512,256]{1,0:T(8,128)(2,1)S(1)}, u32[]{:S(2)}, u32[]{:S(2)}) %collective-permute-start.25) | collective-permute-done | bytes 262176 | tf_op jit(solution)/shard_map/ppermute | solution.py:306
  (61 shorter events, 20.8 us)
Async XLA Ops:
  3.7 20.0 %collective-permute-start.15 = (bf16[256,512]{1,0:T(8,128)(2,1)S(1)}, bf16[256,512]{1,0:T(8,128)(2,1)S(1)}, u32[]{:S(2)}, u32[]{:S(2)}) collective-permute-start(bf16[256,512]{1,0:T(8,128)(2,1)S(1)} %get-tuple-element.20), channel_id=1, source_target_pairs={{0,0},{1,1},{2,2},{3,3},{4,4},{5,5},{6,6},{7,7},{32,36},{33,37},{3... | collective-permute-start | bytes 786440 | tf_op jit(solution)/shard_map/ppermute | solution.py:314
  14.2 15.3 %collective-permute-start.1 = (bf16[512,256]{1,0:T(8,128)(2,1)S(1)}, bf16[512,256]{1,0:T(8,128)(2,1)S(1)}, u32[]{:S(2)}, u32[]{:S(2)}) collective-permute-start(bf16[512,256]{1,0:T(8,128)(2,1)S(1)} %copy-done), channel_id=1, source_target_pairs={{0,7},{1,0},{2,1},{3,2},{4,3},{5,4},{6,5},{7,6},{8,15},{9,8},{10,9... | collective-permute-start | bytes 786440 | tf_op jit(solution)/shard_map/ppermute | solution.py:306
  16.1 17.8 %collective-permute-start.7 = (bf16[256,512]{1,0:T(8,128)(2,1)S(1)}, bf16[256,512]{1,0:T(8,128)(2,1)}, u32[]{:S(2)}, u32[]{:S(2)}) collective-permute-start(bf16[256,512]{1,0:T(8,128)(2,1)S(1)} %get-tuple-element.18), channel_id=1, source_target_pairs={{0,1},{1,2},{2,3},{3,4},{4,5},{5,6},{6,7},{7,0},{32,37},{33,38},{3... | collective-permute-start | bytes 786440 | tf_op jit(solution)/shard_map/ppermute | solution.py:314
  18.0 27.4 %all-to-all-start = ((bf16[8,144,256]{2,1,0:T(8,128)(2,1)}), bf16[8,144,256]{2,1,0:T(8,128)(2,1)S(1)}, u32[]{:S(2)}, u32[]{:S(2)}) async-start(bf16[8,144,256]{2,1,0:T(8,128)(2,1)} %get-tuple-element.19), calls=%async_computation | async-start | bytes 1179648 | tf_op jit(solution)/shard_map/all_to_all | solution.py:323
  23.7 15.7 %collective-permute-start.16 = (bf16[256,512]{1,0:T(8,128)(2,1)S(1)}, bf16[256,512]{1,0:T(8,128)(2,1)S(1)}, u32[]{:S(2)}, u32[]{:S(2)}) collective-permute-start(bf16[256,512]{1,0:T(8,128)(2,1)S(1)} %collective-permute-done.15.refs_0_.refs_8_), channel_id=1, source_target_pairs={{0,64},{64,128},{128,192},{192,0},{1,65},{65,129},{129,193},{193,1... | collective-permute-start | bytes 786440 | tf_op jit(solution)/shard_map/ppermute | solution.py:306
  26.0 14.1 %collective-permute-start.2 = (bf16[512,256]{1,0:T(8,128)(2,1)S(1)}, bf16[512,256]{1,0:T(8,128)(2,1)S(1)}, u32[]{:S(2)}, u32[]{:S(2)}) collective-permute-start(bf16[512,256]{1,0:T(8,128)(2,1)S(1)} %collective-permute-done.refs_2_.refs_1_), channel_id=1, source_target_pairs={{0,1},{1,2},{2,3},{3,4},{4,5},{5,6},{6,7},{7,0},{8,9},{9,10},{10,1... | collective-permute-start | bytes 786440 | tf_op jit(solution)/shard_map/ppermute | solution.py:306
  39.3 17.6 %collective-permute-start.9 = (bf16[256,512]{1,0:T(8,128)(2,1)}, bf16[256,512]{1,0:T(8,128)(2,1)S(1)}, u32[]{:S(2)}, u32[]{:S(2)}) collective-permute-start(bf16[256,512]{1,0:T(8,128)(2,1)} %collective-permute-done.7.refs_1_.refs_8_), channel_id=1, source_target_pairs={{0,192},{64,0},{128,64},{192,128},{1,193},{65,1},{129,65},{193,129... | collective-permute-start | bytes 786440 | tf_op jit(solution)/shard_map/ppermute | solution.py:306
  40.1 20.3 %collective-permute-start.8 = (bf16[256,512]{1,0:T(8,128)(2,1)}, bf16[256,512]{1,0:T(8,128)(2,1)S(1)}, u32[]{:S(2)}, u32[]{:S(2)}) collective-permute-start(bf16[256,512]{1,0:T(8,128)(2,1)} %collective-permute-done.7.refs_1_.refs_8_), channel_id=1, source_target_pairs={{0,64},{64,128},{128,192},{192,0},{1,65},{65,129},{129,193},{193,1... | collective-permute-start | bytes 786440 | tf_op jit(solution)/shard_map/ppermute | solution.py:306
  40.8 19.7 %collective-permute-start.18 = (bf16[256,512]{1,0:T(8,128)(2,1)S(1)}, bf16[256,512]{1,0:T(8,128)(2,1)}, u32[]{:S(2)}, u32[]{:S(2)}) collective-permute-start(bf16[256,512]{1,0:T(8,128)(2,1)S(1)} %collective-permute-done.16.refs_0_.refs_9_), channel_id=1, source_target_pairs={{0,64},{64,128},{128,192},{192,0},{1,65},{65,129},{129,193},{193,1... | collective-permute-start | bytes 786440 | tf_op jit(solution)/shard_map/ppermute | solution.py:306
  42.0 19.7 %collective-permute-start.4 = (bf16[512,256]{1,0:T(8,128)(2,1)S(1)}, bf16[512,256]{1,0:T(8,128)(2,1)S(1)}, u32[]{:S(2)}, u32[]{:S(2)}) collective-permute-start(bf16[512,256]{1,0:T(8,128)(2,1)S(1)} %collective-permute-done.2.refs_4_.refs_3_), channel_id=1, source_target_pairs={{0,1},{1,2},{2,3},{3,4},{4,5},{5,6},{6,7},{7,0},{8,9},{9,10},{10,1... | collective-permute-start | bytes 786440 | tf_op jit(solution)/shard_map/ppermute | solution.py:306
  43.5 18.8 %collective-permute-start.5 = (bf16[512,256]{1,0:T(8,128)(2,1)S(1)}, bf16[512,256]{1,0:T(8,128)(2,1)S(1)}, u32[]{:S(2)}, u32[]{:S(2)}) collective-permute-start(bf16[512,256]{1,0:T(8,128)(2,1)S(1)} %collective-permute-done.3.refs_5_.refs_4_), channel_id=1, source_target_pairs={{0,7},{1,0},{2,1},{3,2},{4,3},{5,4},{6,5},{7,6},{8,15},{9,8},{10,9... | collective-permute-start | bytes 786440 | tf_op jit(solution)/shard_map/ppermute | solution.py:306
  51.0 15.6 %all-to-all-start.1 = ((f32[32,16,128]{2,1,0:T(8,128)}), f32[32,16,128]{2,1,0:T(8,128)S(1)}, u32[]{:S(2)}, u32[]{:S(2)}) async-start(f32[32,16,128]{2,1,0:T(8,128)} %get-tuple-element.21), calls=%async_computation.1 | async-start | bytes 524288 | tf_op jit(solution)/shard_map/all_to_all | solution.py:332
  56.9 16.0 %collective-permute-start.20 = (bf16[256,512]{1,0:T(8,128)(2,1)S(1)}, bf16[256,512]{1,0:T(8,128)(2,1)}, u32[]{:S(2)}, u32[]{:S(2)}) collective-permute-start(bf16[256,512]{1,0:T(8,128)(2,1)S(1)} %collective-permute-done.16.refs_0_.refs_9_), channel_id=1, source_target_pairs={{0,32},{32,0},{1,33},{33,1},{2,34},{34,2},{3,35},{35,3},{4,36},{36... | collective-permute-start | bytes 786440 | tf_op jit(solution)/shard_map/ppermute | solution.py:306
  60.4 16.3 %collective-permute-start.21 = (bf16[256,512]{1,0:T(8,128)(2,1)S(1)}, bf16[256,512]{1,0:T(8,128)(2,1)}, u32[]{:S(2)}, u32[]{:S(2)}) collective-permute-start(bf16[256,512]{1,0:T(8,128)(2,1)S(1)} %collective-permute-done.17.refs_2_.refs_10_), channel_id=1, source_target_pairs={{0,32},{32,0},{1,33},{33,1},{2,34},{34,2},{3,35},{35,3},{4,36},{36... | collective-permute-start | bytes 786440 | tf_op jit(solution)/shard_map/ppermute | solution.py:306
  60.5 16.3 %collective-permute-start.10 = (bf16[256,512]{1,0:T(8,128)(2,1)S(1)}, bf16[256,512]{1,0:T(8,128)(2,1)}, u32[]{:S(2)}, u32[]{:S(2)}) collective-permute-start(bf16[256,512]{1,0:T(8,128)(2,1)S(1)} %collective-permute-done.9.refs_3_.refs_10_), channel_id=1, source_target_pairs={{0,192},{64,0},{128,64},{192,128},{1,193},{65,1},{129,65},{193,129... | collective-permute-start | bytes 786440 | tf_op jit(solution)/shard_map/ppermute | solution.py:306
  61.7 15.5 %collective-permute-start.22 = (bf16[256,512]{1,0:T(8,128)(2,1)}, bf16[256,512]{1,0:T(8,128)(2,1)}, u32[]{:S(2)}, u32[]{:S(2)}) collective-permute-start(bf16[256,512]{1,0:T(8,128)(2,1)} %collective-permute-done.18.refs_11_), channel_id=1, source_target_pairs={{0,32},{32,0},{1,33},{33,1},{2,34},{34,2},{3,35},{35,3},{4,36},{36... | collective-permute-start | bytes 786440 | tf_op jit(solution)/shard_map/ppermute | solution.py:306
  62.4 15.0 %collective-permute-start.6 = (bf16[512,256]{1,0:T(8,128)(2,1)S(1)}, bf16[512,256]{1,0:T(8,128)(2,1)}, u32[]{:S(2)}, u32[]{:S(2)}) collective-permute-start(bf16[512,256]{1,0:T(8,128)(2,1)S(1)} %collective-permute-done.4.refs_6_.refs_5_), channel_id=1, source_target_pairs={{0,1},{1,2},{2,3},{3,4},{4,5},{5,6},{6,7},{7,0},{8,9},{9,10},{10,1... | collective-permute-start | bytes 786440 | tf_op jit(solution)/shard_map/ppermute | solution.py:306
  67.2 16.5 %all-to-all-start.2 = ((bf16[32,16,128]{2,1,0:T(8,128)(2,1)}), bf16[32,16,128]{2,1,0:T(8,128)(2,1)S(1)}, u32[]{:S(2)}, u32[]{:S(2)}) async-start(bf16[32,16,128]{2,1,0:T(8,128)(2,1)} %shard_map.75), calls=%async_computation.2 | async-start | bytes 262144 | tf_op jit(solution)/shard_map/all_to_all | solution.py:334
  72.9 22.3 %collective-permute-start.11 = (bf16[256,512]{1,0:T(8,128)(2,1)}, bf16[256,512]{1,0:T(8,128)(2,1)}, u32[]{:S(2)}, u32[]{:S(2)}) collective-permute-start(bf16[256,512]{1,0:T(8,128)(2,1)} %collective-permute-done.7.refs_1_.refs_8_), channel_id=1, source_target_pairs={{0,32},{32,0},{1,33},{33,1},{2,34},{34,2},{3,35},{35,3},{4,36},{36... | collective-permute-start | bytes 786440 | tf_op jit(solution)/shard_map/ppermute | solution.py:306
  76.7 19.5 %collective-permute-start.13 = (bf16[256,512]{1,0:T(8,128)(2,1)S(1)}, bf16[256,512]{1,0:T(8,128)(2,1)}, u32[]{:S(2)}, u32[]{:S(2)}) collective-permute-start(bf16[256,512]{1,0:T(8,128)(2,1)S(1)} %collective-permute-done.9.refs_3_.refs_10_), channel_id=1, source_target_pairs={{0,32},{32,0},{1,33},{33,1},{2,34},{34,2},{3,35},{35,3},{4,36},{36... | collective-permute-start | bytes 786440 | tf_op jit(solution)/shard_map/ppermute | solution.py:306
  76.8 19.4 %collective-permute-start.12 = (bf16[256,512]{1,0:T(8,128)(2,1)S(1)}, bf16[256,512]{1,0:T(8,128)(2,1)}, u32[]{:S(2)}, u32[]{:S(2)}) collective-permute-start(bf16[256,512]{1,0:T(8,128)(2,1)S(1)} %collective-permute-done.8.refs_1_.refs_9_), channel_id=1, source_target_pairs={{0,32},{32,0},{1,33},{33,1},{2,34},{34,2},{3,35},{35,3},{4,36},{36... | collective-permute-start | bytes 786440 | tf_op jit(solution)/shard_map/ppermute | solution.py:306
  77.2 19.0 %collective-permute-start.14 = (bf16[256,512]{1,0:T(8,128)(2,1)}, bf16[256,512]{1,0:T(8,128)(2,1)}, u32[]{:S(2)}, u32[]{:S(2)}) collective-permute-start(bf16[256,512]{1,0:T(8,128)(2,1)} %collective-permute-done.10.refs_11_), channel_id=1, source_target_pairs={{0,32},{32,0},{1,33},{33,1},{2,34},{34,2},{3,35},{35,3},{4,36},{36... | collective-permute-start | bytes 786440 | tf_op jit(solution)/shard_map/ppermute | solution.py:306
  81.9 19.6 %collective-permute-start.23 = (bf16[512,256]{1,0:T(8,128)(2,1)}, bf16[512,256]{1,0:T(8,128)(2,1)S(1)}, u32[]{:S(2)}, u32[]{:S(2)}) collective-permute-start(bf16[512,256]{1,0:T(8,128)(2,1)} %get-tuple-element.26), channel_id=1, source_target_pairs={{0,8},{8,16},{16,24},{24,0},{1,9},{9,17},{17,25},{25,1},{2,10},{10... | collective-permute-start | bytes 786440 | tf_op jit(solution)/shard_map/ppermute | solution.py:306
  88.5 20.1 %all-to-all-start.3 = ((bf16[8,128,256]{2,1,0:T(8,128)(2,1)}), bf16[8,128,256]{2,1,0:T(8,128)(2,1)S(1)}, u32[]{:S(2)}, u32[]{:S(2)}) async-start(bf16[8,128,256]{2,1,0:T(8,128)(2,1)} %get-tuple-element.30), calls=%async_computation.3 | async-start | bytes 1048576 | tf_op jit(solution)/shard_map/all_to_all | solution.py:344
  (15 other events, 123.1 us)

commit v3 on v2

--- a/solution.py
+++ b/solution.py
@@ -29,13 +29,14 @@
 
 
 def cost(flops, nbytes):
-    return pl.CostEstimate(flops=8 * flops, bytes_accessed=8 * nbytes, transcendentals=0)
+    return pl.CostEstimate(flops=flops, bytes_accessed=nbytes, transcendentals=0)
 
 
 def turn_of(chunk, x, c):
     return (x if chunk == 0 else x + 1 - 2 * (x % 2)) + NX * c
 
 
+WEIGHT = (4, 4)
 CHUNKS = ((2, 1), (3, 0))
 
 
@@ -99,7 +100,7 @@
         out_specs=(LOCAL, LOCAL, LOCAL, LOCAL),
         scratch_shapes=[pltpu.SemaphoreType.DMA((4,))],
         compiler_params=params(),
-        cost_estimate=cost(2 * GROUPS * CAP * tokens * width, 4 * GROUPS * ROWS * width),
+        cost_estimate=cost(8 * (2 * GROUPS * CAP * tokens * width), 8 * (4 * GROUPS * ROWS * width)),
     )(in_hbm(owner), in_hbm(slot), in_hbm(rows), in_hbm(weights))
 
 
@@ -162,12 +163,13 @@
             pltpu.SemaphoreType.DMA((PARTS,)),
         ],
         compiler_params=params(),
-        cost_estimate=cost(2 * rows * maps.shape[0] * width, 2 * maps.shape[0] * width),
+        cost_estimate=cost(30 * (2 * rows * maps.shape[0] * width), 30 * (2 * maps.shape[0] * width)),
     )(got, in_hbm(maps), *deps)
 
 
 def total_body(parts_ref, *refs):
-    o_ref = refs[-1]
+    o_ref, token_ref = refs[-2:]
+    token_ref[...] = parts_ref[0, :8, :]
     whole = jnp.sum(parts_ref[...], axis=0).astype(BF16)
     o_ref[...] = jnp.broadcast_to(whole[None], o_ref.shape)
 
@@ -175,11 +177,11 @@
 def total(parts, *deps):
     return pl.pallas_call(
         total_body,
-        out_shape=pltpu.HBM(parts.shape, BF16),
+        out_shape=(pltpu.HBM(parts.shape, BF16), jax.ShapeDtypeStruct((8, 128), F32)),
         in_specs=[LOCAL] + [ANY] * len(deps),
-        out_specs=LOCAL,
+        out_specs=(LOCAL, LOCAL),
         compiler_params=params(4),
-        cost_estimate=cost(parts.size, 6 * parts.size),
+        cost_estimate=cost(30 * (parts.size), 30 * (6 * parts.size)),
     )(parts, *deps)
 
 
@@ -222,7 +224,7 @@
         out_specs=(LOCAL, LOCAL),
         scratch_shapes=[pltpu.VMEM(maps.shape, BF16), pltpu.SemaphoreType.DMA((PARTS,))],
         compiler_params=params(20),
-        cost_estimate=cost(2 * rows * maps.shape[0] * width, 2 * maps.shape[0] * width),
+        cost_estimate=cost(30 * (2 * rows * maps.shape[0] * width), 30 * (2 * maps.shape[0] * width)),
     )(low, slots, in_hbm(maps), *deps)
 
 
@@ -270,7 +272,7 @@
             pltpu.SemaphoreType.DMA((2 * NZ,)),
         ],
         compiler_params=params(),
-        cost_estimate=cost(2 * tokens * NZ * depth * wide, 4 * 1024 * 1024),
+        cost_estimate=cost(WEIGHT[chunk] * 2 * tokens * NZ * depth * wide, WEIGHT[chunk] * 4 * 1024 * 1024),
     )(*ring, *pieces, *deps)
 
 
@@ -321,32 +323,28 @@
     )
     owns = [pass_on(0, first), pass_on(1, second)]
     got = lax.all_to_all(send, ("x", "c"), 0, 0, tiled=True)
-    ring = [rows, shift(rows, "z", 1, NZ), shift(rows, "z", -1, NZ)]
-
-    low_part, slots = down(got, down_maps.reshape(-1, width), *owns, *ring[1:])
+    r1, l1 = shift(rows, "z", 1, NZ), shift(rows, "z", -1, NZ)
+    low_part, slots = down(got, down_maps.reshape(-1, width))
     lefts = [shift(own, "x", 1, NX) for own in owns]
     rights = [shift(own, "x", -1, NX) for own in owns]
-    ring += [shift(ring[1], "z", 1, NZ), shift(ring[2], "z", -1, NZ)]
-    ring += [shift(ring[3], "z", 1, NZ), shift(ring[4], "z", -1, NZ)]
-
+    r2, l2 = shift(r1, "z", 1, NZ), shift(l1, "z", -1, NZ)
     low_part = lax.all_to_all(low_part, ("y", "z"), 0, 0, tiled=True)
-    low_all = total(low_part, *lefts, *rights, *ring[3:])
+    low_all, token = total(low_part)
     low = lax.all_to_all(low_all, ("y", "z"), 0, 0, tiled=True)
-
-    ring.append(shift(ring[5], "z", 1, NZ))
+    r3, l3 = shift(r2, "z", 1, NZ), shift(l2, "z", -1, NZ)
+    r4 = shift(r3, "z", 1, NZ)
+    ring = [rows, r1, l1, r2, l2, r3, l3, r4]
     fars = [shift(lefts[0], "x", 1, NX), shift(rights[1], "x", -1, NX)]
     chunks = []
     for mine in zip(owns, lefts, rights, fars):
         chunks.append([*mine, *(shift(piece, "c", 1, NC) for piece in mine)])
 
-    two, one, token = base_product(0, ring, chunks[0], pltpu.HBM)
-    delta, token = up(low, slots, up_maps.reshape(-1, width), token)
+    delta, token = up(low, slots, up_maps.reshape(-1, width))
     back = lax.all_to_all(delta, ("x", "c"), 0, 0, tiled=True)
-
+    two, one, token = base_product(0, ring, chunks[0], pltpu.HBM, token)
     three, zero, _ = base_product(1, ring, chunks[1], pltpu.VMEM, token)
-    parts = [zero, shift(one, "y", 1, NY), shift(two, "y", 2, NY), shift(three, "y", 3, NY)]
+    parts = [zero, shift(two, "y", 2, NY), shift(one, "y", 1, NY), shift(three, "y", 3, NY)]
     return final(parts, scale.reshape(1, width), target, back)
-
 
 def solution(mesh):
     fine = Mesh(mesh.devices.reshape(NX, NC, NY, NZ), ("x", "c", "y", "z"))

time: 112 us -> 108 us (0.964)
  waiting for transfers between devices: 16.4 us -> 23.9 us
  starting transfers between devices: 67.7 us -> 60.5 us
  local copies, waits for them, and re-layouts: 4.98 us -> 0.97 us
    ppermute x24, starting transfers between devices: 32.3 us -> 24.4 us  [shift(): return lax.ppermute(a, axis, [(i, (i + by) % size) for i in range(size)])]
    ppermute x24, waiting for transfers between devices: 12.8 us -> 20.4 us  [shift(): return lax.ppermute(a, axis, [(i, (i + by) % size) for i in range(size)])]
    unnamed x18 -> x12, local copies, waits for them, and re-layouts: 4.98 us -> 0.97 us
    ppermute x2, starting transfers between devices: 11.6 us -> 7.74 us  [pass_on(): return lax.ppermute(a, ('x', 'c', 'z'), pairs)]
    all_to_all x1, waiting for transfers between devices: 0.01 us -> 3.51 us  [on_device(): low = lax.all_to_all(low_all, ('y', 'z'), 0, 0, tiled=True)]
    all_to_all x1, waiting for transfers between devices: 2.63 us -> 0.01 us  [on_device(): low_part = lax.all_to_all(low_part, ('y', 'z'), 0, 0, tiled=True)]
    all_to_all x1, starting transfers between devices: 5.66 us -> 8.24 us  [on_device(): low = lax.all_to_all(low_all, ('y', 'z'), 0, 0, tiled=True)]
    all_to_all x1, starting transfers between devices: 5.89 us -> 8.02 us  [on_device(): low_part = lax.all_to_all(low_part, ('y', 'z'), 0, 0, tiled=True)]
where the time goes in v3:
time: 108 us; the launch traced here: 107 us
  starting transfers between devices  60.5 us (56%)
  waiting for transfers between devices  23.9 us (22%)
  Pallas kernels  21.4 us (20%)
    ppermute x24, starting transfers between devices, shift(): return lax.ppermute(a, axis, [(i, (i + by) % size) for i in range(size)])  24.4 us
    ppermute x24, waiting for transfers between devices, shift(): return lax.ppermute(a, axis, [(i, (i + by) % size) for i in range(size)])  20.4 us
    all_to_all x1, starting transfers between devices, on_device(): low = lax.all_to_all(low_all, ('y', 'z'), 0, 0, tiled=True)  8.24 us
    all_to_all x1, starting transfers between devices, on_device(): low_part = lax.all_to_all(low_part, ('y', 'z'), 0, 0, tiled=True)  8.02 us
    ppermute x2, starting transfers between devices, pass_on(): return lax.ppermute(a, ('x', 'c', 'z'), pairs)  7.74 us
    all_to_all x1, starting transfers between devices, on_device(): got = lax.all_to_all(send, ('x', 'c'), 0, 0, tiled=True)  6.69 us
    pallas_call x2, Pallas kernels, base_product(): pl.pallas_call(body, out_shape=[space((tokens, width), BF16)] * 2 + [jax....  6.45 us
    all_to_all x1, starting transfers between devices, on_device(): back = lax.all_to_all(delta, ('x', 'c'), 0, 0, tiled=True)  5.37 us
  transfers between devices with their start and end apart: 30, of which 7 were waited for; matrix products, arithmetic and copies ran while one was open for 0% of the time, Pallas kernels for 15%

profile of v3, /device:TPU:1, one launch (start us, length us, event | category | flops | bytes accessed | tf_op | source)
XLA Modules:
  0.0 106.9 jit_solution(7808598356129899149)
XLA Ops:
  0.0 3.7 %shard_map.73 = (bf16[256,512]{1,0:T(8,128)(2,1)S(1)}, bf16[256,512]{1,0:T(8,128)(2,1)S(1)}, bf16[8,144,256]{2,1,0:T(8,128)(2,1)}, f32[8,512]{1,0:T(8,128)S(1)}) custom-call(s32[1,512]{1,0:T(1,128)} %bitcast.8, s32[1,512]{1,0:T(1,128)} %bitcast.9, bf16[512,256]{1,0:T(8,128)(2,1)} %refs_0_.3, bf16[256,8192]{1,0:T(8,128)(2,1)} %w_ref.1), custom_call_target="tpu_custom_call" | custom-call | flops 2147483648 | bytes 9437184 | tf_op jit(solution)/shard_map/pallas_call | solution.py:91
  3.7 6.7 %all-to-all-start = ((bf16[8,144,256]{2,1,0:T(8,128)(2,1)}), bf16[8,144,256]{2,1,0:T(8,128)(2,1)S(1)}, u32[]{:S(2)}, u32[]{:S(2)}) async-start(bf16[8,144,256]{2,1,0:T(8,128)(2,1)} %get-tuple-element.21), calls=%async_computation | async-start | bytes 1179648 | tf_op jit(solution)/shard_map/all_to_all | solution.py:325
  11.2 4.0 %collective-permute-start.1 = (bf16[512,256]{1,0:T(8,128)(2,1)S(1)}, bf16[512,256]{1,0:T(8,128)(2,1)S(1)}, u32[]{:S(2)}, u32[]{:S(2)}) collective-permute-start(bf16[512,256]{1,0:T(8,128)(2,1)S(1)} %copy-done.1), channel_id=1, source_target_pairs={{0,7},{1,0},{2,1},{3,2},{4,3},{5,4},{6,5},{7,6},{8,15},{9,8},{10,9... | collective-permute-start | bytes 786440 | tf_op jit(solution)/shard_map/ppermute | solution.py:308
  15.2 5.8 %collective-permute-start.15 = (bf16[256,512]{1,0:T(8,128)(2,1)S(1)}, bf16[256,512]{1,0:T(8,128)(2,1)S(1)}, u32[]{:S(2)}, u32[]{:S(2)}) collective-permute-start(bf16[256,512]{1,0:T(8,128)(2,1)S(1)} %get-tuple-element.20), channel_id=1, source_target_pairs={{0,0},{1,1},{2,2},{3,3},{4,4},{5,5},{6,6},{7,7},{32,36},{33,37},{3... | collective-permute-start | bytes 786440 | tf_op jit(solution)/shard_map/ppermute | solution.py:316
  21.0 1.9 %collective-permute-start.7 = (bf16[256,512]{1,0:T(8,128)(2,1)S(1)}, bf16[256,512]{1,0:T(8,128)(2,1)S(1)}, u32[]{:S(2)}, u32[]{:S(2)}) collective-permute-start(bf16[256,512]{1,0:T(8,128)(2,1)S(1)} %get-tuple-element.19), channel_id=1, source_target_pairs={{0,1},{1,2},{2,3},{3,4},{4,5},{5,6},{6,7},{7,0},{32,37},{33,38},{3... | collective-permute-start | bytes 786440 | tf_op jit(solution)/shard_map/ppermute | solution.py:316
  23.0 4.6 %shard_map.74 = (f32[32,16,128]{2,1,0:T(8,128)}, f32[8,1024]{1,0:T(8,128)S(1)}) custom-call(bf16[8,144,256]{2,1,0:T(8,128)(2,1)S(1)} %all-to-all-done.got_ref, bf16[4096,256]{1,0:T(8,128)(2,1)} %bitcast.6), custom_call_target="tpu_custom_call" | custom-call | flops 64424509440 | bytes 62914560 | tf_op jit(solution)/shard_map/pallas_call | solution.py:152
  27.5 8.0 %all-to-all-start.1 = ((f32[32,16,128]{2,1,0:T(8,128)}), f32[32,16,128]{2,1,0:T(8,128)S(1)}, u32[]{:S(2)}, u32[]{:S(2)}) async-start(f32[32,16,128]{2,1,0:T(8,128)} %get-tuple-element.22), calls=%async_computation.1 | async-start | bytes 524288 | tf_op jit(solution)/shard_map/all_to_all | solution.py:331
  35.6 1.4 %collective-permute-start.16 = (bf16[256,512]{1,0:T(8,128)(2,1)S(1)}, bf16[256,512]{1,0:T(8,128)(2,1)S(1)}, u32[]{:S(2)}, u32[]{:S(2)}) collective-permute-start(bf16[256,512]{1,0:T(8,128)(2,1)S(1)} %collective-permute-done.15.refs_8_), channel_id=1, source_target_pairs={{0,64},{64,128},{128,192},{192,0},{1,65},{65,129},{129,193},{193,1... | collective-permute-start | bytes 786440 | tf_op jit(solution)/shard_map/ppermute | solution.py:308
  37.0 1.3 %collective-permute-start.17 = (bf16[256,512]{1,0:T(8,128)(2,1)S(1)}, bf16[256,512]{1,0:T(8,128)(2,1)S(1)}, u32[]{:S(2)}, u32[]{:S(2)}) collective-permute-start(bf16[256,512]{1,0:T(8,128)(2,1)S(1)} %collective-permute-done.15.refs_8_), channel_id=1, source_target_pairs={{0,192},{64,0},{128,64},{192,128},{1,193},{65,1},{129,65},{193,129... | collective-permute-start | bytes 786440 | tf_op jit(solution)/shard_map/ppermute | solution.py:308
  38.3 3.2 %collective-permute-start.2 = (bf16[512,256]{1,0:T(8,128)(2,1)S(1)}, bf16[512,256]{1,0:T(8,128)(2,1)S(1)}, u32[]{:S(2)}, u32[]{:S(2)}) collective-permute-start(bf16[512,256]{1,0:T(8,128)(2,1)S(1)} %collective-permute-done.refs_1_), channel_id=1, source_target_pairs={{0,1},{1,2},{2,3},{3,4},{4,5},{5,6},{6,7},{7,0},{8,9},{9,10},{10,1... | collective-permute-start | bytes 786440 | tf_op jit(solution)/shard_map/ppermute | solution.py:308
  45.0 5.2 %collective-permute-done.2.refs_3_ = bf16[512,256]{1,0:T(8,128)(2,1)S(1)} collective-permute-done((bf16[512,256]{1,0:T(8,128)(2,1)S(1)}, bf16[512,256]{1,0:T(8,128)(2,1)S(1)}, u32[]{:S(2)}, u32[]{:S(2)}) %collective-permute-start.2) | collective-permute-done | bytes 262176 | tf_op jit(solution)/shard_map/ppermute | solution.py:308
  50.2 1.4 %collective-permute-start.18 = (bf16[256,512]{1,0:T(8,128)(2,1)S(1)}, bf16[256,512]{1,0:T(8,128)(2,1)}, u32[]{:S(2)}, u32[]{:S(2)}) collective-permute-start(bf16[256,512]{1,0:T(8,128)(2,1)S(1)} %collective-permute-done.16.refs_9_), channel_id=1, source_target_pairs={{0,64},{64,128},{128,192},{192,0},{1,65},{65,129},{129,193},{193,1... | collective-permute-start | bytes 786440 | tf_op jit(solution)/shard_map/ppermute | solution.py:308
  53.3 8.2 %all-to-all-start.2 = ((bf16[32,16,128]{2,1,0:T(8,128)(2,1)}), bf16[32,16,128]{2,1,0:T(8,128)(2,1)S(1)}, u32[]{:S(2)}, u32[]{:S(2)}) async-start(bf16[32,16,128]{2,1,0:T(8,128)(2,1)} %get-tuple-element.23), calls=%async_computation.2 | async-start | bytes 262144 | tf_op jit(solution)/shard_map/all_to_all | solution.py:333
  62.5 2.7 %collective-permute-start.5 = (bf16[512,256]{1,0:T(8,128)(2,1)S(1)}, bf16[512,256]{1,0:T(8,128)(2,1)}, u32[]{:S(2)}, u32[]{:S(2)}) collective-permute-start(bf16[512,256]{1,0:T(8,128)(2,1)S(1)} %collective-permute-done.3.refs_4_), channel_id=1, source_target_pairs={{0,7},{1,0},{2,1},{3,2},{4,3},{5,4},{6,5},{7,6},{8,15},{9,8},{10,9... | collective-permute-start | bytes 786440 | tf_op jit(solution)/shard_map/ppermute | solution.py:308
  65.2 1.3 %collective-permute-start.10 = (bf16[256,512]{1,0:T(8,128)(2,1)S(1)}, bf16[256,512]{1,0:T(8,128)(2,1)}, u32[]{:S(2)}, u32[]{:S(2)}) collective-permute-start(bf16[256,512]{1,0:T(8,128)(2,1)S(1)} %collective-permute-done.9.refs_10_), channel_id=1, source_target_pairs={{0,192},{64,0},{128,64},{192,128},{1,193},{65,1},{129,65},{193,129... | collective-permute-start | bytes 786440 | tf_op jit(solution)/shard_map/ppermute | solution.py:308
  67.2 3.5 %all-to-all-done.2.low_ref = bf16[32,16,128]{2,1,0:T(8,128)(2,1)S(1)} async-done(((bf16[32,16,128]{2,1,0:T(8,128)(2,1)}), bf16[32,16,128]{2,1,0:T(8,128)(2,1)S(1)}, u32[]{:S(2)}, u32[]{:S(2)}) %all-to-all-start.2) | async-done | bytes 131104 | tf_op jit(solution)/shard_map/all_to_all | solution.py:333
  70.7 4.7 %shard_map.76 = (bf16[8,128,256]{2,1,0:T(8,128)(2,1)}, f32[8,128]{1,0:T(8,128)S(1)}) custom-call(bf16[32,16,128]{2,1,0:T(8,128)(2,1)S(1)} %all-to-all-done.2.low_ref, f32[8,1024]{1,0:T(8,128)S(1)} %get-tuple-element.24.slot_ref, bf16[4096,256]{1,0:T(8,128)(2,1)} %bitcast.7), custom_call_target="tpu_custom_call" | custom-call | flops 64424509440 | bytes 62914560 | tf_op jit(solution)/shard_map/pallas_call | solution.py:217
  75.5 5.4 %all-to-all-start.3 = ((bf16[8,128,256]{2,1,0:T(8,128)(2,1)}), bf16[8,128,256]{2,1,0:T(8,128)(2,1)S(1)}, u32[]{:S(2)}, u32[]{:S(2)}) async-start(bf16[8,128,256]{2,1,0:T(8,128)(2,1)} %get-tuple-element.32), calls=%async_computation.3 | async-start | bytes 1048576 | tf_op jit(solution)/shard_map/all_to_all | solution.py:343
  82.8 3.7 %shard_map.77 = (bf16[512,256]{1,0:T(8,128)(2,1)}, bf16[512,256]{1,0:T(8,128)(2,1)}, f32[8,128]{1,0:T(8,128)S(1)}) custom-call(bf16[512,256]{1,0:T(8,128)(2,1)S(1)} %copy-done.1, bf16[512,256]{1,0:T(8,128)(2,1)S(1)} %collective-permute-done.refs_1_, bf16[512,256]{1,0:T(8,128)(2,1)S(1)} %collective-permute-done.1.refs_2_, ...), custom_call_target="tpu_custom_call" | custom-call | flops 4294967296 | bytes 16777216 | tf_op jit(solution)/shard_map/pallas_call | solution.py:264
  86.6 2.7 %shard_map.78 = (bf16[512,256]{1,0:T(8,128)(2,1)S(1)}, bf16[512,256]{1,0:T(8,128)(2,1)S(1)}, f32[8,128]{1,0:T(8,128)}) custom-call(bf16[512,256]{1,0:T(8,128)(2,1)S(1)} %copy-done.1, bf16[512,256]{1,0:T(8,128)(2,1)S(1)} %collective-permute-done.refs_1_, bf16[512,256]{1,0:T(8,128)(2,1)S(1)} %collective-permute-done.1.refs_2_, ...), custom_call_target="tpu_custom_call" | custom-call | flops 4294967296 | bytes 16777216 | tf_op jit(solution)/shard_map/pallas_call | solution.py:264
  90.3 1.2 %collective-permute-start.23 = (bf16[512,256]{1,0:T(8,128)(2,1)S(1)}, bf16[512,256]{1,0:T(8,128)(2,1)S(1)}, u32[]{:S(2)}, u32[]{:S(2)}) collective-permute-start(bf16[512,256]{1,0:T(8,128)(2,1)S(1)} %copy-done.5), channel_id=1, source_target_pairs={{0,16},{8,24},{16,0},{24,8},{1,17},{9,25},{17,1},{25,9},{2,18},{10... | collective-permute-start | bytes 786440 | tf_op jit(solution)/shard_map/ppermute | solution.py:308
  91.6 5.6 %collective-permute-done.25.refs_3_ = bf16[512,256]{1,0:T(8,128)(2,1)S(1)} collective-permute-done((bf16[512,256]{1,0:T(8,128)(2,1)S(1)}, bf16[512,256]{1,0:T(8,128)(2,1)S(1)}, u32[]{:S(2)}, u32[]{:S(2)}) %collective-permute-start.25) | collective-permute-done | bytes 262176 | tf_op jit(solution)/shard_map/ppermute | solution.py:308
  97.2 2.1 %collective-permute-done.23.refs_1_ = bf16[512,256]{1,0:T(8,128)(2,1)S(1)} collective-permute-done((bf16[512,256]{1,0:T(8,128)(2,1)S(1)}, bf16[512,256]{1,0:T(8,128)(2,1)S(1)}, u32[]{:S(2)}, u32[]{:S(2)}) %collective-permute-start.23) | collective-permute-done | bytes 262176 | tf_op jit(solution)/shard_map/ppermute | solution.py:308
  99.3 6.4 %collective-permute-done.24.refs_2_ = bf16[512,256]{1,0:T(8,128)(2,1)S(1)} collective-permute-done((bf16[512,256]{1,0:T(8,128)(2,1)S(1)}, bf16[512,256]{1,0:T(8,128)(2,1)S(1)}, u32[]{:S(2)}, u32[]{:S(2)}) %collective-permute-start.24) | collective-permute-done | bytes 262176 | tf_op jit(solution)/shard_map/ppermute | solution.py:308
  (55 shorter events, 11.8 us)
Async XLA Ops:
  3.7 19.3 %all-to-all-start = ((bf16[8,144,256]{2,1,0:T(8,128)(2,1)}), bf16[8,144,256]{2,1,0:T(8,128)(2,1)S(1)}, u32[]{:S(2)}, u32[]{:S(2)}) async-start(bf16[8,144,256]{2,1,0:T(8,128)(2,1)} %get-tuple-element.21), calls=%async_computation | async-start | bytes 1179648 | tf_op jit(solution)/shard_map/all_to_all | solution.py:325
  10.4 27.9 %collective-permute-start = (bf16[512,256]{1,0:T(8,128)(2,1)S(1)}, bf16[512,256]{1,0:T(8,128)(2,1)S(1)}, u32[]{:S(2)}, u32[]{:S(2)}) collective-permute-start(bf16[512,256]{1,0:T(8,128)(2,1)S(1)} %copy-done.1), channel_id=1, source_target_pairs={{0,1},{1,2},{2,3},{3,4},{4,5},{5,6},{6,7},{7,0},{8,9},{9,10},{10,1... | collective-permute-start | bytes 786440 | tf_op jit(solution)/shard_map/ppermute | solution.py:308
  11.2 30.3 %collective-permute-start.1 = (bf16[512,256]{1,0:T(8,128)(2,1)S(1)}, bf16[512,256]{1,0:T(8,128)(2,1)S(1)}, u32[]{:S(2)}, u32[]{:S(2)}) collective-permute-start(bf16[512,256]{1,0:T(8,128)(2,1)S(1)} %copy-done.1), channel_id=1, source_target_pairs={{0,7},{1,0},{2,1},{3,2},{4,3},{5,4},{6,5},{7,6},{8,15},{9,8},{10,9... | collective-permute-start | bytes 786440 | tf_op jit(solution)/shard_map/ppermute | solution.py:308
  15.2 20.4 %collective-permute-start.15 = (bf16[256,512]{1,0:T(8,128)(2,1)S(1)}, bf16[256,512]{1,0:T(8,128)(2,1)S(1)}, u32[]{:S(2)}, u32[]{:S(2)}) collective-permute-start(bf16[256,512]{1,0:T(8,128)(2,1)S(1)} %get-tuple-element.20), channel_id=1, source_target_pairs={{0,0},{1,1},{2,2},{3,3},{4,4},{5,5},{6,6},{7,7},{32,36},{33,37},{3... | collective-permute-start | bytes 786440 | tf_op jit(solution)/shard_map/ppermute | solution.py:316
  21.0 20.7 %collective-permute-start.7 = (bf16[256,512]{1,0:T(8,128)(2,1)S(1)}, bf16[256,512]{1,0:T(8,128)(2,1)S(1)}, u32[]{:S(2)}, u32[]{:S(2)}) collective-permute-start(bf16[256,512]{1,0:T(8,128)(2,1)S(1)} %get-tuple-element.19), channel_id=1, source_target_pairs={{0,1},{1,2},{2,3},{3,4},{4,5},{5,6},{6,7},{7,0},{32,37},{33,38},{3... | collective-permute-start | bytes 786440 | tf_op jit(solution)/shard_map/ppermute | solution.py:316
  27.5 25.1 %all-to-all-start.1 = ((f32[32,16,128]{2,1,0:T(8,128)}), f32[32,16,128]{2,1,0:T(8,128)S(1)}, u32[]{:S(2)}, u32[]{:S(2)}) async-start(f32[32,16,128]{2,1,0:T(8,128)} %get-tuple-element.22), calls=%async_computation.1 | async-start | bytes 524288 | tf_op jit(solution)/shard_map/all_to_all | solution.py:331
  35.6 8.0 %collective-permute-start.16 = (bf16[256,512]{1,0:T(8,128)(2,1)S(1)}, bf16[256,512]{1,0:T(8,128)(2,1)S(1)}, u32[]{:S(2)}, u32[]{:S(2)}) collective-permute-start(bf16[256,512]{1,0:T(8,128)(2,1)S(1)} %collective-permute-done.15.refs_8_), channel_id=1, source_target_pairs={{0,64},{64,128},{128,192},{192,0},{1,65},{65,129},{129,193},{193,1... | collective-permute-start | bytes 786440 | tf_op jit(solution)/shard_map/ppermute | solution.py:308
  38.3 11.9 %collective-permute-start.2 = (bf16[512,256]{1,0:T(8,128)(2,1)S(1)}, bf16[512,256]{1,0:T(8,128)(2,1)S(1)}, u32[]{:S(2)}, u32[]{:S(2)}) collective-permute-start(bf16[512,256]{1,0:T(8,128)(2,1)S(1)} %collective-permute-done.refs_1_), channel_id=1, source_target_pairs={{0,1},{1,2},{2,3},{3,4},{4,5},{5,6},{6,7},{7,0},{8,9},{9,10},{10,1... | collective-permute-start | bytes 786440 | tf_op jit(solution)/shard_map/ppermute | solution.py:308
  41.5 10.0 %collective-permute-start.19 = (bf16[256,512]{1,0:T(8,128)(2,1)S(1)}, bf16[256,512]{1,0:T(8,128)(2,1)S(1)}, u32[]{:S(2)}, u32[]{:S(2)}) collective-permute-start(bf16[256,512]{1,0:T(8,128)(2,1)S(1)} %collective-permute-done.15.refs_8_), channel_id=1, source_target_pairs={{0,32},{32,0},{1,33},{33,1},{2,34},{34,2},{3,35},{35,3},{4,36},{36... | collective-permute-start | bytes 786440 | tf_op jit(solution)/shard_map/ppermute | solution.py:308
  41.8 10.8 %collective-permute-start.3 = (bf16[512,256]{1,0:T(8,128)(2,1)S(1)}, bf16[512,256]{1,0:T(8,128)(2,1)S(1)}, u32[]{:S(2)}, u32[]{:S(2)}) collective-permute-start(bf16[512,256]{1,0:T(8,128)(2,1)S(1)} %collective-permute-done.1.refs_2_), channel_id=1, source_target_pairs={{0,7},{1,0},{2,1},{3,2},{4,3},{5,4},{6,5},{7,6},{8,15},{9,8},{10,9... | collective-permute-start | bytes 786440 | tf_op jit(solution)/shard_map/ppermute | solution.py:308
  43.6 18.0 %collective-permute-start.9 = (bf16[256,512]{1,0:T(8,128)(2,1)S(1)}, bf16[256,512]{1,0:T(8,128)(2,1)S(1)}, u32[]{:S(2)}, u32[]{:S(2)}) collective-permute-start(bf16[256,512]{1,0:T(8,128)(2,1)S(1)} %collective-permute-done.7.refs_8_), channel_id=1, source_target_pairs={{0,192},{64,0},{128,64},{192,128},{1,193},{65,1},{129,65},{193,129... | collective-permute-start | bytes 786440 | tf_op jit(solution)/shard_map/ppermute | solution.py:308
  44.5 18.0 %collective-permute-start.8 = (bf16[256,512]{1,0:T(8,128)(2,1)S(1)}, bf16[256,512]{1,0:T(8,128)(2,1)S(1)}, u32[]{:S(2)}, u32[]{:S(2)}) collective-permute-start(bf16[256,512]{1,0:T(8,128)(2,1)S(1)} %collective-permute-done.7.refs_8_), channel_id=1, source_target_pairs={{0,64},{64,128},{128,192},{192,0},{1,65},{65,129},{129,193},{193,1... | collective-permute-start | bytes 786440 | tf_op jit(solution)/shard_map/ppermute | solution.py:308
  50.2 15.0 %collective-permute-start.18 = (bf16[256,512]{1,0:T(8,128)(2,1)S(1)}, bf16[256,512]{1,0:T(8,128)(2,1)}, u32[]{:S(2)}, u32[]{:S(2)}) collective-permute-start(bf16[256,512]{1,0:T(8,128)(2,1)S(1)} %collective-permute-done.16.refs_9_), channel_id=1, source_target_pairs={{0,64},{64,128},{128,192},{192,0},{1,65},{65,129},{129,193},{193,1... | collective-permute-start | bytes 786440 | tf_op jit(solution)/shard_map/ppermute | solution.py:308
  51.6 15.0 %collective-permute-start.20 = (bf16[256,512]{1,0:T(8,128)(2,1)S(1)}, bf16[256,512]{1,0:T(8,128)(2,1)}, u32[]{:S(2)}, u32[]{:S(2)}) collective-permute-start(bf16[256,512]{1,0:T(8,128)(2,1)S(1)} %collective-permute-done.16.refs_9_), channel_id=1, source_target_pairs={{0,32},{32,0},{1,33},{33,1},{2,34},{34,2},{3,35},{35,3},{4,36},{36... | collective-permute-start | bytes 786440 | tf_op jit(solution)/shard_map/ppermute | solution.py:308
  52.6 14.6 %collective-permute-start.4 = (bf16[512,256]{1,0:T(8,128)(2,1)S(1)}, bf16[512,256]{1,0:T(8,128)(2,1)}, u32[]{:S(2)}, u32[]{:S(2)}) collective-permute-start(bf16[512,256]{1,0:T(8,128)(2,1)S(1)} %collective-permute-done.2.refs_3_), channel_id=1, source_target_pairs={{0,1},{1,2},{2,3},{3,4},{4,5},{5,6},{6,7},{7,0},{8,9},{9,10},{10,1... | collective-permute-start | bytes 786440 | tf_op jit(solution)/shard_map/ppermute | solution.py:308
  53.3 17.4 %all-to-all-start.2 = ((bf16[32,16,128]{2,1,0:T(8,128)(2,1)}), bf16[32,16,128]{2,1,0:T(8,128)(2,1)S(1)}, u32[]{:S(2)}, u32[]{:S(2)}) async-start(bf16[32,16,128]{2,1,0:T(8,128)(2,1)} %get-tuple-element.23), calls=%async_computation.2 | async-start | bytes 262144 | tf_op jit(solution)/shard_map/all_to_all | solution.py:333
  61.6 19.3 %collective-permute-start.21 = (bf16[256,512]{1,0:T(8,128)(2,1)S(1)}, bf16[256,512]{1,0:T(8,128)(2,1)}, u32[]{:S(2)}, u32[]{:S(2)}) collective-permute-start(bf16[256,512]{1,0:T(8,128)(2,1)S(1)} %collective-permute-done.17.refs_10_), channel_id=1, source_target_pairs={{0,32},{32,0},{1,33},{33,1},{2,34},{34,2},{3,35},{35,3},{4,36},{36... | collective-permute-start | bytes 786440 | tf_op jit(solution)/shard_map/ppermute | solution.py:308
  62.5 18.5 %collective-permute-start.5 = (bf16[512,256]{1,0:T(8,128)(2,1)S(1)}, bf16[512,256]{1,0:T(8,128)(2,1)}, u32[]{:S(2)}, u32[]{:S(2)}) collective-permute-start(bf16[512,256]{1,0:T(8,128)(2,1)S(1)} %collective-permute-done.3.refs_4_), channel_id=1, source_target_pairs={{0,7},{1,0},{2,1},{3,2},{4,3},{5,4},{6,5},{7,6},{8,15},{9,8},{10,9... | collective-permute-start | bytes 786440 | tf_op jit(solution)/shard_map/ppermute | solution.py:308
  65.2 16.1 %collective-permute-start.10 = (bf16[256,512]{1,0:T(8,128)(2,1)S(1)}, bf16[256,512]{1,0:T(8,128)(2,1)}, u32[]{:S(2)}, u32[]{:S(2)}) collective-permute-start(bf16[256,512]{1,0:T(8,128)(2,1)S(1)} %collective-permute-done.9.refs_10_), channel_id=1, source_target_pairs={{0,192},{64,0},{128,64},{192,128},{1,193},{65,1},{129,65},{193,129... | collective-permute-start | bytes 786440 | tf_op jit(solution)/shard_map/ppermute | solution.py:308
  66.6 15.0 %collective-permute-start.22 = (bf16[256,512]{1,0:T(8,128)(2,1)}, bf16[256,512]{1,0:T(8,128)(2,1)}, u32[]{:S(2)}, u32[]{:S(2)}) collective-permute-start(bf16[256,512]{1,0:T(8,128)(2,1)} %collective-permute-done.18.refs_11_), channel_id=1, source_target_pairs={{0,32},{32,0},{1,33},{33,1},{2,34},{34,2},{3,35},{35,3},{4,36},{36... | collective-permute-start | bytes 786440 | tf_op jit(solution)/shard_map/ppermute | solution.py:308
  67.2 14.7 %collective-permute-start.6 = (bf16[512,256]{1,0:T(8,128)(2,1)}, bf16[512,256]{1,0:T(8,128)(2,1)}, u32[]{:S(2)}, u32[]{:S(2)}) collective-permute-start(bf16[512,256]{1,0:T(8,128)(2,1)} %collective-permute-done.4.refs_5_), channel_id=1, source_target_pairs={{0,1},{1,2},{2,3},{3,4},{4,5},{5,6},{6,7},{7,0},{8,9},{9,10},{10,1... | collective-permute-start | bytes 786440 | tf_op jit(solution)/shard_map/ppermute | solution.py:308
  75.5 30.2 %all-to-all-start.3 = ((bf16[8,128,256]{2,1,0:T(8,128)(2,1)}), bf16[8,128,256]{2,1,0:T(8,128)(2,1)S(1)}, u32[]{:S(2)}, u32[]{:S(2)}) async-start(bf16[8,128,256]{2,1,0:T(8,128)(2,1)} %get-tuple-element.32), calls=%async_computation.3 | async-start | bytes 1048576 | tf_op jit(solution)/shard_map/all_to_all | solution.py:343
  90.3 8.9 %collective-permute-start.23 = (bf16[512,256]{1,0:T(8,128)(2,1)S(1)}, bf16[512,256]{1,0:T(8,128)(2,1)S(1)}, u32[]{:S(2)}, u32[]{:S(2)}) collective-permute-start(bf16[512,256]{1,0:T(8,128)(2,1)S(1)} %copy-done.5), channel_id=1, source_target_pairs={{0,16},{8,24},{16,0},{24,8},{1,17},{9,25},{17,1},{25,9},{2,18},{10... | collective-permute-start | bytes 786440 | tf_op jit(solution)/shard_map/ppermute | solution.py:308
  91.6 14.1 %collective-permute-start.24 = (bf16[512,256]{1,0:T(8,128)(2,1)S(1)}, bf16[512,256]{1,0:T(8,128)(2,1)S(1)}, u32[]{:S(2)}, u32[]{:S(2)}) collective-permute-start(bf16[512,256]{1,0:T(8,128)(2,1)S(1)} %copy-done.4), channel_id=1, source_target_pairs={{0,8},{8,16},{16,24},{24,0},{1,9},{9,17},{17,25},{25,1},{2,10},{10... | collective-permute-start | bytes 786440 | tf_op jit(solution)/shard_map/ppermute | solution.py:308
  (12 other events, 99.8 us)

commit v4 on v3

--- a/solution.py
+++ b/solution.py
@@ -230,10 +230,10 @@
 
 def base_body(chunk, *refs):
     ring, pieces = refs[:NZ], refs[NZ : 2 * NZ]
-    o_ref, p_ref, token_ref, a_ref, w_ref, sem = refs[-6:]
+    token_ref, a_ref, w_ref, sem = refs[-4:]
     token_ref[...] = jnp.zeros_like(token_ref)
     x, c = lax.axis_index("x"), lax.axis_index("c")
-    depth, width = w_ref.shape[1], o_ref.shape[1]
+    depth, width = w_ref.shape[1], ring[0].shape[1]
     copies = []
     for at, slot in enumerate((0, 1, 7, 2, 6, 3, 5, 4)):
         copies.append(pltpu.make_async_copy(ring[at], a_ref.at[slot], sem.at[at]))
@@ -250,8 +250,16 @@
         w_ref[...].reshape(NZ * depth, w_ref.shape[2]),
         preferred_element_type=F32,
     )
-    o_ref[...] = whole[:, :width].astype(BF16)
-    p_ref[...] = whole[:, width:].astype(BF16)
+    whole = whole.astype(BF16)
+    if chunk == 0:
+        top_ref, bottom_ref, p_ref = refs[-7:-4]
+        half = whole.shape[0] // 2
+        top_ref[...] = whole[:half, :width]
+        bottom_ref[...] = whole[half:, :width]
+    else:
+        o_ref, p_ref = refs[-6:-4]
+        o_ref[...] = whole[:, :width]
+    p_ref[...] = whole[:, width:]
 
 
 def base_product(chunk, ring, pieces, space, *deps):
@@ -261,11 +269,13 @@
     def body(*refs):
         base_body(chunk, *refs)
 
+    block, half = space((tokens, width), BF16), space((tokens // 2, width), BF16)
+    outs = [half, half, block] if chunk == 0 else [block, block]
     return pl.pallas_call(
         body,
-        out_shape=[space((tokens, width), BF16)] * 2 + [jax.ShapeDtypeStruct((8, 128), F32)],
+        out_shape=[*outs, jax.ShapeDtypeStruct((8, 128), F32)],
         in_specs=[ANY] * (2 * NZ + len(deps)),
-        out_specs=[LOCAL] * 3,
+        out_specs=[LOCAL] * (len(outs) + 1),
         scratch_shapes=[
             pltpu.VMEM((NZ, tokens, width), BF16),
             pltpu.VMEM((NZ, depth, wide), BF16),
@@ -277,17 +287,17 @@
 
 
 def final_body(*refs):
-    parts, (scale_ref, target_ref, back_ref, o_ref) = refs[:NY], refs[NY:]
+    parts, halves, (scale_ref, target_ref, back_ref, o_ref) = refs[:3], refs[3:5], refs[5:]
     tokens = o_ref.shape[0]
     back = back_ref[...].reshape(GROUPS * CAP, back_ref.shape[2])
-    step = 256
+    step = tokens // 2
     for b in range(tokens // step):
         here = slice(b * step, (b + 1) * step)
         spot = lax.broadcasted_iota(jnp.int32, (GROUPS * CAP, step), 0).astype(F32)
         select = jnp.where(spot == target_ref[:1, here], 1.0, 0.0).astype(BF16)
         delta = lax.dot_general(select, back, TN, preferred_element_type=F32)
-        summed = parts[0][here, :].astype(F32)
-        for part in parts[1:]:
+        summed = halves[b][...].astype(F32)
+        for part in parts:
             summed += part[here, :].astype(F32)
         o_ref[here, :] = (summed * scale_ref[...] + delta).astype(BF16)
 
@@ -297,7 +307,7 @@
     return pl.pallas_call(
         final_body,
         out_shape=jax.ShapeDtypeStruct((tokens, width), BF16),
-        in_specs=[LOCAL] * (NY + 3),
+        in_specs=[LOCAL] * (NY + 4),
         out_specs=LOCAL,
         compiler_params=params(),
         cost_estimate=cost(2 * GROUPS * CAP * tokens * width, 4 * 1024 * 1024),
@@ -341,9 +351,10 @@
 
     delta, token = up(low, slots, up_maps.reshape(-1, width))
     back = lax.all_to_all(delta, ("x", "c"), 0, 0, tiled=True)
-    two, one, token = base_product(0, ring, chunks[0], pltpu.HBM, token)
+    top, bottom, one, token = base_product(0, ring, chunks[0], pltpu.HBM, token)
     three, zero, _ = base_product(1, ring, chunks[1], pltpu.VMEM, token)
-    parts = [zero, shift(two, "y", 2, NY), shift(one, "y", 1, NY), shift(three, "y", 3, NY)]
+    bottom = shift(shift(bottom, "y", 3, NY), "y", 3, NY)
+    parts = [zero, shift(one, "y", 1, NY), shift(three, "y", 3, NY), shift(top, "y", 2, NY), bottom]
     return final(parts, scale.reshape(1, width), target, back)
 
 def solution(mesh):

time: 108 us -> 106 us (0.981)
  waiting for transfers between devices: 23.9 us -> 19.3 us
  starting transfers between devices: 60.5 us -> 64.3 us
    ppermute x24 -> x26, starting transfers between devices: 24.4 us -> 29.1 us  [shift(): return lax.ppermute(a, axis, [(i, (i + by) % size) for i in range(size)])]
    ppermute x24 -> x26, waiting for transfers between devices: 20.4 us -> 15.8 us  [shift(): return lax.ppermute(a, axis, [(i, (i + by) % size) for i in range(size)])]
  transfers between devices with their start and end apart: 30 -> 32, of which waited for: 7 -> 6; matrix products, arithmetic and copies ran while one was open for 0% -> 0% of each run, Pallas kernels for 15% -> 16%
where the time goes in v4:
time: 106 us; the launch traced here: 105 us
  starting transfers between devices  64.3 us (61%)
  Pallas kernels  21.6 us (20%)
  waiting for transfers between devices  19.3 us (18%)
    ppermute x26, starting transfers between devices, shift(): return lax.ppermute(a, axis, [(i, (i + by) % size) for i in range(size)])  29.1 us
    ppermute x26, waiting for transfers between devices, shift(): return lax.ppermute(a, axis, [(i, (i + by) % size) for i in range(size)])  15.8 us
    all_to_all x1, starting transfers between devices, on_device(): low = lax.all_to_all(low_all, ('y', 'z'), 0, 0, tiled=True)  8.24 us
    all_to_all x1, starting transfers between devices, on_device(): low_part = lax.all_to_all(low_part, ('y', 'z'), 0, 0, tiled=True)  8.03 us
    ppermute x2, starting transfers between devices, pass_on(): return lax.ppermute(a, ('x', 'c', 'z'), pairs)  7.74 us
    pallas_call x2, Pallas kernels, base_product(): pl.pallas_call(body, out_shape=[*outs, jax.ShapeDtypeStruct((8, 128), F32...  6.71 us
    all_to_all x1, starting transfers between devices, on_device(): got = lax.all_to_all(send, ('x', 'c'), 0, 0, tiled=True)  6.69 us
    pallas_call x1, Pallas kernels, up(): pl.pallas_call(up_body, out_shape=(pltpu.HBM((GROUPS, CAP, width), BF16),...  4.72 us
  transfers between devices with their start and end apart: 32, of which 6 were waited for; matrix products, arithmetic and copies ran while one was open for 0% of the time, Pallas kernels for 16%

profile of v4, /device:TPU:1, one launch (start us, length us, event | category | flops | bytes accessed | tf_op | source)
XLA Modules:
  0.0 105.5 jit_solution(10356960242676988715)
XLA Ops:
  0.0 3.7 %shard_map.73 = (bf16[256,512]{1,0:T(8,128)(2,1)S(1)}, bf16[256,512]{1,0:T(8,128)(2,1)S(1)}, bf16[8,144,256]{2,1,0:T(8,128)(2,1)}, f32[8,512]{1,0:T(8,128)S(1)}) custom-call(s32[1,512]{1,0:T(1,128)} %bitcast.8, s32[1,512]{1,0:T(1,128)} %bitcast.9, bf16[512,256]{1,0:T(8,128)(2,1)} %refs_0_.3, bf16[256,8192]{1,0:T(8,128)(2,1)} %w_ref.1), custom_call_target="tpu_custom_call" | custom-call | flops 2147483648 | bytes 9437184 | tf_op jit(solution)/shard_map/pallas_call | solution.py:91
  3.7 6.7 %all-to-all-start = ((bf16[8,144,256]{2,1,0:T(8,128)(2,1)}), bf16[8,144,256]{2,1,0:T(8,128)(2,1)S(1)}, u32[]{:S(2)}, u32[]{:S(2)}) async-start(bf16[8,144,256]{2,1,0:T(8,128)(2,1)} %get-tuple-element.22), calls=%async_computation | async-start | bytes 1179648 | tf_op jit(solution)/shard_map/all_to_all | solution.py:335
  11.2 4.0 %collective-permute-start.1 = (bf16[512,256]{1,0:T(8,128)(2,1)S(1)}, bf16[512,256]{1,0:T(8,128)(2,1)S(1)}, u32[]{:S(2)}, u32[]{:S(2)}) collective-permute-start(bf16[512,256]{1,0:T(8,128)(2,1)S(1)} %copy-done.1), channel_id=1, source_target_pairs={{0,7},{1,0},{2,1},{3,2},{4,3},{5,4},{6,5},{7,6},{8,15},{9,8},{10,9... | collective-permute-start | bytes 786440 | tf_op jit(solution)/shard_map/ppermute | solution.py:318
  15.2 5.8 %collective-permute-start.15 = (bf16[256,512]{1,0:T(8,128)(2,1)S(1)}, bf16[256,512]{1,0:T(8,128)(2,1)S(1)}, u32[]{:S(2)}, u32[]{:S(2)}) collective-permute-start(bf16[256,512]{1,0:T(8,128)(2,1)S(1)} %get-tuple-element.21), channel_id=1, source_target_pairs={{0,0},{1,1},{2,2},{3,3},{4,4},{5,5},{6,6},{7,7},{32,36},{33,37},{3... | collective-permute-start | bytes 786440 | tf_op jit(solution)/shard_map/ppermute | solution.py:326
  21.0 1.9 %collective-permute-start.7 = (bf16[256,512]{1,0:T(8,128)(2,1)S(1)}, bf16[256,512]{1,0:T(8,128)(2,1)S(1)}, u32[]{:S(2)}, u32[]{:S(2)}) collective-permute-start(bf16[256,512]{1,0:T(8,128)(2,1)S(1)} %get-tuple-element.20), channel_id=1, source_target_pairs={{0,1},{1,2},{2,3},{3,4},{4,5},{5,6},{6,7},{7,0},{32,37},{33,38},{3... | collective-permute-start | bytes 786440 | tf_op jit(solution)/shard_map/ppermute | solution.py:326
  23.0 4.5 %shard_map.74 = (f32[32,16,128]{2,1,0:T(8,128)}, f32[8,1024]{1,0:T(8,128)S(1)}) custom-call(bf16[8,144,256]{2,1,0:T(8,128)(2,1)S(1)} %all-to-all-done.got_ref, bf16[4096,256]{1,0:T(8,128)(2,1)} %bitcast.6), custom_call_target="tpu_custom_call" | custom-call | flops 64424509440 | bytes 62914560 | tf_op jit(solution)/shard_map/pallas_call | solution.py:152
  27.5 8.0 %all-to-all-start.1 = ((f32[32,16,128]{2,1,0:T(8,128)}), f32[32,16,128]{2,1,0:T(8,128)S(1)}, u32[]{:S(2)}, u32[]{:S(2)}) async-start(f32[32,16,128]{2,1,0:T(8,128)} %get-tuple-element.23), calls=%async_computation.1 | async-start | bytes 524288 | tf_op jit(solution)/shard_map/all_to_all | solution.py:341
  35.6 1.4 %collective-permute-start.16 = (bf16[256,512]{1,0:T(8,128)(2,1)S(1)}, bf16[256,512]{1,0:T(8,128)(2,1)S(1)}, u32[]{:S(2)}, u32[]{:S(2)}) collective-permute-start(bf16[256,512]{1,0:T(8,128)(2,1)S(1)} %collective-permute-done.15.refs_8_), channel_id=1, source_target_pairs={{0,64},{64,128},{128,192},{192,0},{1,65},{65,129},{129,193},{193,1... | collective-permute-start | bytes 786440 | tf_op jit(solution)/shard_map/ppermute | solution.py:318
  37.0 1.3 %collective-permute-start.17 = (bf16[256,512]{1,0:T(8,128)(2,1)S(1)}, bf16[256,512]{1,0:T(8,128)(2,1)S(1)}, u32[]{:S(2)}, u32[]{:S(2)}) collective-permute-start(bf16[256,512]{1,0:T(8,128)(2,1)S(1)} %collective-permute-done.15.refs_8_), channel_id=1, source_target_pairs={{0,192},{64,0},{128,64},{192,128},{1,193},{65,1},{129,65},{193,129... | collective-permute-start | bytes 786440 | tf_op jit(solution)/shard_map/ppermute | solution.py:318
  38.3 3.2 %collective-permute-start.2 = (bf16[512,256]{1,0:T(8,128)(2,1)S(1)}, bf16[512,256]{1,0:T(8,128)(2,1)S(1)}, u32[]{:S(2)}, u32[]{:S(2)}) collective-permute-start(bf16[512,256]{1,0:T(8,128)(2,1)S(1)} %collective-permute-done.refs_1_), channel_id=1, source_target_pairs={{0,1},{1,2},{2,3},{3,4},{4,5},{5,6},{6,7},{7,0},{8,9},{9,10},{10,1... | collective-permute-start | bytes 786440 | tf_op jit(solution)/shard_map/ppermute | solution.py:318
  45.0 5.2 %collective-permute-done.2.refs_3_ = bf16[512,256]{1,0:T(8,128)(2,1)S(1)} collective-permute-done((bf16[512,256]{1,0:T(8,128)(2,1)S(1)}, bf16[512,256]{1,0:T(8,128)(2,1)S(1)}, u32[]{:S(2)}, u32[]{:S(2)}) %collective-permute-start.2) | collective-permute-done | bytes 262176 | tf_op jit(solution)/shard_map/ppermute | solution.py:318
  50.2 1.4 %collective-permute-start.18 = (bf16[256,512]{1,0:T(8,128)(2,1)S(1)}, bf16[256,512]{1,0:T(8,128)(2,1)}, u32[]{:S(2)}, u32[]{:S(2)}) collective-permute-start(bf16[256,512]{1,0:T(8,128)(2,1)S(1)} %collective-permute-done.16.refs_9_), channel_id=1, source_target_pairs={{0,64},{64,128},{128,192},{192,0},{1,65},{65,129},{129,193},{193,1... | collective-permute-start | bytes 786440 | tf_op jit(solution)/shard_map/ppermute | solution.py:318
  53.3 8.2 %all-to-all-start.2 = ((bf16[32,16,128]{2,1,0:T(8,128)(2,1)}), bf16[32,16,128]{2,1,0:T(8,128)(2,1)S(1)}, u32[]{:S(2)}, u32[]{:S(2)}) async-start(bf16[32,16,128]{2,1,0:T(8,128)(2,1)} %get-tuple-element.24), calls=%async_computation.2 | async-start | bytes 262144 | tf_op jit(solution)/shard_map/all_to_all | solution.py:343
  62.5 2.7 %collective-permute-start.5 = (bf16[512,256]{1,0:T(8,128)(2,1)S(1)}, bf16[512,256]{1,0:T(8,128)(2,1)}, u32[]{:S(2)}, u32[]{:S(2)}) collective-permute-start(bf16[512,256]{1,0:T(8,128)(2,1)S(1)} %collective-permute-done.3.refs_4_), channel_id=1, source_target_pairs={{0,7},{1,0},{2,1},{3,2},{4,3},{5,4},{6,5},{7,6},{8,15},{9,8},{10,9... | collective-permute-start | bytes 786440 | tf_op jit(solution)/shard_map/ppermute | solution.py:318
  65.2 1.3 %collective-permute-start.10 = (bf16[256,512]{1,0:T(8,128)(2,1)S(1)}, bf16[256,512]{1,0:T(8,128)(2,1)}, u32[]{:S(2)}, u32[]{:S(2)}) collective-permute-start(bf16[256,512]{1,0:T(8,128)(2,1)S(1)} %collective-permute-done.9.refs_10_), channel_id=1, source_target_pairs={{0,192},{64,0},{128,64},{192,128},{1,193},{65,1},{129,65},{193,129... | collective-permute-start | bytes 786440 | tf_op jit(solution)/shard_map/ppermute | solution.py:318
  67.2 3.5 %all-to-all-done.2.low_ref = bf16[32,16,128]{2,1,0:T(8,128)(2,1)S(1)} async-done(((bf16[32,16,128]{2,1,0:T(8,128)(2,1)}), bf16[32,16,128]{2,1,0:T(8,128)(2,1)S(1)}, u32[]{:S(2)}, u32[]{:S(2)}) %all-to-all-start.2) | async-done | bytes 131104 | tf_op jit(solution)/shard_map/all_to_all | solution.py:343
  70.7 4.7 %shard_map.76 = (bf16[8,128,256]{2,1,0:T(8,128)(2,1)}, f32[8,128]{1,0:T(8,128)S(1)}) custom-call(bf16[32,16,128]{2,1,0:T(8,128)(2,1)S(1)} %all-to-all-done.2.low_ref, f32[8,1024]{1,0:T(8,128)S(1)} %get-tuple-element.25.slot_ref, bf16[4096,256]{1,0:T(8,128)(2,1)} %bitcast.7), custom_call_target="tpu_custom_call" | custom-call | flops 64424509440 | bytes 62914560 | tf_op jit(solution)/shard_map/pallas_call | solution.py:217
  75.5 2.1 %collective-permute-start.11 = (bf16[256,512]{1,0:T(8,128)(2,1)S(1)}, bf16[256,512]{1,0:T(8,128)(2,1)}, u32[]{:S(2)}, u32[]{:S(2)}) collective-permute-start(bf16[256,512]{1,0:T(8,128)(2,1)S(1)} %collective-permute-done.7.refs_8_), channel_id=1, source_target_pairs={{0,32},{32,0},{1,33},{33,1},{2,34},{34,2},{3,35},{35,3},{4,36},{36... | collective-permute-start | bytes 786440 | tf_op jit(solution)/shard_map/ppermute | solution.py:318
  78.2 3.7 %shard_map.77 = (bf16[256,256]{1,0:T(8,128)(2,1)}, bf16[256,256]{1,0:T(8,128)(2,1)}, bf16[512,256]{1,0:T(8,128)(2,1)}, f32[8,128]{1,0:T(8,128)S(1)}) custom-call(bf16[512,256]{1,0:T(8,128)(2,1)S(1)} %copy-done.1, bf16[512,256]{1,0:T(8,128)(2,1)S(1)} %collective-permute-done.refs_1_, bf16[512,256]{1,0:T(8,128)(2,1)S(1)} %collective-permute-done.1.refs_2_, ...), custom_call_target="tpu_custom_call" | custom-call | flops 4294967296 | bytes 16777216 | tf_op jit(solution)/shard_map/pallas_call | solution.py:274
  82.9 4.5 %all-to-all-start.3 = ((bf16[8,128,256]{2,1,0:T(8,128)(2,1)}), bf16[8,128,256]{2,1,0:T(8,128)(2,1)S(1)}, u32[]{:S(2)}, u32[]{:S(2)}) async-start(bf16[8,128,256]{2,1,0:T(8,128)(2,1)} %get-tuple-element.34), calls=%async_computation.3 | async-start | bytes 1048576 | tf_op jit(solution)/shard_map/all_to_all | solution.py:353
  87.5 3.0 %shard_map.78 = (bf16[512,256]{1,0:T(8,128)(2,1)S(1)}, bf16[512,256]{1,0:T(8,128)(2,1)S(1)}, f32[8,128]{1,0:T(8,128)}) custom-call(bf16[512,256]{1,0:T(8,128)(2,1)S(1)} %copy-done.1, bf16[512,256]{1,0:T(8,128)(2,1)S(1)} %collective-permute-done.refs_1_, bf16[512,256]{1,0:T(8,128)(2,1)S(1)} %collective-permute-done.1.refs_2_, ...), custom_call_target="tpu_custom_call" | custom-call | flops 4294967296 | bytes 16777216 | tf_op jit(solution)/shard_map/pallas_call | solution.py:274
  93.0 1.7 %collective-permute-start.27 = (bf16[256,256]{1,0:T(8,128)(2,1)S(1)}, bf16[256,256]{1,0:T(8,128)(2,1)S(1)}, u32[]{:S(2)}, u32[]{:S(2)}) collective-permute-start(bf16[256,256]{1,0:T(8,128)(2,1)S(1)} %collective-permute-done.26), channel_id=1, source_target_pairs={{0,24},{8,0},{16,8},{24,16},{1,25},{9,1},{17,9},{25,17},{2,26},{10... | collective-permute-start | bytes 393224 | tf_op jit(solution)/shard_map/ppermute | solution.py:318
  94.8 7.1 %collective-permute-done.25.refs_3_ = bf16[256,256]{1,0:T(8,128)(2,1)S(1)} collective-permute-done((bf16[256,256]{1,0:T(8,128)(2,1)S(1)}, bf16[256,256]{1,0:T(8,128)(2,1)S(1)}, u32[]{:S(2)}, u32[]{:S(2)}) %collective-permute-start.25) | collective-permute-done | bytes 131104 | tf_op jit(solution)/shard_map/ppermute | solution.py:318
  101.8 2.4 %collective-permute-done.27.refs_4_ = bf16[256,256]{1,0:T(8,128)(2,1)S(1)} collective-permute-done((bf16[256,256]{1,0:T(8,128)(2,1)S(1)}, bf16[256,256]{1,0:T(8,128)(2,1)S(1)}, u32[]{:S(2)}, u32[]{:S(2)}) %collective-permute-start.27) | collective-permute-done | bytes 131104 | tf_op jit(solution)/shard_map/ppermute | solution.py:318
  (55 shorter events, 13.0 us)
Async XLA Ops:
  3.7 19.3 %all-to-all-start = ((bf16[8,144,256]{2,1,0:T(8,128)(2,1)}), bf16[8,144,256]{2,1,0:T(8,128)(2,1)S(1)}, u32[]{:S(2)}, u32[]{:S(2)}) async-start(bf16[8,144,256]{2,1,0:T(8,128)(2,1)} %get-tuple-element.22), calls=%async_computation | async-start | bytes 1179648 | tf_op jit(solution)/shard_map/all_to_all | solution.py:335
  10.4 27.9 %collective-permute-start = (bf16[512,256]{1,0:T(8,128)(2,1)S(1)}, bf16[512,256]{1,0:T(8,128)(2,1)S(1)}, u32[]{:S(2)}, u32[]{:S(2)}) collective-permute-start(bf16[512,256]{1,0:T(8,128)(2,1)S(1)} %copy-done.1), channel_id=1, source_target_pairs={{0,1},{1,2},{2,3},{3,4},{4,5},{5,6},{6,7},{7,0},{8,9},{9,10},{10,1... | collective-permute-start | bytes 786440 | tf_op jit(solution)/shard_map/ppermute | solution.py:318
  11.2 30.3 %collective-permute-start.1 = (bf16[512,256]{1,0:T(8,128)(2,1)S(1)}, bf16[512,256]{1,0:T(8,128)(2,1)S(1)}, u32[]{:S(2)}, u32[]{:S(2)}) collective-permute-start(bf16[512,256]{1,0:T(8,128)(2,1)S(1)} %copy-done.1), channel_id=1, source_target_pairs={{0,7},{1,0},{2,1},{3,2},{4,3},{5,4},{6,5},{7,6},{8,15},{9,8},{10,9... | collective-permute-start | bytes 786440 | tf_op jit(solution)/shard_map/ppermute | solution.py:318
  15.2 20.4 %collective-permute-start.15 = (bf16[256,512]{1,0:T(8,128)(2,1)S(1)}, bf16[256,512]{1,0:T(8,128)(2,1)S(1)}, u32[]{:S(2)}, u32[]{:S(2)}) collective-permute-start(bf16[256,512]{1,0:T(8,128)(2,1)S(1)} %get-tuple-element.21), channel_id=1, source_target_pairs={{0,0},{1,1},{2,2},{3,3},{4,4},{5,5},{6,6},{7,7},{32,36},{33,37},{3... | collective-permute-start | bytes 786440 | tf_op jit(solution)/shard_map/ppermute | solution.py:326
  21.0 20.7 %collective-permute-start.7 = (bf16[256,512]{1,0:T(8,128)(2,1)S(1)}, bf16[256,512]{1,0:T(8,128)(2,1)S(1)}, u32[]{:S(2)}, u32[]{:S(2)}) collective-permute-start(bf16[256,512]{1,0:T(8,128)(2,1)S(1)} %get-tuple-element.20), channel_id=1, source_target_pairs={{0,1},{1,2},{2,3},{3,4},{4,5},{5,6},{6,7},{7,0},{32,37},{33,38},{3... | collective-permute-start | bytes 786440 | tf_op jit(solution)/shard_map/ppermute | solution.py:326
  27.5 25.1 %all-to-all-start.1 = ((f32[32,16,128]{2,1,0:T(8,128)}), f32[32,16,128]{2,1,0:T(8,128)S(1)}, u32[]{:S(2)}, u32[]{:S(2)}) async-start(f32[32,16,128]{2,1,0:T(8,128)} %get-tuple-element.23), calls=%async_computation.1 | async-start | bytes 524288 | tf_op jit(solution)/shard_map/all_to_all | solution.py:341
  38.3 11.9 %collective-permute-start.2 = (bf16[512,256]{1,0:T(8,128)(2,1)S(1)}, bf16[512,256]{1,0:T(8,128)(2,1)S(1)}, u32[]{:S(2)}, u32[]{:S(2)}) collective-permute-start(bf16[512,256]{1,0:T(8,128)(2,1)S(1)} %collective-permute-done.refs_1_), channel_id=1, source_target_pairs={{0,1},{1,2},{2,3},{3,4},{4,5},{5,6},{6,7},{7,0},{8,9},{9,10},{10,1... | collective-permute-start | bytes 786440 | tf_op jit(solution)/shard_map/ppermute | solution.py:318
  43.6 18.0 %collective-permute-start.9 = (bf16[256,512]{1,0:T(8,128)(2,1)S(1)}, bf16[256,512]{1,0:T(8,128)(2,1)S(1)}, u32[]{:S(2)}, u32[]{:S(2)}) collective-permute-start(bf16[256,512]{1,0:T(8,128)(2,1)S(1)} %collective-permute-done.7.refs_8_), channel_id=1, source_target_pairs={{0,192},{64,0},{128,64},{192,128},{1,193},{65,1},{129,65},{193,129... | collective-permute-start | bytes 786440 | tf_op jit(solution)/shard_map/ppermute | solution.py:318
  44.5 18.0 %collective-permute-start.8 = (bf16[256,512]{1,0:T(8,128)(2,1)S(1)}, bf16[256,512]{1,0:T(8,128)(2,1)S(1)}, u32[]{:S(2)}, u32[]{:S(2)}) collective-permute-start(bf16[256,512]{1,0:T(8,128)(2,1)S(1)} %collective-permute-done.7.refs_8_), channel_id=1, source_target_pairs={{0,64},{64,128},{128,192},{192,0},{1,65},{65,129},{129,193},{193,1... | collective-permute-start | bytes 786440 | tf_op jit(solution)/shard_map/ppermute | solution.py:318
  50.2 15.0 %collective-permute-start.18 = (bf16[256,512]{1,0:T(8,128)(2,1)S(1)}, bf16[256,512]{1,0:T(8,128)(2,1)}, u32[]{:S(2)}, u32[]{:S(2)}) collective-permute-start(bf16[256,512]{1,0:T(8,128)(2,1)S(1)} %collective-permute-done.16.refs_9_), channel_id=1, source_target_pairs={{0,64},{64,128},{128,192},{192,0},{1,65},{65,129},{129,193},{193,1... | collective-permute-start | bytes 786440 | tf_op jit(solution)/shard_map/ppermute | solution.py:318
  51.6 15.0 %collective-permute-start.20 = (bf16[256,512]{1,0:T(8,128)(2,1)S(1)}, bf16[256,512]{1,0:T(8,128)(2,1)}, u32[]{:S(2)}, u32[]{:S(2)}) collective-permute-start(bf16[256,512]{1,0:T(8,128)(2,1)S(1)} %collective-permute-done.16.refs_9_), channel_id=1, source_target_pairs={{0,32},{32,0},{1,33},{33,1},{2,34},{34,2},{3,35},{35,3},{4,36},{36... | collective-permute-start | bytes 786440 | tf_op jit(solution)/shard_map/ppermute | solution.py:318
  52.6 14.6 %collective-permute-start.4 = (bf16[512,256]{1,0:T(8,128)(2,1)S(1)}, bf16[512,256]{1,0:T(8,128)(2,1)}, u32[]{:S(2)}, u32[]{:S(2)}) collective-permute-start(bf16[512,256]{1,0:T(8,128)(2,1)S(1)} %collective-permute-done.2.refs_3_), channel_id=1, source_target_pairs={{0,1},{1,2},{2,3},{3,4},{4,5},{5,6},{6,7},{7,0},{8,9},{9,10},{10,1... | collective-permute-start | bytes 786440 | tf_op jit(solution)/shard_map/ppermute | solution.py:318
  53.3 17.4 %all-to-all-start.2 = ((bf16[32,16,128]{2,1,0:T(8,128)(2,1)}), bf16[32,16,128]{2,1,0:T(8,128)(2,1)S(1)}, u32[]{:S(2)}, u32[]{:S(2)}) async-start(bf16[32,16,128]{2,1,0:T(8,128)(2,1)} %get-tuple-element.24), calls=%async_computation.2 | async-start | bytes 262144 | tf_op jit(solution)/shard_map/all_to_all | solution.py:343
  61.6 13.9 %collective-permute-start.21 = (bf16[256,512]{1,0:T(8,128)(2,1)S(1)}, bf16[256,512]{1,0:T(8,128)(2,1)}, u32[]{:S(2)}, u32[]{:S(2)}) collective-permute-start(bf16[256,512]{1,0:T(8,128)(2,1)S(1)} %collective-permute-done.17.refs_10_), channel_id=1, source_target_pairs={{0,32},{32,0},{1,33},{33,1},{2,34},{34,2},{3,35},{35,3},{4,36},{36... | collective-permute-start | bytes 786440 | tf_op jit(solution)/shard_map/ppermute | solution.py:318
  62.5 15.0 %collective-permute-start.5 = (bf16[512,256]{1,0:T(8,128)(2,1)S(1)}, bf16[512,256]{1,0:T(8,128)(2,1)}, u32[]{:S(2)}, u32[]{:S(2)}) collective-permute-start(bf16[512,256]{1,0:T(8,128)(2,1)S(1)} %collective-permute-done.3.refs_4_), channel_id=1, source_target_pairs={{0,7},{1,0},{2,1},{3,2},{4,3},{5,4},{6,5},{7,6},{8,15},{9,8},{10,9... | collective-permute-start | bytes 786440 | tf_op jit(solution)/shard_map/ppermute | solution.py:318
  65.2 12.4 %collective-permute-start.10 = (bf16[256,512]{1,0:T(8,128)(2,1)S(1)}, bf16[256,512]{1,0:T(8,128)(2,1)}, u32[]{:S(2)}, u32[]{:S(2)}) collective-permute-start(bf16[256,512]{1,0:T(8,128)(2,1)S(1)} %collective-permute-done.9.refs_10_), channel_id=1, source_target_pairs={{0,192},{64,0},{128,64},{192,128},{1,193},{65,1},{129,65},{193,129... | collective-permute-start | bytes 786440 | tf_op jit(solution)/shard_map/ppermute | solution.py:318
  66.6 11.5 %collective-permute-start.22 = (bf16[256,512]{1,0:T(8,128)(2,1)}, bf16[256,512]{1,0:T(8,128)(2,1)}, u32[]{:S(2)}, u32[]{:S(2)}) collective-permute-start(bf16[256,512]{1,0:T(8,128)(2,1)} %collective-permute-done.18.refs_11_), channel_id=1, source_target_pairs={{0,32},{32,0},{1,33},{33,1},{2,34},{34,2},{3,35},{35,3},{4,36},{36... | collective-permute-start | bytes 786440 | tf_op jit(solution)/shard_map/ppermute | solution.py:318
  67.2 11.0 %collective-permute-start.6 = (bf16[512,256]{1,0:T(8,128)(2,1)}, bf16[512,256]{1,0:T(8,128)(2,1)}, u32[]{:S(2)}, u32[]{:S(2)}) collective-permute-start(bf16[512,256]{1,0:T(8,128)(2,1)} %collective-permute-done.4.refs_5_), channel_id=1, source_target_pairs={{0,1},{1,2},{2,3},{3,4},{4,5},{5,6},{6,7},{7,0},{8,9},{9,10},{10,1... | collective-permute-start | bytes 786440 | tf_op jit(solution)/shard_map/ppermute | solution.py:318
  75.5 11.9 %collective-permute-start.11 = (bf16[256,512]{1,0:T(8,128)(2,1)S(1)}, bf16[256,512]{1,0:T(8,128)(2,1)}, u32[]{:S(2)}, u32[]{:S(2)}) collective-permute-start(bf16[256,512]{1,0:T(8,128)(2,1)S(1)} %collective-permute-done.7.refs_8_), channel_id=1, source_target_pairs={{0,32},{32,0},{1,33},{33,1},{2,34},{34,2},{3,35},{35,3},{4,36},{36... | collective-permute-start | bytes 786440 | tf_op jit(solution)/shard_map/ppermute | solution.py:318
  81.9 11.2 %collective-permute-start.26 = (bf16[256,256]{1,0:T(8,128)(2,1)}, bf16[256,256]{1,0:T(8,128)(2,1)S(1)}, u32[]{:S(2)}, u32[]{:S(2)}) collective-permute-start(bf16[256,256]{1,0:T(8,128)(2,1)} %get-tuple-element.32), channel_id=1, source_target_pairs={{0,24},{8,0},{16,8},{24,16},{1,25},{9,1},{17,9},{25,17},{2,26},{10... | collective-permute-start | bytes 393224 | tf_op jit(solution)/shard_map/ppermute | solution.py:318
  82.9 21.4 %all-to-all-start.3 = ((bf16[8,128,256]{2,1,0:T(8,128)(2,1)}), bf16[8,128,256]{2,1,0:T(8,128)(2,1)S(1)}, u32[]{:S(2)}, u32[]{:S(2)}) async-start(bf16[8,128,256]{2,1,0:T(8,128)(2,1)} %get-tuple-element.34), calls=%async_computation.3 | async-start | bytes 1048576 | tf_op jit(solution)/shard_map/all_to_all | solution.py:353
  90.5 13.7 %collective-permute-start.24 = (bf16[512,256]{1,0:T(8,128)(2,1)S(1)}, bf16[512,256]{1,0:T(8,128)(2,1)S(1)}, u32[]{:S(2)}, u32[]{:S(2)}) collective-permute-start(bf16[512,256]{1,0:T(8,128)(2,1)S(1)} %get-tuple-element.30), channel_id=1, source_target_pairs={{0,24},{8,0},{16,8},{24,16},{1,25},{9,1},{17,9},{25,17},{2,26},{10... | collective-permute-start | bytes 786440 | tf_op jit(solution)/shard_map/ppermute | solution.py:318
  91.3 12.9 %collective-permute-start.23 = (bf16[512,256]{1,0:T(8,128)(2,1)S(1)}, bf16[512,256]{1,0:T(8,128)(2,1)S(1)}, u32[]{:S(2)}, u32[]{:S(2)}) collective-permute-start(bf16[512,256]{1,0:T(8,128)(2,1)S(1)} %copy-done.2), channel_id=1, source_target_pairs={{0,8},{8,16},{16,24},{24,0},{1,9},{9,17},{17,25},{25,1},{2,10},{10... | collective-permute-start | bytes 786440 | tf_op jit(solution)/shard_map/ppermute | solution.py:318
  93.0 11.2 %collective-permute-start.27 = (bf16[256,256]{1,0:T(8,128)(2,1)S(1)}, bf16[256,256]{1,0:T(8,128)(2,1)S(1)}, u32[]{:S(2)}, u32[]{:S(2)}) collective-permute-start(bf16[256,256]{1,0:T(8,128)(2,1)S(1)} %collective-permute-done.26), channel_id=1, source_target_pairs={{0,24},{8,0},{16,8},{24,16},{1,25},{9,1},{17,9},{25,17},{2,26},{10... | collective-permute-start | bytes 393224 | tf_op jit(solution)/shard_map/ppermute | solution.py:318
  (12 other events, 110.8 us)

commit v5 on v4

--- a/solution.py
+++ b/solution.py
@@ -144,7 +144,7 @@
                 for i in range(RANK // 16):
                     low_ref[(2 * b + g) * (RANK // 16) + i] = total[
                         16 * i : 16 * (i + 1), g * CAP : (g + 1) * CAP
-                    ]
+                    ].astype(BF16)
 
 
 def down(got, maps, *deps):
@@ -152,7 +152,7 @@
     return pl.pallas_call(
         down_body,
         out_shape=(
-            pltpu.HBM((NY * NZ, 16, CAP), F32),
+            pltpu.HBM((NY * NZ, 16, CAP), BF16),
             jax.ShapeDtypeStruct((8, rows), F32),
         ),
         in_specs=[LOCAL, REMOTE] + [ANY] * len(deps),
@@ -169,8 +169,8 @@
 
 def total_body(parts_ref, *refs):
     o_ref, token_ref = refs[-2:]
-    token_ref[...] = parts_ref[0, :8, :]
-    whole = jnp.sum(parts_ref[...], axis=0).astype(BF16)
+    token_ref[...] = parts_ref[0].astype(F32)[:8, :]
+    whole = jnp.sum(parts_ref[...].astype(F32), axis=0).astype(BF16)
     o_ref[...] = jnp.broadcast_to(whole[None], o_ref.shape)
 
 

time: 106 us -> 115 us (1.085)
  local copies, waits for them, and re-layouts: 0.02 us -> 3.6 us
  starting transfers between devices: 64.3 us -> 67.7 us
  waiting for transfers between devices: 19.3 us -> 21.8 us
    ppermute x2, waiting for transfers between devices: 0.01 us -> 7 us  [pass_on(): return lax.ppermute(a, ('x', 'c', 'z'), pairs)]
    ppermute x26, waiting for transfers between devices: 15.8 us -> 9.24 us  [shift(): return lax.ppermute(a, axis, [(i, (i + by) % size) for i in range(size)])]
    unnamed x8 -> x28, local copies, waits for them, and re-layouts: 0.02 us -> 3.6 us
    all_to_all x1, waiting for transfers between devices: 0.01 us -> 2.59 us  [on_device(): low_part = lax.all_to_all(low_part, ('y', 'z'), 0, 0, tiled=True)]
    all_to_all x1, starting transfers between devices: 8.24 us -> 5.69 us  [on_device(): low = lax.all_to_all(low_all, ('y', 'z'), 0, 0, tiled=True)]
    all_to_all x1, starting transfers between devices: 4.53 us -> 6.73 us  [on_device(): back = lax.all_to_all(delta, ('x', 'c'), 0, 0, tiled=True)]
    ppermute x2, starting transfers between devices: 7.74 us -> 9.83 us  [pass_on(): return lax.ppermute(a, ('x', 'c', 'z'), pairs)]
    all_to_all x1, starting transfers between devices: 8.03 us -> 9.35 us  [on_device(): low_part = lax.all_to_all(low_part, ('y', 'z'), 0, 0, tiled=True)]
  transfers between devices with their start and end apart: 32 -> 32, of which waited for: 6 -> 7; matrix products, arithmetic and copies ran while one was open for 0% -> 0% of each run, Pallas kernels for 16% -> 14%
where the time goes in v5:
time: 115 us
  starting transfers between devices  67.7 us (59%)
  waiting for transfers between devices  21.8 us (19%)
  Pallas kernels  21.2 us (18%)
  local copies, waits for them, and re-layouts  3.6 us (3%)
    ppermute x26, starting transfers between devices, shift(): return lax.ppermute(a, axis, [(i, (i + by) % size) for i in range(size)])  29.4 us
    ppermute x2, starting transfers between devices, pass_on(): return lax.ppermute(a, ('x', 'c', 'z'), pairs)  9.83 us
    all_to_all x1, starting transfers between devices, on_device(): low_part = lax.all_to_all(low_part, ('y', 'z'), 0, 0, tiled=True)  9.35 us
    ppermute x26, waiting for transfers between devices, shift(): return lax.ppermute(a, axis, [(i, (i + by) % size) for i in range(size)])  9.24 us
    ppermute x2, waiting for transfers between devices, pass_on(): return lax.ppermute(a, ('x', 'c', 'z'), pairs)  7 us
    all_to_all x1, starting transfers between devices, on_device(): back = lax.all_to_all(delta, ('x', 'c'), 0, 0, tiled=True)  6.73 us
    all_to_all x1, starting transfers between devices, on_device(): got = lax.all_to_all(send, ('x', 'c'), 0, 0, tiled=True)  6.69 us
    pallas_call x2, Pallas kernels, base_product(): pl.pallas_call(body, out_shape=[*outs, jax.ShapeDtypeStruct((8, 128), F32...  6.36 us
  transfers between devices with their start and end apart: 32, of which 7 were waited for; matrix products, arithmetic and copies ran while one was open for 0% of the time, Pallas kernels for 14%

profile of v5, /device:TPU:1, one launch (start us, length us, event | category | flops | bytes accessed | tf_op | source)
XLA Modules:
  0.0 114.6 jit_solution(17249590389067858365)
XLA Ops:
  0.0 3.7 %shard_map.73 = (bf16[256,512]{1,0:T(8,128)(2,1)S(1)}, bf16[256,512]{1,0:T(8,128)(2,1)S(1)}, bf16[8,144,256]{2,1,0:T(8,128)(2,1)}, f32[8,512]{1,0:T(8,128)S(1)}) custom-call(s32[1,512]{1,0:T(1,128)} %bitcast.8, s32[1,512]{1,0:T(1,128)} %bitcast.9, bf16[512,256]{1,0:T(8,128)(2,1)} %refs_0_.3, bf16[256,8192]{1,0:T(8,128)(2,1)} %w_ref.1), custom_call_target="tpu_custom_call" | custom-call | flops 2147483648 | bytes 9437184 | tf_op jit(solution)/shard_map/pallas_call | solution.py:91
  3.7 6.7 %all-to-all-start = ((bf16[8,144,256]{2,1,0:T(8,128)(2,1)}), bf16[8,144,256]{2,1,0:T(8,128)(2,1)S(1)}, u32[]{:S(2)}, u32[]{:S(2)}) async-start(bf16[8,144,256]{2,1,0:T(8,128)(2,1)} %get-tuple-element.22), calls=%async_computation | async-start | bytes 1179648 | tf_op jit(solution)/shard_map/all_to_all | solution.py:335
  10.4 7.9 %collective-permute-start.15 = (bf16[256,512]{1,0:T(8,128)(2,1)S(1)}, bf16[256,512]{1,0:T(8,128)(2,1)S(1)}, u32[]{:S(2)}, u32[]{:S(2)}) collective-permute-start(bf16[256,512]{1,0:T(8,128)(2,1)S(1)} %get-tuple-element.21), channel_id=1, source_target_pairs={{0,0},{1,1},{2,2},{3,3},{4,4},{5,5},{6,6},{7,7},{32,36},{33,37},{3... | collective-permute-start | bytes 786440 | tf_op jit(solution)/shard_map/ppermute | solution.py:326
  19.2 1.9 %collective-permute-start.1 = (bf16[512,256]{1,0:T(8,128)(2,1)S(1)}, bf16[512,256]{1,0:T(8,128)(2,1)S(1)}, u32[]{:S(2)}, u32[]{:S(2)}) collective-permute-start(bf16[512,256]{1,0:T(8,128)(2,1)S(1)} %copy-done.1), channel_id=1, source_target_pairs={{0,7},{1,0},{2,1},{3,2},{4,3},{5,4},{6,5},{7,6},{8,15},{9,8},{10,9... | collective-permute-start | bytes 786440 | tf_op jit(solution)/shard_map/ppermute | solution.py:318
  21.1 1.9 %collective-permute-start.7 = (bf16[256,512]{1,0:T(8,128)(2,1)S(1)}, bf16[256,512]{1,0:T(8,128)(2,1)S(1)}, u32[]{:S(2)}, u32[]{:S(2)}) collective-permute-start(bf16[256,512]{1,0:T(8,128)(2,1)S(1)} %get-tuple-element.20), channel_id=1, source_target_pairs={{0,1},{1,2},{2,3},{3,4},{4,5},{5,6},{6,7},{7,0},{32,37},{33,38},{3... | collective-permute-start | bytes 786440 | tf_op jit(solution)/shard_map/ppermute | solution.py:326
  23.0 3.9 %collective-permute-done.15.refs_8_ = bf16[256,512]{1,0:T(8,128)(2,1)S(1)} collective-permute-done((bf16[256,512]{1,0:T(8,128)(2,1)S(1)}, bf16[256,512]{1,0:T(8,128)(2,1)S(1)}, u32[]{:S(2)}, u32[]{:S(2)}) %collective-permute-start.15) | collective-permute-done | bytes 262176 | tf_op jit(solution)/shard_map/ppermute | solution.py:326
  26.9 3.9 %collective-permute-start.16 = (bf16[256,512]{1,0:T(8,128)(2,1)S(1)}, bf16[256,512]{1,0:T(8,128)(2,1)S(1)}, u32[]{:S(2)}, u32[]{:S(2)}) collective-permute-start(bf16[256,512]{1,0:T(8,128)(2,1)S(1)} %collective-permute-done.15.refs_8_), channel_id=1, source_target_pairs={{0,64},{64,128},{128,192},{192,0},{1,65},{65,129},{129,193},{193,1... | collective-permute-start | bytes 786440 | tf_op jit(solution)/shard_map/ppermute | solution.py:318
  31.2 3.2 %collective-permute-start.2 = (bf16[512,256]{1,0:T(8,128)(2,1)S(1)}, bf16[512,256]{1,0:T(8,128)(2,1)S(1)}, u32[]{:S(2)}, u32[]{:S(2)}) collective-permute-start(bf16[512,256]{1,0:T(8,128)(2,1)S(1)} %collective-permute-done.refs_1_), channel_id=1, source_target_pairs={{0,1},{1,2},{2,3},{3,4},{4,5},{5,6},{6,7},{7,0},{8,9},{9,10},{10,1... | collective-permute-start | bytes 786440 | tf_op jit(solution)/shard_map/ppermute | solution.py:318
  34.4 3.1 %collective-permute-done.7.refs_8_ = bf16[256,512]{1,0:T(8,128)(2,1)S(1)} collective-permute-done((bf16[256,512]{1,0:T(8,128)(2,1)S(1)}, bf16[256,512]{1,0:T(8,128)(2,1)S(1)}, u32[]{:S(2)}, u32[]{:S(2)}) %collective-permute-start.7) | collective-permute-done | bytes 262176 | tf_op jit(solution)/shard_map/ppermute | solution.py:326
  37.6 4.5 %shard_map.74 = (bf16[32,16,128]{2,1,0:T(8,128)(2,1)}, f32[8,1024]{1,0:T(8,128)S(1)}) custom-call(bf16[8,144,256]{2,1,0:T(8,128)(2,1)S(1)} %all-to-all-done.got_ref, bf16[4096,256]{1,0:T(8,128)(2,1)} %bitcast.6), custom_call_target="tpu_custom_call" | custom-call | flops 64424509440 | bytes 62914560 | tf_op jit(solution)/shard_map/pallas_call | solution.py:152
  42.7 9.3 %all-to-all-start.1 = ((bf16[32,16,128]{2,1,0:T(8,128)(2,1)}), bf16[32,16,128]{2,1,0:T(8,128)(2,1)S(1)}, u32[]{:S(2)}, u32[]{:S(2)}) async-start(bf16[32,16,128]{2,1,0:T(8,128)(2,1)} %get-tuple-element.23), calls=%async_computation.1 | async-start | bytes 262144 | tf_op jit(solution)/shard_map/all_to_all | solution.py:341
  52.2 3.3 %collective-permute-start.8 = (bf16[256,512]{1,0:T(8,128)(2,1)S(1)}, bf16[256,512]{1,0:T(8,128)(2,1)S(1)}, u32[]{:S(2)}, u32[]{:S(2)}) collective-permute-start(bf16[256,512]{1,0:T(8,128)(2,1)S(1)} %collective-permute-done.7.refs_8_), channel_id=1, source_target_pairs={{0,64},{64,128},{128,192},{192,0},{1,65},{65,129},{129,193},{193,1... | collective-permute-start | bytes 786440 | tf_op jit(solution)/shard_map/ppermute | solution.py:318
  58.7 2.6 %all-to-all-done.1.parts_ref = bf16[32,16,128]{2,1,0:T(8,128)(2,1)S(1)} async-done(((bf16[32,16,128]{2,1,0:T(8,128)(2,1)}), bf16[32,16,128]{2,1,0:T(8,128)(2,1)S(1)}, u32[]{:S(2)}, u32[]{:S(2)}) %all-to-all-start.1) | async-done | bytes 131104 | tf_op jit(solution)/shard_map/all_to_all | solution.py:341
  62.0 5.7 %all-to-all-start.2 = ((bf16[32,16,128]{2,1,0:T(8,128)(2,1)}), bf16[32,16,128]{2,1,0:T(8,128)(2,1)S(1)}, u32[]{:S(2)}, u32[]{:S(2)}) async-start(bf16[32,16,128]{2,1,0:T(8,128)(2,1)} %get-tuple-element.24), calls=%async_computation.2 | async-start | bytes 262144 | tf_op jit(solution)/shard_map/all_to_all | solution.py:343
  68.7 2.7 %collective-permute-start.5 = (bf16[512,256]{1,0:T(8,128)(2,1)S(1)}, bf16[512,256]{1,0:T(8,128)(2,1)}, u32[]{:S(2)}, u32[]{:S(2)}) collective-permute-start(bf16[512,256]{1,0:T(8,128)(2,1)S(1)} %collective-permute-done.3.refs_4_), channel_id=1, source_target_pairs={{0,7},{1,0},{2,1},{3,2},{4,3},{5,4},{6,5},{7,6},{8,15},{9,8},{10,9... | collective-permute-start | bytes 786440 | tf_op jit(solution)/shard_map/ppermute | solution.py:318
  71.4 1.9 %collective-permute-start.10 = (bf16[256,512]{1,0:T(8,128)(2,1)S(1)}, bf16[256,512]{1,0:T(8,128)(2,1)}, u32[]{:S(2)}, u32[]{:S(2)}) collective-permute-start(bf16[256,512]{1,0:T(8,128)(2,1)S(1)} %collective-permute-done.9.refs_10_), channel_id=1, source_target_pairs={{0,192},{64,0},{128,64},{192,128},{1,193},{65,1},{129,65},{193,129... | collective-permute-start | bytes 786440 | tf_op jit(solution)/shard_map/ppermute | solution.py:318
  73.9 2.9 %all-to-all-done.2.low_ref = bf16[32,16,128]{2,1,0:T(8,128)(2,1)S(1)} async-done(((bf16[32,16,128]{2,1,0:T(8,128)(2,1)}), bf16[32,16,128]{2,1,0:T(8,128)(2,1)S(1)}, u32[]{:S(2)}, u32[]{:S(2)}) %all-to-all-start.2) | async-done | bytes 131104 | tf_op jit(solution)/shard_map/all_to_all | solution.py:343
  77.7 4.7 %shard_map.76 = (bf16[8,128,256]{2,1,0:T(8,128)(2,1)}, f32[8,128]{1,0:T(8,128)S(1)}) custom-call(bf16[32,16,128]{2,1,0:T(8,128)(2,1)S(1)} %all-to-all-done.2.low_ref, f32[8,1024]{1,0:T(8,128)S(1)} %copy-done.11, bf16[4096,256]{1,0:T(8,128)(2,1)} %bitcast.7), custom_call_target="tpu_custom_call" | custom-call | flops 64424509440 | bytes 62914560 | tf_op jit(solution)/shard_map/pallas_call | solution.py:217
  83.0 6.7 %all-to-all-start.3 = ((bf16[8,128,256]{2,1,0:T(8,128)(2,1)}), bf16[8,128,256]{2,1,0:T(8,128)(2,1)S(1)}, u32[]{:S(2)}, u32[]{:S(2)}) async-start(bf16[8,128,256]{2,1,0:T(8,128)(2,1)} %get-tuple-element.34), calls=%async_computation.3 | async-start | bytes 1048576 | tf_op jit(solution)/shard_map/all_to_all | solution.py:353
  92.4 3.6 %shard_map.77 = (bf16[256,256]{1,0:T(8,128)(2,1)}, bf16[256,256]{1,0:T(8,128)(2,1)}, bf16[512,256]{1,0:T(8,128)(2,1)}, f32[8,128]{1,0:T(8,128)S(1)}) custom-call(bf16[512,256]{1,0:T(8,128)(2,1)S(1)} %copy-done.1, bf16[512,256]{1,0:T(8,128)(2,1)S(1)} %collective-permute-done.refs_1_, bf16[512,256]{1,0:T(8,128)(2,1)S(1)} %collective-permute-done.1.refs_2_, ...), custom_call_target="tpu_custom_call" | custom-call | flops 4294967296 | bytes 16777216 | tf_op jit(solution)/shard_map/pallas_call | solution.py:274
  97.1 2.7 %shard_map.78 = (bf16[512,256]{1,0:T(8,128)(2,1)S(1)}, bf16[512,256]{1,0:T(8,128)(2,1)S(1)}, f32[8,128]{1,0:T(8,128)}) custom-call(bf16[512,256]{1,0:T(8,128)(2,1)S(1)} %copy-done.1, bf16[512,256]{1,0:T(8,128)(2,1)S(1)} %collective-permute-done.refs_1_, bf16[512,256]{1,0:T(8,128)(2,1)S(1)} %collective-permute-done.1.refs_2_, ...), custom_call_target="tpu_custom_call" | custom-call | flops 4294967296 | bytes 16777216 | tf_op jit(solution)/shard_map/pallas_call | solution.py:274
  102.9 1.7 %collective-permute-start.27 = (bf16[256,256]{1,0:T(8,128)(2,1)S(1)}, bf16[256,256]{1,0:T(8,128)(2,1)S(1)}, u32[]{:S(2)}, u32[]{:S(2)}) collective-permute-start(bf16[256,256]{1,0:T(8,128)(2,1)S(1)} %collective-permute-done.26), channel_id=1, source_target_pairs={{0,24},{8,0},{16,8},{24,16},{1,25},{9,1},{17,9},{25,17},{2,26},{10... | collective-permute-start | bytes 393224 | tf_op jit(solution)/shard_map/ppermute | solution.py:318
  104.6 6.8 %collective-permute-done.25.refs_3_ = bf16[256,256]{1,0:T(8,128)(2,1)S(1)} collective-permute-done((bf16[256,256]{1,0:T(8,128)(2,1)S(1)}, bf16[256,256]{1,0:T(8,128)(2,1)S(1)}, u32[]{:S(2)}, u32[]{:S(2)}) %collective-permute-start.25) | collective-permute-done | bytes 131104 | tf_op jit(solution)/shard_map/ppermute | solution.py:318
  111.4 1.9 %collective-permute-done.27.refs_4_ = bf16[256,256]{1,0:T(8,128)(2,1)S(1)} collective-permute-done((bf16[256,256]{1,0:T(8,128)(2,1)S(1)}, bf16[256,256]{1,0:T(8,128)(2,1)S(1)}, u32[]{:S(2)}, u32[]{:S(2)}) %collective-permute-start.27) | collective-permute-done | bytes 131104 | tf_op jit(solution)/shard_map/ppermute | solution.py:318
  (75 shorter events, 16.7 us)
Async XLA Ops:
  3.7 33.9 %all-to-all-start = ((bf16[8,144,256]{2,1,0:T(8,128)(2,1)}), bf16[8,144,256]{2,1,0:T(8,128)(2,1)S(1)}, u32[]{:S(2)}, u32[]{:S(2)}) async-start(bf16[8,144,256]{2,1,0:T(8,128)(2,1)} %get-tuple-element.22), calls=%async_computation | async-start | bytes 1179648 | tf_op jit(solution)/shard_map/all_to_all | solution.py:335
  10.4 16.5 %collective-permute-start.15 = (bf16[256,512]{1,0:T(8,128)(2,1)S(1)}, bf16[256,512]{1,0:T(8,128)(2,1)S(1)}, u32[]{:S(2)}, u32[]{:S(2)}) collective-permute-start(bf16[256,512]{1,0:T(8,128)(2,1)S(1)} %get-tuple-element.21), channel_id=1, source_target_pairs={{0,0},{1,1},{2,2},{3,3},{4,4},{5,5},{6,6},{7,7},{32,36},{33,37},{3... | collective-permute-start | bytes 786440 | tf_op jit(solution)/shard_map/ppermute | solution.py:326
  18.4 12.9 %collective-permute-start = (bf16[512,256]{1,0:T(8,128)(2,1)S(1)}, bf16[512,256]{1,0:T(8,128)(2,1)S(1)}, u32[]{:S(2)}, u32[]{:S(2)}) collective-permute-start(bf16[512,256]{1,0:T(8,128)(2,1)S(1)} %copy-done.1), channel_id=1, source_target_pairs={{0,1},{1,2},{2,3},{3,4},{4,5},{5,6},{6,7},{7,0},{8,9},{9,10},{10,1... | collective-permute-start | bytes 786440 | tf_op jit(solution)/shard_map/ppermute | solution.py:318
  21.1 16.5 %collective-permute-start.7 = (bf16[256,512]{1,0:T(8,128)(2,1)S(1)}, bf16[256,512]{1,0:T(8,128)(2,1)S(1)}, u32[]{:S(2)}, u32[]{:S(2)}) collective-permute-start(bf16[256,512]{1,0:T(8,128)(2,1)S(1)} %get-tuple-element.20), channel_id=1, source_target_pairs={{0,1},{1,2},{2,3},{3,4},{4,5},{5,6},{6,7},{7,0},{32,37},{33,38},{3... | collective-permute-start | bytes 786440 | tf_op jit(solution)/shard_map/ppermute | solution.py:326
  26.9 25.2 %collective-permute-start.16 = (bf16[256,512]{1,0:T(8,128)(2,1)S(1)}, bf16[256,512]{1,0:T(8,128)(2,1)S(1)}, u32[]{:S(2)}, u32[]{:S(2)}) collective-permute-start(bf16[256,512]{1,0:T(8,128)(2,1)S(1)} %collective-permute-done.15.refs_8_), channel_id=1, source_target_pairs={{0,64},{64,128},{128,192},{192,0},{1,65},{65,129},{129,193},{193,1... | collective-permute-start | bytes 786440 | tf_op jit(solution)/shard_map/ppermute | solution.py:318
  30.8 21.4 %collective-permute-start.17 = (bf16[256,512]{1,0:T(8,128)(2,1)S(1)}, bf16[256,512]{1,0:T(8,128)(2,1)S(1)}, u32[]{:S(2)}, u32[]{:S(2)}) collective-permute-start(bf16[256,512]{1,0:T(8,128)(2,1)S(1)} %collective-permute-done.15.refs_8_), channel_id=1, source_target_pairs={{0,192},{64,0},{128,64},{192,128},{1,193},{65,1},{129,65},{193,129... | collective-permute-start | bytes 786440 | tf_op jit(solution)/shard_map/ppermute | solution.py:318
  31.2 25.7 %collective-permute-start.19 = (bf16[256,512]{1,0:T(8,128)(2,1)S(1)}, bf16[256,512]{1,0:T(8,128)(2,1)S(1)}, u32[]{:S(2)}, u32[]{:S(2)}) collective-permute-start(bf16[256,512]{1,0:T(8,128)(2,1)S(1)} %collective-permute-done.15.refs_8_), channel_id=1, source_target_pairs={{0,32},{32,0},{1,33},{33,1},{2,34},{34,2},{3,35},{35,3},{4,36},{36... | collective-permute-start | bytes 786440 | tf_op jit(solution)/shard_map/ppermute | solution.py:318
  31.2 24.3 %collective-permute-start.2 = (bf16[512,256]{1,0:T(8,128)(2,1)S(1)}, bf16[512,256]{1,0:T(8,128)(2,1)S(1)}, u32[]{:S(2)}, u32[]{:S(2)}) collective-permute-start(bf16[512,256]{1,0:T(8,128)(2,1)S(1)} %collective-permute-done.refs_1_), channel_id=1, source_target_pairs={{0,1},{1,2},{2,3},{3,4},{4,5},{5,6},{6,7},{7,0},{8,9},{9,10},{10,1... | collective-permute-start | bytes 786440 | tf_op jit(solution)/shard_map/ppermute | solution.py:318
  37.6 19.6 %collective-permute-start.3 = (bf16[512,256]{1,0:T(8,128)(2,1)S(1)}, bf16[512,256]{1,0:T(8,128)(2,1)S(1)}, u32[]{:S(2)}, u32[]{:S(2)}) collective-permute-start(bf16[512,256]{1,0:T(8,128)(2,1)S(1)} %collective-permute-done.1.refs_2_), channel_id=1, source_target_pairs={{0,7},{1,0},{2,1},{3,2},{4,3},{5,4},{6,5},{7,6},{8,15},{9,8},{10,9... | collective-permute-start | bytes 786440 | tf_op jit(solution)/shard_map/ppermute | solution.py:318
  42.7 18.6 %all-to-all-start.1 = ((bf16[32,16,128]{2,1,0:T(8,128)(2,1)}), bf16[32,16,128]{2,1,0:T(8,128)(2,1)S(1)}, u32[]{:S(2)}, u32[]{:S(2)}) async-start(bf16[32,16,128]{2,1,0:T(8,128)(2,1)} %get-tuple-element.23), calls=%async_computation.1 | async-start | bytes 262144 | tf_op jit(solution)/shard_map/all_to_all | solution.py:341
  52.1 15.7 %collective-permute-start.9 = (bf16[256,512]{1,0:T(8,128)(2,1)S(1)}, bf16[256,512]{1,0:T(8,128)(2,1)S(1)}, u32[]{:S(2)}, u32[]{:S(2)}) collective-permute-start(bf16[256,512]{1,0:T(8,128)(2,1)S(1)} %collective-permute-done.7.refs_8_), channel_id=1, source_target_pairs={{0,192},{64,0},{128,64},{192,128},{1,193},{65,1},{129,65},{193,129... | collective-permute-start | bytes 786440 | tf_op jit(solution)/shard_map/ppermute | solution.py:318
  52.2 16.5 %collective-permute-start.8 = (bf16[256,512]{1,0:T(8,128)(2,1)S(1)}, bf16[256,512]{1,0:T(8,128)(2,1)S(1)}, u32[]{:S(2)}, u32[]{:S(2)}) collective-permute-start(bf16[256,512]{1,0:T(8,128)(2,1)S(1)} %collective-permute-done.7.refs_8_), channel_id=1, source_target_pairs={{0,64},{64,128},{128,192},{192,0},{1,65},{65,129},{129,193},{193,1... | collective-permute-start | bytes 786440 | tf_op jit(solution)/shard_map/ppermute | solution.py:318
  55.5 15.9 %collective-permute-start.18 = (bf16[256,512]{1,0:T(8,128)(2,1)S(1)}, bf16[256,512]{1,0:T(8,128)(2,1)}, u32[]{:S(2)}, u32[]{:S(2)}) collective-permute-start(bf16[256,512]{1,0:T(8,128)(2,1)S(1)} %collective-permute-done.16.refs_9_), channel_id=1, source_target_pairs={{0,64},{64,128},{128,192},{192,0},{1,65},{65,129},{129,193},{193,1... | collective-permute-start | bytes 786440 | tf_op jit(solution)/shard_map/ppermute | solution.py:318
  56.9 16.4 %collective-permute-start.20 = (bf16[256,512]{1,0:T(8,128)(2,1)S(1)}, bf16[256,512]{1,0:T(8,128)(2,1)S(1)}, u32[]{:S(2)}, u32[]{:S(2)}) collective-permute-start(bf16[256,512]{1,0:T(8,128)(2,1)S(1)} %collective-permute-done.16.refs_9_), channel_id=1, source_target_pairs={{0,32},{32,0},{1,33},{33,1},{2,34},{34,2},{3,35},{35,3},{4,36},{36... | collective-permute-start | bytes 786440 | tf_op jit(solution)/shard_map/ppermute | solution.py:318
  57.2 16.7 %collective-permute-start.4 = (bf16[512,256]{1,0:T(8,128)(2,1)S(1)}, bf16[512,256]{1,0:T(8,128)(2,1)}, u32[]{:S(2)}, u32[]{:S(2)}) collective-permute-start(bf16[512,256]{1,0:T(8,128)(2,1)S(1)} %collective-permute-done.2.refs_3_), channel_id=1, source_target_pairs={{0,1},{1,2},{2,3},{3,4},{4,5},{5,6},{6,7},{7,0},{8,9},{9,10},{10,1... | collective-permute-start | bytes 786440 | tf_op jit(solution)/shard_map/ppermute | solution.py:318
  62.0 14.9 %all-to-all-start.2 = ((bf16[32,16,128]{2,1,0:T(8,128)(2,1)}), bf16[32,16,128]{2,1,0:T(8,128)(2,1)S(1)}, u32[]{:S(2)}, u32[]{:S(2)}) async-start(bf16[32,16,128]{2,1,0:T(8,128)(2,1)} %get-tuple-element.24), calls=%async_computation.2 | async-start | bytes 262144 | tf_op jit(solution)/shard_map/all_to_all | solution.py:343
  67.8 22.0 %collective-permute-start.21 = (bf16[256,512]{1,0:T(8,128)(2,1)S(1)}, bf16[256,512]{1,0:T(8,128)(2,1)}, u32[]{:S(2)}, u32[]{:S(2)}) collective-permute-start(bf16[256,512]{1,0:T(8,128)(2,1)S(1)} %collective-permute-done.17.refs_10_), channel_id=1, source_target_pairs={{0,32},{32,0},{1,33},{33,1},{2,34},{34,2},{3,35},{35,3},{4,36},{36... | collective-permute-start | bytes 786440 | tf_op jit(solution)/shard_map/ppermute | solution.py:318
  68.7 21.2 %collective-permute-start.5 = (bf16[512,256]{1,0:T(8,128)(2,1)S(1)}, bf16[512,256]{1,0:T(8,128)(2,1)}, u32[]{:S(2)}, u32[]{:S(2)}) collective-permute-start(bf16[512,256]{1,0:T(8,128)(2,1)S(1)} %collective-permute-done.3.refs_4_), channel_id=1, source_target_pairs={{0,7},{1,0},{2,1},{3,2},{4,3},{5,4},{6,5},{7,6},{8,15},{9,8},{10,9... | collective-permute-start | bytes 786440 | tf_op jit(solution)/shard_map/ppermute | solution.py:318
  71.4 18.8 %collective-permute-start.10 = (bf16[256,512]{1,0:T(8,128)(2,1)S(1)}, bf16[256,512]{1,0:T(8,128)(2,1)}, u32[]{:S(2)}, u32[]{:S(2)}) collective-permute-start(bf16[256,512]{1,0:T(8,128)(2,1)S(1)} %collective-permute-done.9.refs_10_), channel_id=1, source_target_pairs={{0,192},{64,0},{128,64},{192,128},{1,193},{65,1},{129,65},{193,129... | collective-permute-start | bytes 786440 | tf_op jit(solution)/shard_map/ppermute | solution.py:318
  73.3 17.1 %collective-permute-start.22 = (bf16[256,512]{1,0:T(8,128)(2,1)}, bf16[256,512]{1,0:T(8,128)(2,1)}, u32[]{:S(2)}, u32[]{:S(2)}) collective-permute-start(bf16[256,512]{1,0:T(8,128)(2,1)} %collective-permute-done.18.refs_11_), channel_id=1, source_target_pairs={{0,32},{32,0},{1,33},{33,1},{2,34},{34,2},{3,35},{35,3},{4,36},{36... | collective-permute-start | bytes 786440 | tf_op jit(solution)/shard_map/ppermute | solution.py:318
  73.9 16.8 %collective-permute-start.6 = (bf16[512,256]{1,0:T(8,128)(2,1)}, bf16[512,256]{1,0:T(8,128)(2,1)}, u32[]{:S(2)}, u32[]{:S(2)}) collective-permute-start(bf16[512,256]{1,0:T(8,128)(2,1)} %collective-permute-done.4.refs_5_), channel_id=1, source_target_pairs={{0,1},{1,2},{2,3},{3,4},{4,5},{5,6},{6,7},{7,0},{8,9},{9,10},{10,1... | collective-permute-start | bytes 786440 | tf_op jit(solution)/shard_map/ppermute | solution.py:318
  83.0 30.4 %all-to-all-start.3 = ((bf16[8,128,256]{2,1,0:T(8,128)(2,1)}), bf16[8,128,256]{2,1,0:T(8,128)(2,1)S(1)}, u32[]{:S(2)}, u32[]{:S(2)}) async-start(bf16[8,128,256]{2,1,0:T(8,128)(2,1)} %get-tuple-element.34), calls=%async_computation.3 | async-start | bytes 1048576 | tf_op jit(solution)/shard_map/all_to_all | solution.py:353
  99.9 13.5 %collective-permute-start.24 = (bf16[512,256]{1,0:T(8,128)(2,1)S(1)}, bf16[512,256]{1,0:T(8,128)(2,1)S(1)}, u32[]{:S(2)}, u32[]{:S(2)}) collective-permute-start(bf16[512,256]{1,0:T(8,128)(2,1)S(1)} %get-tuple-element.30), channel_id=1, source_target_pairs={{0,24},{8,0},{16,8},{24,16},{1,25},{9,1},{17,9},{25,17},{2,26},{10... | collective-permute-start | bytes 786440 | tf_op jit(solution)/shard_map/ppermute | solution.py:318
  100.8 12.6 %collective-permute-start.23 = (bf16[512,256]{1,0:T(8,128)(2,1)S(1)}, bf16[512,256]{1,0:T(8,128)(2,1)S(1)}, u32[]{:S(2)}, u32[]{:S(2)}) collective-permute-start(bf16[512,256]{1,0:T(8,128)(2,1)S(1)} %copy-done.12), channel_id=1, source_target_pairs={{0,8},{8,16},{16,24},{24,0},{1,9},{9,17},{17,25},{25,1},{2,10},{10... | collective-permute-start | bytes 786440 | tf_op jit(solution)/shard_map/ppermute | solution.py:318
  (22 other events, 167.8 us)
